TPU v7x, 512 devices: a whole 4x8x8 slice. The times are simulated.
512 devices in a mesh: emb: 16 (over x_lo, z), dp: 8 (over y), tp: 4 (over x_hi, core).
Axes of the slice: x: 4 (x_hi: 2, x_lo: 2; x = x_hi * 2 + x_lo), y: 8, z: 8, core: 2. Of those that a mesh axis runs over, the one named last changes fastest.
Arguments:
- emb_table: float32 [16384, 128], P('emb'), may hold values from -3 to 3
- row_accum: float32 [16384, 128], P('emb'), may hold values from 0.01 to 1
- dense_input: bfloat16 [32768, 128], P(('emb', 'dp')), may hold values from -6 to 6
- row_shard: int32 [32768, 52, 1], P(('emb', 'dp', 'tp')), may hold values from 0 to 15; in each aligned block of 3328 rows (0 to 3327, 3328 to 6655, ..., all dimensions but the last counted through in order) at most 312 rows name the same one
- local_row: int32 [32768, 52], P(('emb', 'dp', 'tp')), may hold values from 0 to 1023
- bag_length: int32 [32768, 13], P(('emb', 'dp', 'tp')), may hold values from 1 to 4
- labels: int32 [32768], P(('emb', 'dp')), may hold values 0 or 1
- feedback: float32 [32768, 1664], P(('emb', 'dp', 'tp')), may hold values from -0.3125 to 0.3125
- cross_down: bfloat16 [1792, 512], P(None, 'tp'), may hold values from -0.125 to 0.125
- cross_up: bfloat16 [512, 1792], P('tp'), may hold values from -0.25 to 0.25
- cross_bias: float32 [1792], replicated, may hold values from -3 to 3
- head_weight: float32 [1792], replicated, may hold values from -0.125 to 0.125
Outputs:
- table_new: float32 [16384, 128], P('emb')
- accum_new: float32 [16384, 128], P('emb')
- carried_new: float32 [32768, 1664], P(('emb', 'dp', 'tp'))
- grad_down: float32 [1792, 512], P(('emb', 'dp'), 'tp')
- grad_up: float32 [512, 1792], P('tp', ('emb', 'dp'))
- grad_bias: float32 [1792], P(('emb', 'dp'))
- grad_head: float32 [1792], P(('emb', 'dp'))
Inputs may be any that keep to these rules, and one draw needn't show every extreme that they name: `row_shard`: within the 3328 lookup slots of one device (aligned blocks of samples), no shard is named by more than 312 slots, a bound that some block reaches in each draw.
All inputs are finite; a program needn't handle non-finite values. No bound on the sum of `labels` on one device may be relied on, other than what follows from the above.
Results may differ from a plain program's by a relative error of at most 0.0068.
Values may be sent and summed in bfloat16 or wider, within the bound.
No kernel may reach another device: no remote copies, remote signals or barrier semaphores. Data moves between devices by JAX's collectives and lax.ppermute only.
A program may use at most 64 MiB of HBM per device.

v0:
```python
import jax
import jax.numpy as jnp
from jax import lax
from jax.sharding import PartitionSpec as P

learn_rate = 0.5


def local(
    emb_table,
    row_accum,
    dense_input,
    row_shard,
    local_row,
    bag_length,
    labels,
    feedback,
    cross_down,
    cross_up,
    cross_bias,
    head_weight,
):
    samples = row_shard.shape[0]
    lookups = row_shard.shape[1]
    features = bag_length.shape[1]
    emb_width = emb_table.shape[1]
    bag_slots = lookups // features
    pooled_width = features * emb_width
    shards = lax.axis_size("emb")
    capacity = 3 * samples * lookups // (2 * shards)
    flat_shard = row_shard.reshape(-1)
    onehot = (flat_shard[:, None] == jnp.arange(shards, dtype=jnp.int32)[None, :]).astype(jnp.int32)
    before = jnp.cumsum(onehot, axis=0) - onehot
    position = jnp.sum(before * onehot, axis=1)
    target = flat_shard * capacity + position
    send_ids = (
        jnp.zeros((shards * capacity,), jnp.int32)
        .at[target]
        .set(local_row.reshape(-1))
        .reshape(shards, capacity)
    )
    ids_received = lax.all_to_all(send_ids, "emb", split_axis=0, concat_axis=0, tiled=True)
    fetched = jnp.take(emb_table, ids_received, axis=0).astype(jnp.bfloat16)
    returned = lax.all_to_all(fetched, "emb", split_axis=0, concat_axis=0, tiled=True)
    looked = jnp.take(returned.reshape(shards * capacity, emb_width), target, axis=0)
    usable = jnp.arange(bag_slots, dtype=jnp.int32)[None, None, :] < bag_length[:, :, None]
    pooled = jnp.sum(
        looked.reshape(samples, features, bag_slots, emb_width).astype(jnp.float32)
        * usable[..., None].astype(jnp.float32),
        axis=2,
    )
    pooled = pooled.astype(jnp.bfloat16).reshape(samples, pooled_width)
    pooled_all = lax.all_gather(pooled, "tp", axis=0, tiled=True)
    x_first = jnp.concatenate([dense_input, pooled_all], axis=1)
    hidden_activation = jnp.dot(x_first, cross_down, preferred_element_type=jnp.float32).astype(
        jnp.bfloat16
    )
    crossed = lax.psum(
        jnp.dot(hidden_activation, cross_up, preferred_element_type=jnp.float32), "tp"
    )
    x_float = x_first.astype(jnp.float32)
    x_next = x_float * (crossed + cross_bias[None, :]) + x_float
    logits = jnp.sum(x_next * head_weight[None, :], axis=1)
    grad_logit = jax.nn.sigmoid(logits) - labels.astype(jnp.float32)
    grad_next = grad_logit[:, None] * head_weight[None, :]
    grad_cross = (grad_next * x_float).astype(jnp.bfloat16)
    hidden_gradient = lax.dot_general(
        grad_cross, cross_up, (((1,), (1,)), ((), ())), preferred_element_type=jnp.float32
    ).astype(jnp.bfloat16)
    back_local = lax.dot_general(
        hidden_gradient,
        cross_down[emb_width:, :],
        (((1,), (1,)), ((), ())),
        preferred_element_type=jnp.float32,
    )
    back_term = lax.psum_scatter(back_local, "tp", scatter_dimension=0, tiled=True)
    quarter = lax.axis_index("tp") * samples
    next_rows = lax.dynamic_slice_in_dim(grad_next, quarter, samples, 0)[:, emb_width:]
    cross_rows = lax.dynamic_slice_in_dim(crossed, quarter, samples, 0)[:, emb_width:]
    grad_pool = next_rows * (cross_rows + cross_bias[None, emb_width:] + 1.0) + back_term
    carried = grad_pool + feedback
    sent = lax.optimization_barrier(carried.astype(jnp.bfloat16))
    lookup_grad = sent.reshape(samples, features, 1, emb_width) * usable[..., None].astype(
        jnp.bfloat16
    )
    send_grads = (
        jnp.zeros((shards * capacity, emb_width), jnp.bfloat16)
        .at[target]
        .set(lookup_grad.reshape(-1, emb_width))
    )
    arrived = lax.all_to_all(
        send_grads.reshape(shards, capacity, emb_width),
        "emb",
        split_axis=0,
        concat_axis=0,
        tiled=True,
    )
    row_grad = (
        jnp.zeros(emb_table.shape, jnp.float32)
        .at[ids_received.reshape(-1)]
        .add(arrived.reshape(-1, emb_width).astype(jnp.float32))
    )
    total = lax.psum(row_grad, ("dp", "tp"))
    accum_new = row_accum + total * total
    table_new = emb_table - learn_rate * total / jnp.sqrt(accum_new)
    grad_down = lax.dot_general(
        x_first, hidden_gradient, (((0,), (0,)), ((), ())), preferred_element_type=jnp.float32
    )
    grad_up = lax.dot_general(
        hidden_activation, grad_cross, (((0,), (0,)), ((), ())), preferred_element_type=jnp.float32
    )
    grad_bias = jnp.sum(grad_next * x_float, axis=0)
    grad_head = jnp.sum(grad_logit[:, None] * x_next, axis=0)
    grad_down, grad_up, grad_bias, grad_head = (
        lax.psum_scatter(grad_down, ("emb", "dp"), scatter_dimension=0, tiled=True),
        lax.psum_scatter(grad_up, ("emb", "dp"), scatter_dimension=1, tiled=True),
        lax.psum_scatter(grad_bias, ("emb", "dp"), scatter_dimension=0, tiled=True),
        lax.psum_scatter(grad_head, ("emb", "dp"), scatter_dimension=0, tiled=True),
    )
    return (table_new, accum_new, carried, grad_down, grad_up, grad_bias, grad_head)


def solution(mesh):
    in_specs = (
        P("emb", None),
        P("emb", None),
        P(("emb", "dp"), None),
        P(("emb", "dp", "tp"), None, None),
        P(("emb", "dp", "tp"), None),
        P(("emb", "dp", "tp"), None),
        P(("emb", "dp")),
        P(("emb", "dp", "tp"), None),
        P(None, "tp"),
        P("tp", None),
        P(),
        P(),
    )
    out_specs = (
        P("emb", None),
        P("emb", None),
        P(("emb", "dp", "tp"), None),
        P(("emb", "dp"), "tp"),
        P("tp", ("emb", "dp")),
        P(("emb", "dp")),
        P(("emb", "dp")),
    )
    return jax.shard_map(local, mesh=mesh, in_specs=in_specs, out_specs=out_specs, check_vma=False)
```

profile of v0, /device:TPU:4, one launch (start us, length us, event | category | flops | bytes accessed | tf_op | source)
XLA Modules:
  0.0 1365.3 jit_solution(8138976836197724590)
XLA Ops:
  10.3 4.6 reduce-window.6
  15.9 12.7 scatter_custom_fusion
  28.8 19.3 %all_to_all.25 = s32[16,1,312]{2,1,0:T(1,128)S(1)} all-to-all(s32[16,1,312]{2,1,0:T(1,128)S(1)} %all_to_all.16), channel_id=1, replica_groups=mesh['emb'=16,'dp'=8,'tp'=4] {'emb'}, dimensions={0} | all-to-all | bytes 39936 | tf_op jit(solution)/shard_map/all_to_all | solution.py:42
  48.3 8.5 gather_fusion
  65.5 28.1 %all-to-all-done.1 = bf16[16,312,128]{2,1,0:T(8,128)(2,1)S(1)} async-done(((bf16[16,312,128]{2,1,0:T(8,128)(2,1)}), bf16[16,312,128]{2,1,0:T(8,128)(2,1)S(1)}, u32[]{:S(2)}, u32[]{:S(2)}) %all-to-all-start.1) | async-done | bytes 1277984 | tf_op jit(solution)/shard_map/all_to_all | solution.py:44
  93.5 7.6 gather_fusion.1
  101.2 5.2 multiply_reduce_fusion.2
  106.5 9.1 all_gather.3
  117.8 62.3 %all-reduce.11.cloned.1.call-done = f32[256,1792]{1,0:T(8,128)} async-done(((f32[256,1792]{1,0:T(8,128)}), f32[256,1792]{1,0:T(8,128)}) %all-reduce.11.cloned.1.call-update) | async-done | bytes 1835024 | tf_op jit(solution)/shard_map/psum | solution.py:58
  187.8 42.5 %reduce-scatter.6.cloned.1.call-done = f32[64,1664]{1,0:T(8,128)} async-done(((f32[256,1664]{1,0:T(8,128)}), f32[64,1664]{1,0:T(8,128)}) %reduce-scatter.6.cloned.1.call-update) | async-done | bytes 426000 | tf_op jit(solution)/shard_map/reduce_scatter | solution.py:76
  232.8 17.1 %scatter_custom_fusion.1 = bf16[4992,128]{1,0:T(8,128)(2,1)} fusion(s32[3328]{0:T(1024)S(1)} %fusion.28, bf16[3328,128]{1,0:T(8,128)(2,1)S(1)} %bitcast.62, bf16[]{:T(256)} %constant.22.clone.1, bf16[3328]{0:T(1024)(128)(2,1)S(1)} %reshape.190), kind=kCustom, calls=%fused_computation.18 | custom fusion | flops 425984 | bytes 2138114 | tf_op jit(solution)/shard_map/scatter | solution.py:89
  249.9 9.4 all-to-all-start.2
  262.5 28.6 %all-to-all-done.2 = bf16[16,312,128]{2,1,0:T(8,128)(2,1)S(1)} async-done(((bf16[16,312,128]{2,1,0:T(8,128)(2,1)}), bf16[16,312,128]{2,1,0:T(8,128)(2,1)S(1)}, u32[]{:S(2)}, u32[]{:S(2)}) %all-to-all-start.2) | async-done | bytes 1277984 | tf_op jit(solution)/shard_map/all_to_all | solution.py:91
  291.1 26.9 %scatter_custom_fusion.2 = f32[1024,128]{1,0:T(8,128)} fusion(s32[4992]{0:T(1024)S(1)} %fusion.27, bf16[4992,128]{1,0:T(8,128)(2,1)S(1)} %bitcast.61, f32[]{:T(128)} %constant.16.clone.1), kind=kCustom, calls=%fused_computation.6 | custom fusion | flops 1277952 | bytes 1802244 | tf_op jit(solution)/shard_map/scatter-add | solution.py:101
  318.0 317.1 %fusion.31 = (f32[16,128]{1,0:T(8,128)S(1)}, f32[128,16]{0,1:T(8,128)S(1)}) fusion(f32[1792,128]{1,0:T(8,128)} %fusion.36, f32[128,1792]{0,1:T(8,128)S(1)} %copy-done.2), kind=kCustom, calls=%all-reduce-scatter.2 | all-reduce-scatter fusion | flops 524289 | bytes 1853440
  639.0 8.9 collective-permute-start.13
  649.3 4.5 collective-permute-start.11
  653.8 11.2 collective-permute-start.10
  665.1 4.3 collective-permute-start.9
  680.7 5.5 collective-permute-start.4
  693.3 5.5 collective-permute-start.1
  700.1 4.3 collective-permute-start.30
  731.3 4.9 collective-permute-start.19
  746.3 604.4 %all-reduce.6 = (f32[1792]{0:T(1024)S(1)}, f32[1792]{0:T(1024)S(1)}) all-reduce(f32[1792]{0:T(1024)S(1)} %get-tuple-element.8, f32[1792]{0:T(1024)S(1)} %get-tuple-element.7), channel_id=5, replica_groups=mesh['emb'=16,'dp'=8,'tp'=4] {'emb','dp'}, use_global_device_ids=true, to_apply=%region_14.15.clone | all-reduce | flops 3584 | bytes 28672
  (153 shorter events, 96.8 us)
Async XLA Ops:
  59.0 34.5 %all-to-all-start.1 = ((bf16[16,312,128]{2,1,0:T(8,128)(2,1)}), bf16[16,312,128]{2,1,0:T(8,128)(2,1)S(1)}, u32[]{:S(2)}, u32[]{:S(2)}) async-start(bf16[16,312,128]{2,1,0:T(8,128)(2,1)} %select_convert_fusion), calls=%async_computation.1 | async-start | bytes 2555904 | tf_op jit(solution)/shard_map/all_to_all | solution.py:44
  62.8 117.2 %all-reduce.11.cloned.1.call-start = ((), (), s32[]{:S(2)}) async-start(), calls=%async_computation.4 | async-start | bytes 3670016 | tf_op jit(solution)/shard_map/psum | solution.py:58
  117.7 112.5 %reduce-scatter.6.cloned.1.call-start = ((), (), s32[]{:S(2)}) async-start(), calls=%async_computation.5 | async-start | bytes 2129920 | tf_op jit(solution)/shard_map/reduce_scatter | solution.py:76
  249.9 41.2 %all-to-all-start.2 = ((bf16[16,312,128]{2,1,0:T(8,128)(2,1)}), bf16[16,312,128]{2,1,0:T(8,128)(2,1)S(1)}, u32[]{:S(2)}, u32[]{:S(2)}) async-start(bf16[16,312,128]{2,1,0:T(8,128)(2,1)} %bitcast.7), calls=%async_computation.3 | async-start | bytes 2555904 | tf_op jit(solution)/shard_map/all_to_all | solution.py:91
  259.3 1097.4 %all-reduce.13.cloned.1.call-start = ((), (), s32[]{:S(2)}) async-start(), calls=%async_computation.6 | async-start | bytes 1048576 | tf_op jit(solution)/shard_map/psum | solution.py:103
  636.4 17.4 %collective-permute-start.15 = (f32[14,128]{1,0:T(8,128)S(1)}, f32[14,128]{1,0:T(8,128)S(1)}, u32[]{:S(2)}, u32[]{:S(2)}) collective-permute-start(f32[14,128]{1,0:T(8,128)S(1)} %slice.30), channel_id=1, source_target_pairs={{0,64},{4,68},{8,72},{12,76},{16,80},{20,84},{24,88},{28,92},{32,9... | collective-permute-start | bytes 21512
  637.7 27.4 %collective-permute-start.14 = (f32[16,128]{1,0:T(8,128)S(1)}, f32[16,128]{1,0:T(8,128)S(1)}, u32[]{:S(2)}, u32[]{:S(2)}) collective-permute-start(f32[16,128]{1,0:T(8,128)S(1)} %get-tuple-element.13), channel_id=1, source_target_pairs={{0,60},{4,64},{8,68},{12,72},{16,76},{20,80},{24,84},{28,88},{32,9... | collective-permute-start | bytes 24584
  639.0 30.4 %collective-permute-start.13 = (f32[16,128]{1,0:T(8,128)S(1)}, f32[16,128]{1,0:T(8,128)S(1)}, u32[]{:S(2)}, u32[]{:S(2)}) collective-permute-start(f32[16,128]{1,0:T(8,128)S(1)} %get-tuple-element.13), channel_id=1, source_target_pairs={{0,56},{4,60},{8,64},{12,68},{16,72},{20,76},{24,80},{28,84},{32,8... | collective-permute-start | bytes 24584
  648.0 22.7 %collective-permute-start.12 = (f32[16,128]{1,0:T(8,128)S(1)}, f32[16,128]{1,0:T(8,128)S(1)}, u32[]{:S(2)}, u32[]{:S(2)}) collective-permute-start(f32[16,128]{1,0:T(8,128)S(1)} %get-tuple-element.13), channel_id=1, source_target_pairs={{0,52},{4,56},{8,60},{12,64},{16,68},{20,72},{24,76},{28,80},{32,8... | collective-permute-start | bytes 24584
  649.3 25.2 %collective-permute-start.11 = (f32[16,128]{1,0:T(8,128)S(1)}, f32[16,128]{1,0:T(8,128)S(1)}, u32[]{:S(2)}, u32[]{:S(2)}) collective-permute-start(f32[16,128]{1,0:T(8,128)S(1)} %get-tuple-element.13), channel_id=1, source_target_pairs={{0,48},{4,52},{8,56},{12,60},{16,64},{20,68},{24,72},{28,76},{32,8... | collective-permute-start | bytes 24584
  653.8 23.8 %collective-permute-start.10 = (f32[16,128]{1,0:T(8,128)S(1)}, f32[16,128]{1,0:T(8,128)S(1)}, u32[]{:S(2)}, u32[]{:S(2)}) collective-permute-start(f32[16,128]{1,0:T(8,128)S(1)} %get-tuple-element.13), channel_id=1, source_target_pairs={{0,44},{4,48},{8,52},{12,56},{16,60},{20,64},{24,68},{28,72},{32,7... | collective-permute-start | bytes 24584
  670.7 18.6 %collective-permute-start.7 = (f32[16,128]{1,0:T(8,128)S(1)}, f32[16,128]{1,0:T(8,128)S(1)}, u32[]{:S(2)}, u32[]{:S(2)}) collective-permute-start(f32[16,128]{1,0:T(8,128)S(1)} %get-tuple-element.13), channel_id=1, source_target_pairs={{0,32},{4,36},{8,40},{12,44},{16,48},{20,52},{24,56},{28,60},{32,6... | collective-permute-start | bytes 24584
  674.5 18.8 %collective-permute-start.6 = (f32[16,128]{1,0:T(8,128)S(1)}, f32[16,128]{1,0:T(8,128)S(1)}, u32[]{:S(2)}, u32[]{:S(2)}) collective-permute-start(f32[16,128]{1,0:T(8,128)S(1)} %get-tuple-element.13), channel_id=1, source_target_pairs={{0,28},{4,32},{8,36},{12,40},{16,44},{20,48},{24,52},{28,56},{32,6... | collective-permute-start | bytes 24584
  677.6 21.2 %collective-permute-start.5 = (f32[16,128]{1,0:T(8,128)S(1)}, f32[16,128]{1,0:T(8,128)S(1)}, u32[]{:S(2)}, u32[]{:S(2)}) collective-permute-start(f32[16,128]{1,0:T(8,128)S(1)} %get-tuple-element.13), channel_id=1, source_target_pairs={{0,24},{4,28},{8,32},{12,36},{16,40},{20,44},{24,48},{28,52},{32,5... | collective-permute-start | bytes 24584
  680.7 19.4 %collective-permute-start.4 = (f32[16,128]{1,0:T(8,128)S(1)}, f32[16,128]{1,0:T(8,128)S(1)}, u32[]{:S(2)}, u32[]{:S(2)}) collective-permute-start(f32[16,128]{1,0:T(8,128)S(1)} %get-tuple-element.13), channel_id=1, source_target_pairs={{0,20},{4,24},{8,28},{12,32},{16,36},{20,40},{24,44},{28,48},{32,5... | collective-permute-start | bytes 24584
  686.2 18.3 %collective-permute-start.3 = (f32[16,128]{1,0:T(8,128)S(1)}, f32[16,128]{1,0:T(8,128)S(1)}, u32[]{:S(2)}, u32[]{:S(2)}) collective-permute-start(f32[16,128]{1,0:T(8,128)S(1)} %get-tuple-element.13), channel_id=1, source_target_pairs={{0,16},{4,20},{8,24},{12,28},{16,32},{20,36},{24,40},{28,44},{32,4... | collective-permute-start | bytes 24584
  689.3 17.3 %collective-permute-start.2 = (f32[16,128]{1,0:T(8,128)S(1)}, f32[16,128]{1,0:T(8,128)S(1)}, u32[]{:S(2)}, u32[]{:S(2)}) collective-permute-start(f32[16,128]{1,0:T(8,128)S(1)} %get-tuple-element.13), channel_id=1, source_target_pairs={{0,12},{4,16},{8,20},{12,24},{16,28},{20,32},{24,36},{28,40},{32,4... | collective-permute-start | bytes 24584
  720.6 17.9 %collective-permute-start.22 = (f32[128,16]{0,1:T(8,128)S(1)}, f32[128,16]{0,1:T(8,128)S(1)}, u32[]{:S(2)}, u32[]{:S(2)}) collective-permute-start(f32[128,16]{0,1:T(8,128)S(1)} %get-tuple-element.14), channel_id=1, source_target_pairs={{0,28},{4,32},{8,36},{12,40},{16,44},{20,48},{24,52},{28,56},{32,6... | collective-permute-start | bytes 24584
  724.5 17.6 %collective-permute-start.21 = (f32[128,16]{0,1:T(8,128)S(1)}, f32[128,16]{0,1:T(8,128)S(1)}, u32[]{:S(2)}, u32[]{:S(2)}) collective-permute-start(f32[128,16]{0,1:T(8,128)S(1)} %get-tuple-element.14), channel_id=1, source_target_pairs={{0,24},{4,28},{8,32},{12,36},{16,40},{20,44},{24,48},{28,52},{32,5... | collective-permute-start | bytes 24584
  727.1 626.5 %collective-permute-start.20 = (f32[128,16]{0,1:T(8,128)S(1)}, f32[128,16]{0,1:T(8,128)S(1)}, u32[]{:S(2)}, u32[]{:S(2)}) collective-permute-start(f32[128,16]{0,1:T(8,128)S(1)} %get-tuple-element.14), channel_id=1, source_target_pairs={{0,20},{4,24},{8,28},{12,32},{16,36},{20,40},{24,44},{28,48},{32,5... | collective-permute-start | bytes 24584
  731.3 622.2 %collective-permute-start.19 = (f32[128,16]{0,1:T(8,128)S(1)}, f32[128,16]{0,1:T(8,128)S(1)}, u32[]{:S(2)}, u32[]{:S(2)}) collective-permute-start(f32[128,16]{0,1:T(8,128)S(1)} %get-tuple-element.14), channel_id=1, source_target_pairs={{0,16},{4,20},{8,24},{12,28},{16,32},{20,36},{24,40},{28,44},{32,4... | collective-permute-start | bytes 24584
  736.3 617.3 %collective-permute-start.18 = (f32[128,16]{0,1:T(8,128)S(1)}, f32[128,16]{0,1:T(8,128)S(1)}, u32[]{:S(2)}, u32[]{:S(2)}) collective-permute-start(f32[128,16]{0,1:T(8,128)S(1)} %get-tuple-element.14), channel_id=1, source_target_pairs={{0,12},{4,16},{8,20},{12,24},{16,28},{20,32},{24,36},{28,40},{32,4... | collective-permute-start | bytes 24584
  738.5 615.1 %collective-permute-start.17 = (f32[128,16]{0,1:T(8,128)S(1)}, f32[128,16]{0,1:T(8,128)S(1)}, u32[]{:S(2)}, u32[]{:S(2)}) collective-permute-start(f32[128,16]{0,1:T(8,128)S(1)} %get-tuple-element.14), channel_id=1, source_target_pairs={{0,8},{4,12},{8,16},{12,20},{16,24},{20,28},{24,32},{28,36},{32,40... | collective-permute-start | bytes 24584
  742.2 611.4 %collective-permute-start.16 = (f32[128,16]{0,1:T(8,128)S(1)}, f32[128,16]{0,1:T(8,128)S(1)}, u32[]{:S(2)}, u32[]{:S(2)}) collective-permute-start(f32[128,16]{0,1:T(8,128)S(1)} %get-tuple-element.14), channel_id=1, source_target_pairs={{0,4},{4,8},{8,12},{12,16},{16,20},{20,24},{24,28},{28,32},{32,36}... | collective-permute-start | bytes 24584
  (29 other events, 2144.1 us)
Sparse Core Ops, SparseCore 0:
  117.9 62.1 all-reduce.10
  184.3 45.9 reduce-scatter.5
  318.1 272.8 all-reduce.12
where the time goes:
time: 1370 us
  blocking collectives  950 us (69%)
  waiting for transfers between devices  162 us (12%)
  starting transfers between devices  122 us (9%)
  other arithmetic  68.2 us (5%)
  local copies, waits for them, and re-layouts  40.7 us (3%)
  between operations  16 us (1%)
    unnamed x2, blocking collectives  921 us
    unnamed x32, starting transfers between devices  109 us
    psum x1, waiting for transfers between devices, local(): lax.psum(jnp.dot(hidden_activation, cross_up, preferred_element_type=jnp....  62.3 us
    reduce_scatter x1, waiting for transfers between devices, local(): lax.psum_scatter(back_local, 'tp', scatter_dimension=0, tiled=True)  42.5 us
    all_to_all x1, waiting for transfers between devices, local(): lax.all_to_all(send_grads.reshape(shards, capacity, emb_width), 'emb', sp...  28.6 us
    all_to_all x1, waiting for transfers between devices, local(): lax.all_to_all(fetched, 'emb', split_axis=0, concat_axis=0, tiled=True)  28.1 us
  transfers between devices with their start and end apart: 37, of which 4 were waited for; matrix products, arithmetic and copies ran while one was open for 24% of the time, Pallas kernels for 0%

commit v1 on v0

v1 whole, which is shorter than its diff:
```python
import jax
import jax.numpy as jnp
from jax import lax
from jax.experimental import pallas as pl
from jax.experimental.pallas import tpu as pltpu
from jax.sharding import Mesh, PartitionSpec as P

BF = jnp.bfloat16
F32 = jnp.float32
I32 = jnp.int32
E = 128
F = 13
BAG = 4
LOOK = F * BAG
N = 64
DENSE = 256
TP = 4
DP = 8
SHARDS = 16
CAP = 312
ROWS = 1024
DX = 1792
POOL = F * E
RANK = 128
GROUP = 14
CHUNK = 32
BAGS = N * F
LEARN = 0.5
EMB = ("xl", "z")
TPA = ("xh", "core")

VMEM = pl.BlockSpec(memory_space=pltpu.VMEM)
SMEM = pl.BlockSpec(memory_space=pltpu.SMEM)


def iota(shape, axis):
    return lax.broadcasted_iota(I32, shape, axis)


def dot(a, b, ca=1, cb=0):
    return lax.dot_general(a, b, (((ca,), (cb,)), ((), ())), preferred_element_type=F32)


def call(kernel, outs, ins, name, scratch=(), limit=40, flops=0):
    nbytes = sum(x.size * x.dtype.itemsize for x in ins)
    return pl.pallas_call(
        kernel,
        out_shape=outs,
        in_specs=[SMEM if x.size < 8 else VMEM for x in ins],
        out_specs=jax.tree.map(lambda _: VMEM, outs),
        scratch_shapes=scratch,
        compiler_params=pltpu.CompilerParams(vmem_limit_bytes=limit << 20),
        cost_estimate=pl.CostEstimate(flops=flops, bytes_accessed=nbytes, transcendentals=0),
        name=name,
    )(*ins)


def index_kernel(shard_ref, row_ref, len_ref, ids_ref, src_ref, src_t_ref):
    def spread(values):
        parts = []
        for j in range(BAG):
            pick = (iota((F, LOOK), 1) == BAG * iota((F, LOOK), 0) + j).astype(F32).astype(BF)
            parts.append(dot(pick, values.astype(F32).astype(BF), 1, 1))
        return jnp.concatenate(parts, axis=1)

    shard = spread(shard_ref[...])
    rows = row_ref[...]
    row_lo, row_hi = spread(rows & 255), spread(rows >> 8)
    eye = (iota((F, F), 0) == iota((F, F), 1)).astype(F32).astype(BF)
    lens = dot(eye, len_ref[...].astype(F32).astype(BF), 1, 1)
    lens = jnp.concatenate([lens] * BAG, axis=1)
    wide = (F, BAG * N)
    lane = iota(wide, 1)
    usable = (lane >> 6).astype(F32) < lens
    bag = jnp.where(usable, iota(wide, 0) * N + (lane & (N - 1)) + 1, 0)
    bag_lo, bag_hi = (bag & 255).astype(F32), (bag & ~255).astype(F32)
    row_hi = row_hi * 256.0

    sq = (BAG * N, BAG * N)
    upper = (iota(sq, 0) < iota(sq, 1)).astype(F32).astype(BF)
    shards = iota((SHARDS, BAG * N), 0).astype(F32)
    slots = iota((CAP, BAG * N), 0).astype(F32)
    base = jnp.zeros((SHARDS, 1), F32)
    ids = jnp.zeros((SHARDS, CAP), F32)
    src = jnp.zeros((SHARDS, CAP), F32)
    src_t = jnp.zeros((CAP, SHARDS), F32)
    for f in range(F):
        hit = shards == shard[f : f + 1, :]
        one = jnp.where(hit, 1.0, 0.0)
        before = dot(one.astype(BF), upper) + base
        base = base + jnp.sum(one, axis=1, keepdims=True)
        rank = jnp.sum(one * before, axis=0, keepdims=True)
        place = jnp.where(slots == rank, 1.0, 0.0).astype(BF)

        def put(v):
            return jnp.where(hit, v[f : f + 1, :], 0.0).astype(BF)

        lo, hi = put(bag_lo), put(bag_hi)
        ids = ids + dot(put(row_lo), place, 1, 1) + dot(put(row_hi), place, 1, 1)
        src = src + dot(lo, place, 1, 1) + dot(hi, place, 1, 1)
        src_t = src_t + dot(place, lo, 1, 1) + dot(place, hi, 1, 1)
    ids_ref[...] = ids.astype(I32)
    src_ref[...] = src.astype(I32) - 1
    src_t_ref[...] = src_t.astype(I32) - 1


def fetch_kernel(ids_ref, table_ref, out_ref):
    table = table_ref[...].astype(BF)
    cols = jnp.transpose(ids_ref[...].astype(F32))
    lanes = iota((CAP, ROWS), 1).astype(F32)
    for s in range(SHARDS):
        pick = jnp.where(cols[:, s : s + 1] == lanes, 1.0, 0.0).astype(BF)
        out_ref[s] = dot(pick, table).astype(BF)


def pool_kernel(rows_ref, src_ref, out_ref, acc_ref):
    bags = iota((BAGS, CAP), 0)
    for s in range(SHARDS):
        pick = jnp.where(bags == src_ref[s : s + 1, :], 1.0, 0.0).astype(BF)
        term = dot(pick, rows_ref[s])
        if s == 0:
            acc_ref[...] = term
        else:
            acc_ref[...] += term
    for f in range(F):
        out_ref[:, f * E : (f + 1) * E] = acc_ref[f * N : (f + 1) * N, :].astype(BF)


def dense_kernel(
    where_ref, pooled_ref, dense_ref, down_ref, up_ref, bias_ref, head_ref, label_ref,
    feedback_ref, src_t_ref, carried_ref, send_ref, small_ref,
):
    first = pl.multiple_of(where_ref[0] * N, N)
    x = jnp.concatenate([dense_ref[pl.ds(first, N), :], pooled_ref[...]], axis=1)
    hidden = jnp.concatenate([dot(x, down_ref[k]).astype(BF) for k in range(TP)], axis=1)
    up = up_ref[...]
    crossed = dot(hidden, up)
    xf = x.astype(F32)
    bias, head = bias_ref[...], head_ref[...]
    x_next = xf * (crossed + bias) + xf
    logits = jnp.sum(x_next * head, axis=1, keepdims=True)
    grad_logit = jax.nn.sigmoid(logits) - label_ref[pl.ds(first, N), :].astype(F32)
    grad_next = grad_logit * head
    grad_cross = (grad_next * xf).astype(BF)
    grad_hidden = dot(grad_cross, up, 1, 1).astype(BF)
    back = dot(grad_hidden[:, :RANK], down_ref[0][E:, :], 1, 1)
    for k in range(1, TP):
        back = back + dot(grad_hidden[:, k * RANK : (k + 1) * RANK], down_ref[k][E:, :], 1, 1)
    carried = grad_next[:, E:] * (crossed[:, E:] + bias[:, E:] + 1.0) + back + feedback_ref[...]
    carried_ref[...] = carried
    sent = carried.astype(BF)
    by_bag = jnp.concatenate([sent[:, f * E : (f + 1) * E] for f in range(F)], axis=0)
    bags = iota((CAP, BAGS), 1)
    for s in range(SHARDS):
        pick = jnp.where(src_t_ref[:, s : s + 1] == bags, 1.0, 0.0).astype(BF)
        send_ref[s] = dot(pick, by_bag).astype(BF)
    small_ref[0:N, :] = jnp.broadcast_to(grad_logit, (N, E))
    grad_head = jnp.sum(grad_logit * x_next, axis=0, keepdims=True)
    for j in range(DX // E):
        small_ref[N + j : N + j + 1, :] = grad_head[:, j * E : (j + 1) * E]
    small_ref[N + DX // E :, :] = jnp.zeros((2, E), F32)


def grads_kernel(
    where_ref, pooled_ref, dense_ref, down_ref, up_ref, head_ref, s0_ref, s1_ref, s2_ref, s3_ref,
    *rest,
):
    outs, (logit_ref, down_grad_ref, up_grad_ref, stage_ref) = rest[:DP], rest[DP:]
    t, y = where_ref[0], where_ref[1]
    for m, ref in enumerate((s0_ref, s1_ref, s2_ref, s3_ref)):
        logit_ref[pl.ds(pl.multiple_of((t ^ m) * N, N), N), :] = ref[0:N, :]
    x = jnp.concatenate([dense_ref[...], pooled_ref[...]], axis=1)
    xf = x.astype(F32)
    hidden = dot(x, down_ref[...]).astype(BF)
    cross = logit_ref[:, 0:1] * head_ref[...] * xf
    grad_bias = jnp.sum(cross, axis=0, keepdims=True)
    grad_cross = cross.astype(BF)
    grad_hidden = dot(grad_cross, up_ref[...], 1, 1).astype(BF)
    down_grad_ref[...] = dot(x, grad_hidden, 0, 0).astype(BF)
    up_grad_ref[...] = dot(grad_cross, hidden, 0, 0).astype(BF)

    tail = slice(N, N + DX // E)
    heads = (s0_ref[tail, :] + s1_ref[tail, :]) + (s2_ref[tail, :] + s3_ref[tail, :])
    grad_head = jnp.concatenate([heads[j : j + 1, :] for j in range(DX // E)], axis=1)
    groups = DX // GROUP
    r = iota((groups, DX), 1) - GROUP * iota((groups, DX), 0)
    own = (r >= 0) & (r < GROUP)
    rows = iota((DX, E), 0)
    rest14 = rows - GROUP * jnp.floor((rows.astype(F32) + 0.5) * (1.0 / GROUP)).astype(I32)
    small = jnp.zeros((groups, E), F32)
    for p, v in enumerate((grad_head, grad_bias)):
        spread = jnp.where(own, v, 0.0).astype(BF)
        lanes = jnp.where(iota((DX, E), 1) == rest14 + 16 * p, 1.0, 0.0).astype(BF)
        small = small + dot(spread, lanes)

    block = DP * GROUP
    q = (DP * CHUNK, 2 * block + 32)
    d, rho, col = iota(q, 0) >> 5, iota(q, 0) & 31, iota(q, 1)
    want = jnp.where(
        rho < GROUP,
        GROUP * d + rho,
        jnp.where(
            rho < 2 * GROUP,
            block + GROUP * d + rho - GROUP,
            jnp.where(rho == 2 * GROUP, 2 * block + d, -1),
        ),
    )
    select = jnp.where(col == want, 1.0, 0.0).astype(BF)
    for e in range(SHARDS):
        part = jnp.concatenate([small[DP * e : DP * e + DP], jnp.zeros((24, E), F32)], axis=0)
        block_rows = jnp.concatenate(
            [
                down_grad_ref[block * e : block * (e + 1), :],
                up_grad_ref[block * e : block * (e + 1), :],
                part.astype(BF),
            ],
            axis=0,
        )
        got = dot(select, block_rows).astype(BF)
        for k in range(DP):
            stage_ref[k, e] = got[CHUNK * k : CHUNK * (k + 1)]
    for s in range(DP):
        outs[s][...] = stage_ref[(y + s) & (DP - 1)]


def scatter_kernel(ids_ref, rows_ref, out_ref, acc_ref):
    rows = iota((ROWS, CAP), 0)
    for s in range(SHARDS):
        pick = jnp.where(rows == ids_ref[s : s + 1, :], 1.0, 0.0).astype(BF)
        term = dot(pick, rows_ref[s])
        if s == 0:
            acc_ref[...] = term
        else:
            acc_ref[...] += term
    out_ref[...] = acc_ref[...].astype(BF)


def total(parts):
    parts = [p.astype(F32) for p in parts]
    while len(parts) > 1:
        parts = [a + b for a, b in zip(parts[::2], parts[1::2])]
    return parts[0]


def sds(shape, dtype):
    return jax.ShapeDtypeStruct(shape, dtype)


def local(
    emb_table, row_accum, dense_input, row_shard, local_row, bag_length, labels, feedback,
    cross_down, cross_up, cross_bias, head_weight,
):
    bias, head = cross_bias.reshape(1, DX), head_weight.reshape(1, DX)
    where = jnp.stack([lax.axis_index(TPA), lax.axis_index("y")]).astype(I32)
    with jax.named_scope("gather_weights"):
        down_all = lax.all_gather(cross_down, TPA, axis=0, tiled=False)
        up_all = lax.all_gather(cross_up, TPA, axis=0, tiled=True)
    ids, src, src_t = call(
        index_kernel,
        (sds((SHARDS, CAP), I32), sds((SHARDS, CAP), I32), sds((CAP, SHARDS), I32)),
        (row_shard.reshape(N, LOOK), local_row, bag_length),
        "index",
        flops=400_000_000,
    )
    ids = lax.all_to_all(ids, EMB, split_axis=0, concat_axis=0, tiled=True)
    fetched = call(
        fetch_kernel, sds((SHARDS, CAP, E), BF), (ids, emb_table), "fetch", flops=1_300_000_000
    )
    returned = lax.all_to_all(fetched, EMB, split_axis=0, concat_axis=0, tiled=True)
    pooled = call(
        pool_kernel,
        sds((N, POOL), BF),
        (returned, src),
        "pool",
        scratch=[pltpu.VMEM((BAGS, E), F32)],
        flops=1_060_000_000,
    )
    pooled_all = lax.all_gather(pooled, TPA, axis=0, tiled=True)
    carried, send, small = call(
        dense_kernel,
        (sds((N, POOL), F32), sds((SHARDS, CAP, E), BF), sds((N + 16, E), F32)),
        (where, pooled, dense_input, down_all, up_all, bias, head, labels.reshape(DENSE, 1), feedback, src_t),
        "dense",
        flops=1_500_000_000,
    )
    arrived = lax.all_to_all(send, EMB, split_axis=0, concat_axis=0, tiled=True)

    swap = [(0, 1), (1, 0)]
    cross4 = [(i, i ^ 3) for i in range(TP)]
    s1 = lax.ppermute(small, "core", swap)
    s2 = lax.ppermute(small, "xh", swap)
    s3 = lax.ppermute(small, TPA, cross4)
    outs = call(
        grads_kernel,
        [sds((SHARDS, CHUNK, E), BF)] * DP,
        (where, pooled_all, dense_input, cross_down, cross_up, head, small, s1, s2, s3),
        "grads",
        scratch=[
            pltpu.VMEM((DENSE, E), F32),
            pltpu.VMEM((DX, RANK), BF),
            pltpu.VMEM((DX, RANK), BF),
            pltpu.VMEM((DP, SHARDS, CHUNK, E), BF),
        ],
        flops=1_000_000_000,
    )
    pieces = [outs[0]]
    for s in range(1, DP):
        pieces.append(lax.ppermute(outs[s], "y", [(i, (i + s) % DP) for i in range(DP)]))
    over_y = total(pieces).astype(BF)
    over_all = lax.all_to_all(over_y, EMB, split_axis=0, concat_axis=0, tiled=True)
    grads = jnp.sum(over_all.astype(F32), axis=0)
    grad_down = grads[0:GROUP]
    grad_up = grads[GROUP : 2 * GROUP].T
    grad_head = grads[2 * GROUP, 0:GROUP]
    grad_bias = grads[2 * GROUP, 16 : 16 + GROUP]

    row_grad = call(
        scatter_kernel,
        sds((ROWS, E), BF),
        (ids, arrived),
        "scatter",
        scratch=[pltpu.VMEM((ROWS, E), F32)],
        flops=1_300_000_000,
    )
    by_y = lax.all_to_all(row_grad, "y", split_axis=0, concat_axis=0, tiled=True)
    mine = jnp.sum(by_y.reshape(DP, ROWS // DP, E).astype(F32), axis=0).astype(BF)
    m1 = lax.ppermute(mine, "core", swap)
    m2 = lax.ppermute(mine, "xh", swap)
    m3 = lax.ppermute(mine, TPA, cross4)
    mine = total([mine, m1, m2, m3]).astype(BF)
    spread = jnp.broadcast_to(mine[None], (DP, ROWS // DP, E)).reshape(ROWS, E)
    full = lax.all_to_all(spread, "y", split_axis=0, concat_axis=0, tiled=True).astype(F32)
    accum_new = row_accum + full * full
    table_new = emb_table - LEARN * full / jnp.sqrt(accum_new)
    return (table_new, accum_new, carried, grad_down, grad_up, grad_bias, grad_head)


def solution(mesh):
    fine = Mesh(mesh.devices.reshape(2, 8, 8, 2, 2), ("xl", "z", "y", "xh", "core"))
    dense = ("xl", "z", "y")
    every = ("xl", "z", "y", "xh", "core")
    in_specs = (
        P(EMB, None),
        P(EMB, None),
        P(dense, None),
        P(every, None, None),
        P(every, None),
        P(every, None),
        P(dense),
        P(every, None),
        P(None, TPA),
        P(TPA, None),
        P(),
        P(),
    )
    out_specs = (
        P(EMB, None),
        P(EMB, None),
        P(every, None),
        P(dense, TPA),
        P(TPA, dense),
        P(dense),
        P(dense),
    )
    return jax.shard_map(local, mesh=fine, in_specs=in_specs, out_specs=out_specs, check_vma=False)
```

time: 1370 us -> 235 us (0.17)
  the two profiles are of different devices: /device:TPU:4 before, /device:TPU:1 now
where the time goes in v1:
time: 235 us; the launch traced here: 232 us
  starting transfers between devices  76.6 us (33%)
  waiting for transfers between devices  73.3 us (31%)
  blocking collectives  31.8 us (14%)
  Pallas kernels  26.2 us (11%)
  between operations  14.4 us (6%)
  local copies, waits for them, and re-layouts  7.58 us (3%)
    all_to_all x1, waiting for transfers between devices, local(): lax.all_to_all(fetched, EMB, split_axis=0, concat_axis=0, tiled=True)  29.1 us
    ppermute x7, starting transfers between devices, local(): lax.ppermute(outs[s], 'y', [(i, (i + s) % DP) for i in range(DP)])  27.3 us
    pallas_call x6, Pallas kernels, call(): pl.pallas_call(kernel, out_shape=outs, in_specs=[SMEM if x.size < 8 else...  26.2 us
    all_to_all x1, waiting for transfers between devices, local(): arrived = lax.all_to_all(send, EMB, split_axis=0, concat_axis=0, tiled=True)  20.5 us
    all_to_all x1, blocking collectives, local(): ids = lax.all_to_all(ids, EMB, split_axis=0, concat_axis=0, tiled=True)  19 us
    all_gather x1, blocking collectives, local(): pooled_all = lax.all_gather(pooled, TPA, axis=0, tiled=True)  12.7 us
    all_to_all x1, waiting for transfers between devices, local(): lax.all_to_all(spread, 'y', split_axis=0, concat_axis=0, tiled=True)  8.22 us
    all_to_all x1, waiting for transfers between devices, local(): lax.all_to_all(over_y, EMB, split_axis=0, concat_axis=0, tiled=True)  7.46 us
  transfers between devices with their start and end apart: 20, of which 5 were waited for; matrix products, arithmetic and copies ran while one was open for 2% of the time, Pallas kernels for 8%

profile of v1, /device:TPU:1, one launch (start us, length us, event | category | flops | bytes accessed | tf_op | source)
XLA Modules:
  0.0 232.0 jit_solution(11373297779291099272)
XLA Ops:
  11.1 5.2 %index.1 = (s32[16,312]{1,0:T(8,128)S(1)}, s32[16,312]{1,0:T(8,128)S(1)}, s32[312,16]{1,0:T(8,128)S(1)}) custom-call(s32[64,52]{1,0:T(8,128)S(1)} %bitcast.23, s32[64,52]{1,0:T(8,128)S(1)} %copy.27.row_ref, s32[64,13]{1,0:T(8,128)S(1)} %copy.28.len_ref), custom_call_target="tpu_custom_call" | custom-call | flops 400000000 | bytes 29952 | tf_op jit(solution)/shard_map/index/pallas_call | solution.py:46
  16.3 19.0 %all_to_all.41 = s32[16,1,312]{2,1,0:T(1,128)S(1)} all-to-all(s32[16,1,312]{2,1,0:T(1,128)S(1)} %copy.29), channel_id=1, replica_groups=mesh['xl'=2,'z'=8,'y'=8,'xh'=2,'core'=2] {'xl','z'}, dimensions={0} | all-to-all | bytes 39936 | tf_op jit(solution)/shard_map/all_to_all | solution.py:265
  35.4 4.1 %fetch.1 = bf16[16,312,128]{2,1,0:T(8,128)(2,1)} custom-call(s32[16,312]{1,0:T(8,128)S(1)} %bitcast.24, f32[1024,128]{1,0:T(8,128)S(1)} %copy-done), custom_call_target="tpu_custom_call" | custom-call | flops 1300000000 | bytes 544256 | tf_op jit(solution)/shard_map/fetch/pallas_call | solution.py:46
  39.5 4.0 %all-to-all-start.1 = ((bf16[16,312,128]{2,1,0:T(8,128)(2,1)}), bf16[16,312,128]{2,1,0:T(8,128)(2,1)S(1)}, u32[]{:S(2)}, u32[]{:S(2)}) async-start(bf16[16,312,128]{2,1,0:T(8,128)(2,1)} %fetch.1), calls=%async_computation.1 | async-start | bytes 2555904 | tf_op jit(solution)/shard_map/all_to_all | solution.py:269
  43.8 29.1 %all-to-all-done.1.rows_ref = bf16[16,312,128]{2,1,0:T(8,128)(2,1)S(1)} async-done(((bf16[16,312,128]{2,1,0:T(8,128)(2,1)}), bf16[16,312,128]{2,1,0:T(8,128)(2,1)S(1)}, u32[]{:S(2)}, u32[]{:S(2)}) %all-to-all-start.1) | async-done | bytes 1277984 | tf_op jit(solution)/shard_map/all_to_all | solution.py:269
  75.7 6.6 %all-gather.6.cloned.1.call-done = bf16[7168,128]{1,0:T(8,128)(2,1)} async-done(((bf16[1792,128]{1,0:T(8,128)(2,1)}), bf16[7168,128]{1,0:T(8,128)(2,1)}) %all-gather.6.cloned.1.call-update) | async-done | bytes 1835024 | tf_op jit(solution)/shard_map/gather_weights/all_gather | solution.py:256
  85.4 6.5 %dense.1 = (f32[64,1664]{1,0:T(8,128)}, bf16[16,312,128]{2,1,0:T(8,128)(2,1)}, f32[80,128]{1,0:T(8,128)S(1)}) custom-call(s32[2]{0:T(128)S(1)} %pad_add_fusion.where_ref, bf16[64,1664]{1,0:T(8,128)(2,1)S(1)} %pool.1.pooled_ref, bf16[256,128]{1,0:T(8,128)(2,1)S(1)} %copy-done.6, bf16[4,1792,128]{2,1,0:T(8,128)(2,1)S(1)} %bitcast.27, ...), custom_call_target="tpu_custom_call" | custom-call | flops 1500000000 | bytes 4409864 | tf_op jit(solution)/shard_map/dense/pallas_call | solution.py:46
  91.9 6.6 %all-to-all-start.2 = ((bf16[16,312,128]{2,1,0:T(8,128)(2,1)}), bf16[16,312,128]{2,1,0:T(8,128)(2,1)S(1)}, u32[]{:S(2)}, u32[]{:S(2)}) async-start(bf16[16,312,128]{2,1,0:T(8,128)(2,1)} %get-tuple-element.24), calls=%async_computation.2 | async-start | bytes 2555904 | tf_op jit(solution)/shard_map/all_to_all | solution.py:286
  101.0 3.7 %collective-permute-start.4 = (f32[80,128]{1,0:T(8,128)S(1)}, f32[80,128]{1,0:T(8,128)S(1)}, u32[]{:S(2)}, u32[]{:S(2)}) collective-permute-start(f32[80,128]{1,0:T(8,128)S(1)} %get-tuple-element.26.s0_ref), channel_id=1, source_target_pairs={{0,2},{2,0},{1,3},{3,1},{4,6},{6,4},{5,7},{7,5},{8,10},{10,8},{9,1... | collective-permute-start | bytes 122888 | tf_op jit(solution)/shard_map/ppermute | solution.py:291
  104.7 3.3 %collective-permute-start.5 = (f32[80,128]{1,0:T(8,128)S(1)}, f32[80,128]{1,0:T(8,128)S(1)}, u32[]{:S(2)}, u32[]{:S(2)}) collective-permute-start(f32[80,128]{1,0:T(8,128)S(1)} %get-tuple-element.26.s0_ref), channel_id=1, source_target_pairs={{0,3},{1,2},{2,1},{3,0},{4,7},{5,6},{6,5},{7,4},{8,11},{9,10},{10,... | collective-permute-start | bytes 122888 | tf_op jit(solution)/shard_map/ppermute | solution.py:292
  108.0 20.5 %all-to-all-done.2.rows_ref = bf16[16,312,128]{2,1,0:T(8,128)(2,1)S(1)} async-done(((bf16[16,312,128]{2,1,0:T(8,128)(2,1)}), bf16[16,312,128]{2,1,0:T(8,128)(2,1)S(1)}, u32[]{:S(2)}, u32[]{:S(2)}) %all-to-all-start.2) | async-done | bytes 1277984 | tf_op jit(solution)/shard_map/all_to_all | solution.py:286
  128.5 4.1 %scatter.1 = bf16[1024,128]{1,0:T(8,128)(2,1)} custom-call(s32[16,312]{1,0:T(8,128)S(1)} %bitcast.25, bf16[16,312,128]{2,1,0:T(8,128)(2,1)S(1)} %all-to-all-done.2.rows_ref), custom_call_target="tpu_custom_call" | custom-call | flops 1300000000 | bytes 1297920 | tf_op jit(solution)/shard_map/scatter/pallas_call | solution.py:46
  132.6 6.9 %all-to-all-start.3 = ((bf16[8,128,128]{2,1,0:T(8,128)(2,1)}), bf16[8,128,128]{2,1,0:T(8,128)(2,1)S(1)}, u32[]{:S(2)}, u32[]{:S(2)}) async-start(bf16[8,128,128]{2,1,0:T(8,128)(2,1)} %bitcast.6), calls=%async_computation.3 | async-start | bytes 524288 | tf_op jit(solution)/shard_map/all_to_all | solution.py:325
  139.5 12.7 %all_gather.15.pooled_ref = bf16[256,1664]{1,0:T(8,128)(2,1)S(1)} all-gather(bf16[64,1664]{1,0:T(8,128)(2,1)S(1)} %pool.1.pooled_ref), channel_id=1, replica_groups=mesh['xl'=2,'z'=8,'y'=8,'xh'=2,'core'=2] {'xh','core'}, dimensions={0}, use_global_device_ids=true | all-gather | bytes 1064960 | tf_op jit(solution)/shard_map/all_gather | solution.py:278
  152.3 3.4 %grads.1 = (bf16[16,32,128]{2,1,0:T(8,128)(2,1)S(1)}, bf16[16,32,128]{2,1,0:T(8,128)(2,1)S(1)}, bf16[16,32,128]{2,1,0:T(8,128)(2,1)S(1)}, bf16[16,32,128]{2,1,0:...) custom-call(s32[2]{0:T(128)S(1)} %pad_add_fusion.where_ref, ...), custom_call_target="tpu_custom_call" | custom-call | flops 1000000000 | bytes 2006024 | tf_op jit(solution)/shard_map/grads/pallas_call | solution.py:46
  155.7 6.7 %collective-permute-start.10 = (bf16[16,32,128]{2,1,0:T(8,128)(2,1)S(1)}, bf16[16,32,128]{2,1,0:T(8,128)(2,1)S(1)}, u32[]{:S(2)}, u32[]{:S(2)}) collective-permute-start(bf16[16,32,128]{2,1,0:T(8,128)(2,1)S(1)} %get-tuple-element.32), channel_id=1, source_target_pairs={{0,20},{4,24},{8,28},{12,0},{16,4},{20,8},{24,12},{28,16},{1,21},{... | collective-permute-start | bytes 393224 | tf_op jit(solution)/shard_map/ppermute | solution.py:308
  173.9 3.1 %collective-permute-start.8 = (bf16[16,32,128]{2,1,0:T(8,128)(2,1)S(1)}, bf16[16,32,128]{2,1,0:T(8,128)(2,1)S(1)}, u32[]{:S(2)}, u32[]{:S(2)}) collective-permute-start(bf16[16,32,128]{2,1,0:T(8,128)(2,1)S(1)} %get-tuple-element.30), channel_id=1, source_target_pairs={{0,12},{4,16},{8,20},{12,24},{16,28},{20,0},{24,4},{28,8},{1,13},{... | collective-permute-start | bytes 393224 | tf_op jit(solution)/shard_map/ppermute | solution.py:308
  177.1 6.1 %collective-permute-start.9 = (bf16[16,32,128]{2,1,0:T(8,128)(2,1)S(1)}, bf16[16,32,128]{2,1,0:T(8,128)(2,1)S(1)}, u32[]{:S(2)}, u32[]{:S(2)}) collective-permute-start(bf16[16,32,128]{2,1,0:T(8,128)(2,1)S(1)} %get-tuple-element.31), channel_id=1, source_target_pairs={{0,16},{4,20},{8,24},{12,28},{16,0},{20,4},{24,8},{28,12},{1,17},{... | collective-permute-start | bytes 393224 | tf_op jit(solution)/shard_map/ppermute | solution.py:308
  183.2 4.0 %collective-permute-start = (bf16[128,128]{1,0:T(8,128)(2,1)S(1)}, bf16[128,128]{1,0:T(8,128)(2,1)S(1)}, u32[]{:S(2)}, u32[]{:S(2)}) collective-permute-start(bf16[128,128]{1,0:T(8,128)(2,1)S(1)} %reduce_sum.21), channel_id=1, source_target_pairs={{0,1},{1,0},{2,3},{3,2},{4,5},{5,4},{6,7},{7,6},{8,9},{9,8},{10,11... | collective-permute-start | bytes 98312 | tf_op jit(solution)/shard_map/ppermute | solution.py:327
  190.4 3.8 %collective-permute-start.2 = (bf16[128,128]{1,0:T(8,128)(2,1)S(1)}, bf16[128,128]{1,0:T(8,128)(2,1)S(1)}, u32[]{:S(2)}, u32[]{:S(2)}) collective-permute-start(bf16[128,128]{1,0:T(8,128)(2,1)S(1)} %reduce_sum.21), channel_id=1, source_target_pairs={{0,3},{1,2},{2,1},{3,0},{4,7},{5,6},{6,5},{7,4},{8,11},{9,10},{10,... | collective-permute-start | bytes 98312 | tf_op jit(solution)/shard_map/ppermute | solution.py:329
  195.0 4.4 %all-to-all-start.5 = ((bf16[16,32,128]{2,1,0:T(8,128)(2,1)}), bf16[16,32,128]{2,1,0:T(8,128)(2,1)S(1)}, u32[]{:S(2)}, u32[]{:S(2)}) async-start(bf16[16,32,128]{2,1,0:T(8,128)(2,1)} %add_convert_fusion), calls=%async_computation.5 | async-start | bytes 262144 | tf_op jit(solution)/shard_map/all_to_all | solution.py:310
  199.5 7.5 %all-to-all-done.5 = bf16[16,32,128]{2,1,0:T(8,128)(2,1)S(1)} async-done(((bf16[16,32,128]{2,1,0:T(8,128)(2,1)}), bf16[16,32,128]{2,1,0:T(8,128)(2,1)S(1)}, u32[]{:S(2)}, u32[]{:S(2)}) %all-to-all-start.5) | async-done | bytes 131104 | tf_op jit(solution)/shard_map/all_to_all | solution.py:310
  207.7 6.8 %all-to-all-start.4 = ((bf16[8,128,128]{2,1,0:T(8,128)(2,1)}), bf16[8,128,128]{2,1,0:T(8,128)(2,1)S(1)}, u32[]{:S(2)}, u32[]{:S(2)}) async-start(bf16[8,128,128]{2,1,0:T(8,128)(2,1)} %broadcast_in_dim.2), calls=%async_computation.4 | async-start | bytes 524288 | tf_op jit(solution)/shard_map/all_to_all | solution.py:332
  215.8 8.2 %all-to-all-done.4 = bf16[8,128,128]{2,1,0:T(8,128)(2,1)S(1)} async-done(((bf16[8,128,128]{2,1,0:T(8,128)(2,1)}), bf16[8,128,128]{2,1,0:T(8,128)(2,1)S(1)}, u32[]{:S(2)}, u32[]{:S(2)}) %all-to-all-start.4) | async-done | bytes 262176 | tf_op jit(solution)/shard_map/all_to_all | solution.py:332
  (66 shorter events, 31.1 us)
Async XLA Ops:
  7.2 28.2 %copy-start = (f32[1024,128]{1,0:T(8,128)S(1)}, f32[1024,128]{1,0:T(8,128)}, u32[]{:S(2)}) copy-start(f32[1024,128]{1,0:T(8,128)} %table_ref.1) | copy-start | bytes 1572868
  7.2 68.6 %all-gather.4.cloned.1.call-start = ((), (), s32[]{:S(2)}) async-start(), calls=%async_computation.6 | async-start | bytes 2293760 | tf_op jit(solution)/shard_map/gather_weights/all_gather | solution.py:257
  7.9 74.4 %all-gather.6.cloned.1.call-start = ((), (), s32[]{:S(2)}) async-start(), calls=%async_computation.7 | async-start | bytes 2293760 | tf_op jit(solution)/shard_map/gather_weights/all_gather | solution.py:256
  39.5 33.4 %all-to-all-start.1 = ((bf16[16,312,128]{2,1,0:T(8,128)(2,1)}), bf16[16,312,128]{2,1,0:T(8,128)(2,1)S(1)}, u32[]{:S(2)}, u32[]{:S(2)}) async-start(bf16[16,312,128]{2,1,0:T(8,128)(2,1)} %fetch.1), calls=%async_computation.1 | async-start | bytes 2555904 | tf_op jit(solution)/shard_map/all_to_all | solution.py:269
  91.9 36.6 %all-to-all-start.2 = ((bf16[16,312,128]{2,1,0:T(8,128)(2,1)}), bf16[16,312,128]{2,1,0:T(8,128)(2,1)S(1)}, u32[]{:S(2)}, u32[]{:S(2)}) async-start(bf16[16,312,128]{2,1,0:T(8,128)(2,1)} %get-tuple-element.24), calls=%async_computation.2 | async-start | bytes 2555904 | tf_op jit(solution)/shard_map/all_to_all | solution.py:286
  98.5 53.7 %collective-permute-start.3 = (f32[80,128]{1,0:T(8,128)S(1)}, f32[80,128]{1,0:T(8,128)S(1)}, u32[]{:S(2)}, u32[]{:S(2)}) collective-permute-start(f32[80,128]{1,0:T(8,128)S(1)} %get-tuple-element.26.s0_ref), channel_id=1, source_target_pairs={{0,1},{1,0},{2,3},{3,2},{4,5},{5,4},{6,7},{7,6},{8,9},{9,8},{10,11... | collective-permute-start | bytes 122888 | tf_op jit(solution)/shard_map/ppermute | solution.py:290
  101.0 51.3 %collective-permute-start.4 = (f32[80,128]{1,0:T(8,128)S(1)}, f32[80,128]{1,0:T(8,128)S(1)}, u32[]{:S(2)}, u32[]{:S(2)}) collective-permute-start(f32[80,128]{1,0:T(8,128)S(1)} %get-tuple-element.26.s0_ref), channel_id=1, source_target_pairs={{0,2},{2,0},{1,3},{3,1},{4,6},{6,4},{5,7},{7,5},{8,10},{10,8},{9,1... | collective-permute-start | bytes 122888 | tf_op jit(solution)/shard_map/ppermute | solution.py:291
  104.7 47.6 %collective-permute-start.5 = (f32[80,128]{1,0:T(8,128)S(1)}, f32[80,128]{1,0:T(8,128)S(1)}, u32[]{:S(2)}, u32[]{:S(2)}) collective-permute-start(f32[80,128]{1,0:T(8,128)S(1)} %get-tuple-element.26.s0_ref), channel_id=1, source_target_pairs={{0,3},{1,2},{2,1},{3,0},{4,7},{5,6},{6,5},{7,4},{8,11},{9,10},{10,... | collective-permute-start | bytes 122888 | tf_op jit(solution)/shard_map/ppermute | solution.py:292
  132.6 19.7 %copy-start.1 = (bf16[128,1792]{1,0:T(8,128)(2,1)S(1)}, bf16[128,1792]{1,0:T(8,128)(2,1)}, u32[]{:S(2)}) copy-start(bf16[128,1792]{1,0:T(8,128)(2,1)} %up_ref.1) | copy-start | bytes 1376260
  132.6 19.7 %copy-start.2 = (bf16[1792,128]{1,0:T(8,128)(2,1)S(1)}, bf16[1792,128]{1,0:T(8,128)(2,1)}, u32[]{:S(2)}) copy-start(bf16[1792,128]{1,0:T(8,128)(2,1)} %down_ref.1) | copy-start | bytes 1376260
  132.6 50.5 %all-to-all-start.3 = ((bf16[8,128,128]{2,1,0:T(8,128)(2,1)}), bf16[8,128,128]{2,1,0:T(8,128)(2,1)S(1)}, u32[]{:S(2)}, u32[]{:S(2)}) async-start(bf16[8,128,128]{2,1,0:T(8,128)(2,1)} %bitcast.6), calls=%async_computation.3 | async-start | bytes 524288 | tf_op jit(solution)/shard_map/all_to_all | solution.py:325
  155.7 18.2 %collective-permute-start.10 = (bf16[16,32,128]{2,1,0:T(8,128)(2,1)S(1)}, bf16[16,32,128]{2,1,0:T(8,128)(2,1)S(1)}, u32[]{:S(2)}, u32[]{:S(2)}) collective-permute-start(bf16[16,32,128]{2,1,0:T(8,128)(2,1)S(1)} %get-tuple-element.32), channel_id=1, source_target_pairs={{0,20},{4,24},{8,28},{12,0},{16,4},{20,8},{24,12},{28,16},{1,21},{... | collective-permute-start | bytes 393224 | tf_op jit(solution)/shard_map/ppermute | solution.py:308
  162.4 14.6 %collective-permute-start.11 = (bf16[16,32,128]{2,1,0:T(8,128)(2,1)S(1)}, bf16[16,32,128]{2,1,0:T(8,128)(2,1)S(1)}, u32[]{:S(2)}, u32[]{:S(2)}) collective-permute-start(bf16[16,32,128]{2,1,0:T(8,128)(2,1)S(1)} %get-tuple-element.33), channel_id=1, source_target_pairs={{0,24},{4,28},{8,0},{12,4},{16,8},{20,12},{24,16},{28,20},{1,25},{... | collective-permute-start | bytes 393224 | tf_op jit(solution)/shard_map/ppermute | solution.py:308
  165.5 17.7 %collective-permute-start.12 = (bf16[16,32,128]{2,1,0:T(8,128)(2,1)S(1)}, bf16[16,32,128]{2,1,0:T(8,128)(2,1)S(1)}, u32[]{:S(2)}, u32[]{:S(2)}) collective-permute-start(bf16[16,32,128]{2,1,0:T(8,128)(2,1)S(1)} %get-tuple-element.34), channel_id=1, source_target_pairs={{0,28},{4,0},{8,4},{12,8},{16,12},{20,16},{24,20},{28,24},{1,29},{... | collective-permute-start | bytes 393224 | tf_op jit(solution)/shard_map/ppermute | solution.py:308
  167.7 19.5 %collective-permute-start.6 = (bf16[16,32,128]{2,1,0:T(8,128)(2,1)S(1)}, bf16[16,32,128]{2,1,0:T(8,128)(2,1)S(1)}, u32[]{:S(2)}, u32[]{:S(2)}) collective-permute-start(bf16[16,32,128]{2,1,0:T(8,128)(2,1)S(1)} %get-tuple-element.28), channel_id=1, source_target_pairs={{0,4},{4,8},{8,12},{12,16},{16,20},{20,24},{24,28},{28,0},{1,5},{5... | collective-permute-start | bytes 393224 | tf_op jit(solution)/shard_map/ppermute | solution.py:308
  170.8 19.6 %collective-permute-start.7 = (bf16[16,32,128]{2,1,0:T(8,128)(2,1)S(1)}, bf16[16,32,128]{2,1,0:T(8,128)(2,1)S(1)}, u32[]{:S(2)}, u32[]{:S(2)}) collective-permute-start(bf16[16,32,128]{2,1,0:T(8,128)(2,1)S(1)} %get-tuple-element.29), channel_id=1, source_target_pairs={{0,8},{4,12},{8,16},{12,20},{16,24},{20,28},{24,0},{28,4},{1,9},{5... | collective-permute-start | bytes 393224 | tf_op jit(solution)/shard_map/ppermute | solution.py:308
  173.9 20.3 %collective-permute-start.8 = (bf16[16,32,128]{2,1,0:T(8,128)(2,1)S(1)}, bf16[16,32,128]{2,1,0:T(8,128)(2,1)S(1)}, u32[]{:S(2)}, u32[]{:S(2)}) collective-permute-start(bf16[16,32,128]{2,1,0:T(8,128)(2,1)S(1)} %get-tuple-element.30), channel_id=1, source_target_pairs={{0,12},{4,16},{8,20},{12,24},{16,28},{20,0},{24,4},{28,8},{1,13},{... | collective-permute-start | bytes 393224 | tf_op jit(solution)/shard_map/ppermute | solution.py:308
  177.1 17.2 %collective-permute-start.9 = (bf16[16,32,128]{2,1,0:T(8,128)(2,1)S(1)}, bf16[16,32,128]{2,1,0:T(8,128)(2,1)S(1)}, u32[]{:S(2)}, u32[]{:S(2)}) collective-permute-start(bf16[16,32,128]{2,1,0:T(8,128)(2,1)S(1)} %get-tuple-element.31), channel_id=1, source_target_pairs={{0,16},{4,20},{8,24},{12,28},{16,0},{20,4},{24,8},{28,12},{1,17},{... | collective-permute-start | bytes 393224 | tf_op jit(solution)/shard_map/ppermute | solution.py:308
  183.2 16.3 %collective-permute-start = (bf16[128,128]{1,0:T(8,128)(2,1)S(1)}, bf16[128,128]{1,0:T(8,128)(2,1)S(1)}, u32[]{:S(2)}, u32[]{:S(2)}) collective-permute-start(bf16[128,128]{1,0:T(8,128)(2,1)S(1)} %reduce_sum.21), channel_id=1, source_target_pairs={{0,1},{1,0},{2,3},{3,2},{4,5},{5,4},{6,7},{7,6},{8,9},{9,8},{10,11... | collective-permute-start | bytes 98312 | tf_op jit(solution)/shard_map/ppermute | solution.py:327
  187.2 12.2 %collective-permute-start.1 = (bf16[128,128]{1,0:T(8,128)(2,1)S(1)}, bf16[128,128]{1,0:T(8,128)(2,1)S(1)}, u32[]{:S(2)}, u32[]{:S(2)}) collective-permute-start(bf16[128,128]{1,0:T(8,128)(2,1)S(1)} %reduce_sum.21), channel_id=1, source_target_pairs={{0,2},{2,0},{1,3},{3,1},{4,6},{6,4},{5,7},{7,5},{8,10},{10,8},{9,1... | collective-permute-start | bytes 98312 | tf_op jit(solution)/shard_map/ppermute | solution.py:328
  190.4 9.1 %collective-permute-start.2 = (bf16[128,128]{1,0:T(8,128)(2,1)S(1)}, bf16[128,128]{1,0:T(8,128)(2,1)S(1)}, u32[]{:S(2)}, u32[]{:S(2)}) collective-permute-start(bf16[128,128]{1,0:T(8,128)(2,1)S(1)} %reduce_sum.21), channel_id=1, source_target_pairs={{0,3},{1,2},{2,1},{3,0},{4,7},{5,6},{6,5},{7,4},{8,11},{9,10},{10,... | collective-permute-start | bytes 98312 | tf_op jit(solution)/shard_map/ppermute | solution.py:329
  195.0 11.9 %all-to-all-start.5 = ((bf16[16,32,128]{2,1,0:T(8,128)(2,1)}), bf16[16,32,128]{2,1,0:T(8,128)(2,1)S(1)}, u32[]{:S(2)}, u32[]{:S(2)}) async-start(bf16[16,32,128]{2,1,0:T(8,128)(2,1)} %add_convert_fusion), calls=%async_computation.5 | async-start | bytes 262144 | tf_op jit(solution)/shard_map/all_to_all | solution.py:310
  199.4 24.6 %copy-start.7 = (f32[1024,128]{1,0:T(8,128)S(1)}, f32[1024,128]{1,0:T(8,128)}, u32[]{:S(2)}) copy-start(f32[1024,128]{1,0:T(8,128)} %param.13) | copy-start | bytes 1572868
  207.7 16.3 %all-to-all-start.4 = ((bf16[8,128,128]{2,1,0:T(8,128)(2,1)}), bf16[8,128,128]{2,1,0:T(8,128)(2,1)S(1)}, u32[]{:S(2)}, u32[]{:S(2)}) async-start(bf16[8,128,128]{2,1,0:T(8,128)(2,1)} %broadcast_in_dim.2), calls=%async_computation.4 | async-start | bytes 524288 | tf_op jit(solution)/shard_map/all_to_all | solution.py:332
  (7 other events, 34.3 us)
Sparse Core Ops, SparseCore 0:
  10.1 36.5 all-gather.3
  48.8 33.5 all-gather.5

commit v2 on v1

--- a/solution.py
+++ b/solution.py
@@ -24,6 +24,8 @@
 RANK = 128
 GROUP = 14
 CHUNK = 32
+XROWS = 80
+BLOCKS = DX // E
 BAGS = N * F
 LEARN = 0.5
 EMB = ("xl", "z")
@@ -55,19 +57,23 @@
     )(*ins)
 
 
-def index_kernel(shard_ref, row_ref, len_ref, ids_ref, src_ref, src_t_ref):
+def index_kernel(
+    shard_ref, row_ref, len_ref, down_ref, up_ref, ids_ref, src_ref, src_t_ref, pack_ref
+):
     def spread(values):
         parts = []
         for j in range(BAG):
             pick = (iota((F, LOOK), 1) == BAG * iota((F, LOOK), 0) + j).astype(F32).astype(BF)
-            parts.append(dot(pick, values.astype(F32).astype(BF), 1, 1))
+            parts.append(dot(pick, values.astype(F32).astype(BF)))
         return jnp.concatenate(parts, axis=1)
 
-    shard = spread(shard_ref[...])
+    for j in range(DX // E):
+        pack_ref[j] = down_ref[j * E : (j + 1) * E, :]
+        pack_ref[DX // E + j] = up_ref[:, j * E : (j + 1) * E]
+    shard = spread(shard_ref[...].reshape(LOOK, N))
     rows = row_ref[...]
     row_lo, row_hi = spread(rows & 255), spread(rows >> 8)
-    eye = (iota((F, F), 0) == iota((F, F), 1)).astype(F32).astype(BF)
-    lens = dot(eye, len_ref[...].astype(F32).astype(BF), 1, 1)
+    lens = len_ref[...].astype(F32)
     lens = jnp.concatenate([lens] * BAG, axis=1)
     wide = (F, BAG * N)
     lane = iota(wide, 1)
@@ -113,7 +119,10 @@
         out_ref[s] = dot(pick, table).astype(BF)
 
 
-def pool_kernel(rows_ref, src_ref, out_ref, acc_ref):
+def pool_kernel(where_ref, rows_ref, src_ref, dense_ref, out_ref, acc_ref):
+    first = pl.multiple_of(where_ref[0] * N, N)
+    out_ref[0:N, 0:E] = dense_ref[pl.ds(first, N), :]
+    out_ref[N:, :] = jnp.zeros((XROWS - N, DX), BF)
     bags = iota((BAGS, CAP), 0)
     for s in range(SHARDS):
         pick = jnp.where(bags == src_ref[s : s + 1, :], 1.0, 0.0).astype(BF)
@@ -123,16 +132,21 @@
         else:
             acc_ref[...] += term
     for f in range(F):
-        out_ref[:, f * E : (f + 1) * E] = acc_ref[f * N : (f + 1) * N, :].astype(BF)
+        out_ref[0:N, (f + 1) * E : (f + 2) * E] = acc_ref[f * N : (f + 1) * N, :].astype(BF)
 
 
 def dense_kernel(
-    where_ref, pooled_ref, dense_ref, down_ref, up_ref, bias_ref, head_ref, label_ref,
-    feedback_ref, src_t_ref, carried_ref, send_ref, small_ref,
+    where_ref, x_ref, pack_ref, bias_ref, head_ref, label_ref, feedback_ref, src_t_ref,
+    carried_ref, send_ref, small_ref, down_ref, up_ref,
 ):
     first = pl.multiple_of(where_ref[0] * N, N)
-    x = jnp.concatenate([dense_ref[pl.ds(first, N), :], pooled_ref[...]], axis=1)
-    hidden = jnp.concatenate([dot(x, down_ref[k]).astype(BF) for k in range(TP)], axis=1)
+    for k in range(TP):
+        block = slice(k * RANK, (k + 1) * RANK)
+        for j in range(BLOCKS):
+            down_ref[j * E : (j + 1) * E, block] = pack_ref[k, j]
+            up_ref[block, j * E : (j + 1) * E] = pack_ref[k, BLOCKS + j]
+    x = x_ref[0:N, :]
+    hidden = dot(x, down_ref[...]).astype(BF)
     up = up_ref[...]
     crossed = dot(hidden, up)
     xf = x.astype(F32)
@@ -143,9 +157,7 @@
     grad_next = grad_logit * head
     grad_cross = (grad_next * xf).astype(BF)
     grad_hidden = dot(grad_cross, up, 1, 1).astype(BF)
-    back = dot(grad_hidden[:, :RANK], down_ref[0][E:, :], 1, 1)
-    for k in range(1, TP):
-        back = back + dot(grad_hidden[:, k * RANK : (k + 1) * RANK], down_ref[k][E:, :], 1, 1)
+    back = dot(grad_hidden, down_ref[E:, :], 1, 1)
     carried = grad_next[:, E:] * (crossed[:, E:] + bias[:, E:] + 1.0) + back + feedback_ref[...]
     carried_ref[...] = carried
     sent = carried.astype(BF)
@@ -162,14 +174,13 @@
 
 
 def grads_kernel(
-    where_ref, pooled_ref, dense_ref, down_ref, up_ref, head_ref, s0_ref, s1_ref, s2_ref, s3_ref,
-    *rest,
+    where_ref, x_ref, down_ref, up_ref, head_ref, s0_ref, s1_ref, s2_ref, s3_ref,
+    keep_ref, send_ref, logit_ref, down_grad_ref, up_grad_ref, stage_ref,
 ):
-    outs, (logit_ref, down_grad_ref, up_grad_ref, stage_ref) = rest[:DP], rest[DP:]
-    t, y = where_ref[0], where_ref[1]
+    t, y, u = where_ref[0], where_ref[1], where_ref[2]
     for m, ref in enumerate((s0_ref, s1_ref, s2_ref, s3_ref)):
         logit_ref[pl.ds(pl.multiple_of((t ^ m) * N, N), N), :] = ref[0:N, :]
-    x = jnp.concatenate([dense_ref[...], pooled_ref[...]], axis=1)
+    x = jnp.concatenate([x_ref[XROWS * k : XROWS * k + N, :] for k in range(TP)], axis=0)
     xf = x.astype(F32)
     hidden = dot(x, down_ref[...]).astype(BF)
     cross = logit_ref[:, 0:1] * head_ref[...] * xf
@@ -217,10 +228,13 @@
             axis=0,
         )
         got = dot(select, block_rows).astype(BF)
+        w = u ^ e
+        place = ((w >> 3) & 1) * 8 + (w & 1) * 4 + ((w >> 1) & 3)
         for k in range(DP):
-            stage_ref[k, e] = got[CHUNK * k : CHUNK * (k + 1)]
-    for s in range(DP):
-        outs[s][...] = stage_ref[(y + s) & (DP - 1)]
+            v = y ^ k
+            stage_ref[v & 1, v >> 1, place] = got[CHUNK * k : CHUNK * (k + 1)]
+    keep_ref[...] = stage_ref[0]
+    send_ref[...] = stage_ref[1]
 
 
 def scatter_kernel(ids_ref, rows_ref, out_ref, acc_ref):
@@ -251,69 +265,70 @@
     cross_down, cross_up, cross_bias, head_weight,
 ):
     bias, head = cross_bias.reshape(1, DX), head_weight.reshape(1, DX)
-    where = jnp.stack([lax.axis_index(TPA), lax.axis_index("y")]).astype(I32)
-    with jax.named_scope("gather_weights"):
-        down_all = lax.all_gather(cross_down, TPA, axis=0, tiled=False)
-        up_all = lax.all_gather(cross_up, TPA, axis=0, tiled=True)
-    ids, src, src_t = call(
+    where = jnp.stack([lax.axis_index(TPA), lax.axis_index("y"), lax.axis_index(EMB)]).astype(I32)
+    ids, src, src_t, pack = call(
         index_kernel,
-        (sds((SHARDS, CAP), I32), sds((SHARDS, CAP), I32), sds((CAP, SHARDS), I32)),
-        (row_shard.reshape(N, LOOK), local_row, bag_length),
+        (
+            sds((SHARDS, CAP), I32),
+            sds((SHARDS, CAP), I32),
+            sds((CAP, SHARDS), I32),
+            sds((2 * BLOCKS, E, E), BF),
+        ),
+        (row_shard.transpose(1, 2, 0), local_row.T, bag_length.T, cross_down, cross_up),
         "index",
         flops=400_000_000,
     )
+    with jax.named_scope("gather_weights"):
+        pack_all = lax.all_gather(pack, TPA, axis=0, tiled=False)
     ids = lax.all_to_all(ids, EMB, split_axis=0, concat_axis=0, tiled=True)
     fetched = call(
         fetch_kernel, sds((SHARDS, CAP, E), BF), (ids, emb_table), "fetch", flops=1_300_000_000
     )
     returned = lax.all_to_all(fetched, EMB, split_axis=0, concat_axis=0, tiled=True)
-    pooled = call(
+    x = call(
         pool_kernel,
-        sds((N, POOL), BF),
-        (returned, src),
+        sds((XROWS, DX), BF),
+        (where, returned, src, dense_input),
         "pool",
         scratch=[pltpu.VMEM((BAGS, E), F32)],
         flops=1_060_000_000,
     )
-    pooled_all = lax.all_gather(pooled, TPA, axis=0, tiled=True)
+    x_all = lax.all_gather(x, TPA, axis=0, tiled=True)
     carried, send, small = call(
         dense_kernel,
         (sds((N, POOL), F32), sds((SHARDS, CAP, E), BF), sds((N + 16, E), F32)),
-        (where, pooled, dense_input, down_all, up_all, bias, head, labels.reshape(DENSE, 1), feedback, src_t),
+        (where, x, pack_all, bias, head, labels.reshape(DENSE, 1), feedback, src_t),
         "dense",
+        scratch=[pltpu.VMEM((DX, TP * RANK), BF), pltpu.VMEM((TP * RANK, DX), BF)],
         flops=1_500_000_000,
     )
     arrived = lax.all_to_all(send, EMB, split_axis=0, concat_axis=0, tiled=True)
 
-    swap = [(0, 1), (1, 0)]
-    cross4 = [(i, i ^ 3) for i in range(TP)]
-    s1 = lax.ppermute(small, "core", swap)
-    s2 = lax.ppermute(small, "xh", swap)
-    s3 = lax.ppermute(small, TPA, cross4)
-    outs = call(
+    def partner(value, axes, mask):
+        size = lax.axis_size(axes)
+        return lax.ppermute(value, axes, [(i, i ^ mask) for i in range(size)])
+
+    s1 = partner(small, TPA, 1)
+    s2 = partner(small, TPA, 2)
+    s3 = partner(small, TPA, 3)
+    keep, give = call(
         grads_kernel,
-        [sds((SHARDS, CHUNK, E), BF)] * DP,
-        (where, pooled_all, dense_input, cross_down, cross_up, head, small, s1, s2, s3),
+        [sds((DP // 2, SHARDS, CHUNK, E), BF)] * 2,
+        (where, x_all, cross_down, cross_up, head, small, s1, s2, s3),
         "grads",
         scratch=[
             pltpu.VMEM((DENSE, E), F32),
             pltpu.VMEM((DX, RANK), BF),
             pltpu.VMEM((DX, RANK), BF),
-            pltpu.VMEM((DP, SHARDS, CHUNK, E), BF),
+            pltpu.VMEM((2, DP // 2, SHARDS, CHUNK, E), BF),
         ],
         flops=1_000_000_000,
     )
-    pieces = [outs[0]]
-    for s in range(1, DP):
-        pieces.append(lax.ppermute(outs[s], "y", [(i, (i + s) % DP) for i in range(DP)]))
-    over_y = total(pieces).astype(BF)
-    over_all = lax.all_to_all(over_y, EMB, split_axis=0, concat_axis=0, tiled=True)
-    grads = jnp.sum(over_all.astype(F32), axis=0)
-    grad_down = grads[0:GROUP]
-    grad_up = grads[GROUP : 2 * GROUP].T
-    grad_head = grads[2 * GROUP, 0:GROUP]
-    grad_bias = grads[2 * GROUP, 16 : 16 + GROUP]
-
+    got = partner(give, "y", 1)
+    part = [keep[m].astype(F32) + got[m].astype(F32) for m in range(DP // 2)]
+    part = [part[0]] + [p.astype(BF) for p in part[1:]]
+    arrived, *part = lax.optimization_barrier((arrived, *part))
+    part = part[:1] + [partner(part[m], "y", 2 * m) for m in range(1, DP // 2)]
     row_grad = call(
         scatter_kernel,
         sds((ROWS, E), BF),
@@ -322,16 +337,30 @@
         scratch=[pltpu.VMEM((ROWS, E), F32)],
         flops=1_300_000_000,
     )
-    by_y = lax.all_to_all(row_grad, "y", split_axis=0, concat_axis=0, tiled=True)
-    mine = jnp.sum(by_y.reshape(DP, ROWS // DP, E).astype(F32), axis=0).astype(BF)
-    m1 = lax.ppermute(mine, "core", swap)
-    m2 = lax.ppermute(mine, "xh", swap)
-    m3 = lax.ppermute(mine, TPA, cross4)
-    mine = total([mine, m1, m2, m3]).astype(BF)
-    spread = jnp.broadcast_to(mine[None], (DP, ROWS // DP, E)).reshape(ROWS, E)
-    full = lax.all_to_all(spread, "y", split_axis=0, concat_axis=0, tiled=True).astype(F32)
+    owners = ("y", "core")
+    pieces = 2 * DP
+    by_y = lax.all_to_all(row_grad, owners, split_axis=0, concat_axis=0, tiled=True)
+    over_y = total(part)
+    part = [over_y[0:4]] + [over_y[4 * c : 4 * c + 4].astype(BF) for c in (1, 2, 3)]
+    by_y, *part = lax.optimization_barrier((by_y, *part))
+    part = part[:1] + [partner(part[c], EMB, mask) for c, mask in ((1, 1), (2, 8), (3, 9))]
+    mine = jnp.sum(by_y.reshape(pieces, ROWS // pieces, E).astype(F32), axis=0)
+    mine = (mine + partner(mine, "xh", 1)).astype(BF)
+    spread = jnp.broadcast_to(mine[None], (pieces, ROWS // pieces, E)).reshape(ROWS, E)
+    full = lax.all_to_all(spread, owners, split_axis=0, concat_axis=0, tiled=True)
+    over_pair = total(part)
+    part = [over_pair[0]] + [over_pair[i].astype(BF) for i in (1, 2, 3)]
+    full, *part = lax.optimization_barrier((full, *part))
+    part = part[:1] + [partner(part[i], EMB, 2 * i) for i in (1, 2, 3)]
+    full = full.astype(F32)
     accum_new = row_accum + full * full
     table_new = emb_table - LEARN * full / jnp.sqrt(accum_new)
+    grads = total(part)
+    grad_down = grads[0:GROUP]
+    grad_up = grads[GROUP : 2 * GROUP].T
+    grad_head = grads[2 * GROUP, 0:GROUP]
+    grad_bias = grads[2 * GROUP, 16 : 16 + GROUP]
+
     return (table_new, accum_new, carried, grad_down, grad_up, grad_bias, grad_head)
 
 

time: 235 us -> 227 us (0.966)
  blocking collectives: 31.8 us -> 19 us
  Pallas kernels: 26.2 us -> 29.3 us
  waiting for transfers between devices: 73.3 us -> 76 us
    all_to_all x1, waiting for transfers between devices: 20.5 us -> 0.01 us  [local(): arrived = lax.all_to_all(send, EMB, split_axis=0, concat_axis=0, tiled=True)]
    all_gather x1 -> x0, blocking collectives: 12.7 us -> none  [local(): pooled_all = lax.all_gather(pooled, TPA, axis=0, tiled=True)]
    ppermute x13 -> x14, waiting for transfers between devices: 0.03 us -> 12.6 us  [partner(): return lax.ppermute(value, axes, [(i, i ^ mask) for i in range(size)])]
    all_to_all x3 -> x2, waiting for transfers between devices: 15.7 us -> 23.3 us  [the longest x1 11.8 us: local(): lax.all_to_all(spread, owners, split_axis=0, concat_axis=0, tiled=True)]
    all_to_all x3 -> x2, starting transfers between devices: 18.1 us -> 12.8 us  [the longest x1 8.78 us: local(): lax.all_to_all(row_grad, owners, split_axis=0, concat_axis=0, tiled=True)]
    ppermute x13 -> x14, starting transfers between devices: 47.7 us -> 52.4 us  [partner(): return lax.ppermute(value, axes, [(i, i ^ mask) for i in range(size)])]
    all_gather x2, waiting for transfers between devices: 6.63 us -> 10.7 us  [the longest x1 10.7 us: local(): x_all = lax.all_gather(x, TPA, axis=0, tiled=True)]
    pallas_call x6, Pallas kernels: 26.2 us -> 29.3 us  [call(): pl.pallas_call(kernel, out_shape=outs, in_specs=[SMEM if x.size < 8 else...]
  transfers between devices with their start and end apart: 20 -> 20, of which waited for: 5 -> 7; matrix products, arithmetic and copies ran while one was open for 2% -> 1% of each run, Pallas kernels for 8% -> 10%
where the time goes in v2:
time: 227 us; the launch traced here: 226 us
  starting transfers between devices  76.2 us (34%)
  waiting for transfers between devices  76 us (33%)
  Pallas kernels  29.3 us (13%)
  blocking collectives  19 us (8%)
  between operations  14.5 us (6%)
  local copies, waits for them, and re-layouts  9.68 us (4%)
    ppermute x14, starting transfers between devices, partner(): return lax.ppermute(value, axes, [(i, i ^ mask) for i in range(size)])  52.4 us
    all_to_all x1, waiting for transfers between devices, local(): lax.all_to_all(fetched, EMB, split_axis=0, concat_axis=0, tiled=True)  29.3 us
    pallas_call x6, Pallas kernels, call(): pl.pallas_call(kernel, out_shape=outs, in_specs=[SMEM if x.size < 8 else...  29.3 us
    all_to_all x1, blocking collectives, local(): ids = lax.all_to_all(ids, EMB, split_axis=0, concat_axis=0, tiled=True)  19 us
    ppermute x14, waiting for transfers between devices, partner(): return lax.ppermute(value, axes, [(i, i ^ mask) for i in range(size)])  12.6 us
    all_to_all x1, waiting for transfers between devices, local(): lax.all_to_all(spread, owners, split_axis=0, concat_axis=0, tiled=True)  11.8 us
    all_to_all x1, waiting for transfers between devices, local(): lax.all_to_all(row_grad, owners, split_axis=0, concat_axis=0, tiled=True)  11.6 us
    all_gather x1, waiting for transfers between devices, local(): x_all = lax.all_gather(x, TPA, axis=0, tiled=True)  10.7 us
  transfers between devices with their start and end apart: 20, of which 7 were waited for; matrix products, arithmetic and copies ran while one was open for 1% of the time, Pallas kernels for 10%

profile of v2, /device:TPU:1, one launch (start us, length us, event | category | flops | bytes accessed | tf_op | source)
XLA Modules:
  0.0 226.0 jit_solution(6302908973752716512)
XLA Ops:
  11.4 6.1 %index.1 = (s32[16,312]{1,0:T(8,128)S(1)}, s32[16,312]{1,0:T(8,128)S(1)}, s32[312,16]{1,0:T(8,128)S(1)}, bf16[28,128,128]{2,1,0:T(8,128)(2,1)}) custom-call(s32[52,1,64]{2,1,0:T(1,128)S(1)} %bitcast.44, s32[52,64]{1,0:T(8,128)S(1)} %bitcast.43, s32[13,64]{1,0:T(8,128)S(1)} %bitcast.45, bf16[1792,128]{1,0:T(8,128)(2,1)S(1)} %copy-done.3, ...), custom_call_target="tpu_custom_call" | custom-call | flops 400000000 | bytes 947456 | tf_op jit(solution)/shard_map/index/pallas_call | solution.py:48
  17.6 19.0 %all_to_all.42 = s32[16,1,312]{2,1,0:T(1,128)S(1)} all-to-all(s32[16,1,312]{2,1,0:T(1,128)S(1)} %copy.20), channel_id=1, replica_groups=mesh['xl'=2,'z'=8,'y'=8,'xh'=2,'core'=2] {'xl','z'}, dimensions={0} | all-to-all | bytes 39936 | tf_op jit(solution)/shard_map/all_to_all | solution.py:283
  36.7 4.2 %fetch.1 = bf16[16,312,128]{2,1,0:T(8,128)(2,1)} custom-call(s32[16,312]{1,0:T(8,128)S(1)} %bitcast.39, f32[1024,128]{1,0:T(8,128)S(1)} %copy-done), custom_call_target="tpu_custom_call" | custom-call | flops 1300000000 | bytes 544256 | tf_op jit(solution)/shard_map/fetch/pallas_call | solution.py:48
  40.9 3.8 %all-to-all-start.1 = ((bf16[16,312,128]{2,1,0:T(8,128)(2,1)}), bf16[16,312,128]{2,1,0:T(8,128)(2,1)S(1)}, u32[]{:S(2)}, u32[]{:S(2)}) async-start(bf16[16,312,128]{2,1,0:T(8,128)(2,1)} %fetch.1), calls=%async_computation.1 | async-start | bytes 2555904 | tf_op jit(solution)/shard_map/all_to_all | solution.py:287
  45.0 29.3 %all-to-all-done.1.rows_ref = bf16[16,312,128]{2,1,0:T(8,128)(2,1)S(1)} async-done(((bf16[16,312,128]{2,1,0:T(8,128)(2,1)}), bf16[16,312,128]{2,1,0:T(8,128)(2,1)S(1)}, u32[]{:S(2)}, u32[]{:S(2)}) %all-to-all-start.1) | async-done | bytes 1277984 | tf_op jit(solution)/shard_map/all_to_all | solution.py:287
  74.4 4.1 %pool.1.x_ref = bf16[80,1792]{1,0:T(8,128)(2,1)} custom-call(s32[3]{0:T(128)S(1)} %pad_add_fusion.where_ref, bf16[16,312,128]{2,1,0:T(8,128)(2,1)S(1)} %all-to-all-done.1.rows_ref, s32[16,312]{1,0:T(8,128)S(1)} %get-tuple-element.32.src_ref, bf16[256,128]{1,0:T(8,128)(2,1)S(1)} %copy-done.8), custom_call_target="tpu_custom_call" | custom-call | flops 1060000000 | bytes 1363468 | tf_op jit(solution)/shard_map/pool/pallas_call | solution.py:48
  80.8 7.3 %dense.1 = (f32[64,1664]{1,0:T(8,128)}, bf16[16,312,128]{2,1,0:T(8,128)(2,1)}, f32[80,128]{1,0:T(8,128)S(1)}) custom-call(s32[3]{0:T(128)S(1)} %pad_add_fusion.where_ref, bf16[80,1792]{1,0:T(8,128)(2,1)} %pool.1.x_ref, bf16[4,28,128,128]{3,2,1,0:T(8,128)(2,1)S(1)} %bitcast.42, f32[1,1792]{1,0:T(1,128)S(1)} %reshape.53.bias_ref, ...), custom_call_target="tpu_custom_call" | custom-call | flops 1500000000 | bytes 4418060 | tf_op jit(solution)/shard_map/dense/pallas_call | solution.py:48
  88.1 6.9 %all-to-all-start.2 = ((bf16[16,312,128]{2,1,0:T(8,128)(2,1)}), bf16[16,312,128]{2,1,0:T(8,128)(2,1)S(1)}, u32[]{:S(2)}, u32[]{:S(2)}) async-start(bf16[16,312,128]{2,1,0:T(8,128)(2,1)} %get-tuple-element.35), calls=%async_computation.2 | async-start | bytes 2555904 | tf_op jit(solution)/shard_map/all_to_all | solution.py:305
  94.9 2.9 %collective-permute-start = (f32[80,128]{1,0:T(8,128)S(1)}, f32[80,128]{1,0:T(8,128)S(1)}, u32[]{:S(2)}, u32[]{:S(2)}) collective-permute-start(f32[80,128]{1,0:T(8,128)S(1)} %get-tuple-element.36.s0_ref), channel_id=1, source_target_pairs={{0,1},{1,0},{2,3},{3,2},{4,5},{5,4},{6,7},{7,6},{8,9},{9,8},{10,11... | collective-permute-start | bytes 122888 | tf_op jit(solution)/shard_map/ppermute | solution.py:309
  97.8 4.4 %collective-permute-start.1 = (f32[80,128]{1,0:T(8,128)S(1)}, f32[80,128]{1,0:T(8,128)S(1)}, u32[]{:S(2)}, u32[]{:S(2)}) collective-permute-start(f32[80,128]{1,0:T(8,128)S(1)} %get-tuple-element.36.s0_ref), channel_id=1, source_target_pairs={{0,2},{1,3},{2,0},{3,1},{4,6},{5,7},{6,4},{7,5},{8,10},{9,11},{10,... | collective-permute-start | bytes 122888 | tf_op jit(solution)/shard_map/ppermute | solution.py:309
  104.8 10.7 %all-gather.4.cloned.1.call-done.x_ref = bf16[320,1792]{1,0:T(8,128)(2,1)} async-done(((bf16[80,1792]{1,0:T(8,128)(2,1)}), bf16[320,1792]{1,0:T(8,128)(2,1)}) %all-gather.4.cloned.1.call-update) | async-done | bytes 1146896 | tf_op jit(solution)/shard_map/all_gather | solution.py:296
  116.8 3.4 %grads.1 = (bf16[4,16,32,128]{3,2,1,0:T(8,128)(2,1)S(1)}, bf16[4,16,32,128]{3,2,1,0:T(8,128)(2,1)S(1)}) custom-call(s32[3]{0:T(128)S(1)} %pad_add_fusion.where_ref, bf16[320,1792]{1,0:T(8,128)(2,1)S(1)} %copy-done.2, bf16[1792,128]{1,0:T(8,128)(2,1)S(1)} %copy-done.4, bf16[128,1792]{1,0:T(8,128)(2,1)S(1)} %copy-done.6, f32[1,1792]{1,0:T(1,128)S(1)} %reshape.54.head_ref, ...), custom_call_target="tpu_custom_call" | custom-call | flops 1000000000 | bytes 2235404 | tf_op jit(solution)/shard_map/grads/pallas_call | solution.py:48
  120.2 3.2 %collective-permute-start.3 = (bf16[4,16,32,128]{3,2,1,0:T(8,128)(2,1)S(1)}, bf16[4,16,32,128]{3,2,1,0:T(8,128)(2,1)S(1)}, u32[]{:S(2)}, u32[]{:S(2)}) collective-permute-start(bf16[4,16,32,128]{3,2,1,0:T(8,128)(2,1)S(1)} %get-tuple-element.38), channel_id=1, source_target_pairs={{0,4},{4,0},{8,12},{12,8},{16,20},{20,16},{24,28},{28,24},{1,5},{5... | collective-permute-start | bytes 1572872 | tf_op jit(solution)/shard_map/ppermute | solution.py:309
  123.4 11.9 %collective-permute-done.3 = bf16[4,16,32,128]{3,2,1,0:T(8,128)(2,1)S(1)} collective-permute-done((bf16[4,16,32,128]{3,2,1,0:T(8,128)(2,1)S(1)}, bf16[4,16,32,128]{3,2,1,0:T(8,128)(2,1)S(1)}, u32[]{:S(2)}, u32[]{:S(2)}) %collective-permute-start.3) | collective-permute-done | bytes 524320 | tf_op jit(solution)/shard_map/ppermute | solution.py:309
  135.5 4.2 %collective-permute-start.4 = (bf16[16,32,128]{2,1,0:T(8,128)(2,1)S(1)}, bf16[16,32,128]{2,1,0:T(8,128)(2,1)S(1)}, u32[]{:S(2)}, u32[]{:S(2)}) collective-permute-start(bf16[16,32,128]{2,1,0:T(8,128)(2,1)S(1)} %get-tuple-element.41), channel_id=1, source_target_pairs={{0,8},{4,12},{8,0},{12,4},{16,24},{20,28},{24,16},{28,20},{1,9},{5... | collective-permute-start | bytes 393224 | tf_op jit(solution)/shard_map/ppermute | solution.py:309
  139.8 5.6 %collective-permute-start.5 = (bf16[16,32,128]{2,1,0:T(8,128)(2,1)S(1)}, bf16[16,32,128]{2,1,0:T(8,128)(2,1)S(1)}, u32[]{:S(2)}, u32[]{:S(2)}) collective-permute-start(bf16[16,32,128]{2,1,0:T(8,128)(2,1)S(1)} %get-tuple-element.42), channel_id=1, source_target_pairs={{0,16},{4,20},{8,24},{12,28},{16,0},{20,4},{24,8},{28,12},{1,17},{... | collective-permute-start | bytes 393224 | tf_op jit(solution)/shard_map/ppermute | solution.py:309
  147.5 4.1 %scatter.1 = bf16[1024,128]{1,0:T(8,128)(2,1)} custom-call(s32[16,312]{1,0:T(8,128)S(1)} %bitcast.40, bf16[16,312,128]{2,1,0:T(8,128)(2,1)S(1)} %all-to-all-done.2.rows_ref), custom_call_target="tpu_custom_call" | custom-call | flops 1300000000 | bytes 1297920 | tf_op jit(solution)/shard_map/scatter/pallas_call | solution.py:48
  151.6 8.8 %all-to-all-start.3 = ((bf16[16,64,128]{2,1,0:T(8,128)(2,1)}), bf16[16,64,128]{2,1,0:T(8,128)(2,1)S(1)}, u32[]{:S(2)}, u32[]{:S(2)}) async-start(bf16[16,64,128]{2,1,0:T(8,128)(2,1)} %bitcast.13), calls=%async_computation.3 | async-start | bytes 524288 | tf_op jit(solution)/shard_map/all_to_all | solution.py:342
  160.5 11.6 %all-to-all-done.3 = bf16[16,64,128]{2,1,0:T(8,128)(2,1)S(1)} async-done(((bf16[16,64,128]{2,1,0:T(8,128)(2,1)}), bf16[16,64,128]{2,1,0:T(8,128)(2,1)S(1)}, u32[]{:S(2)}, u32[]{:S(2)}) %all-to-all-start.3) | async-done | bytes 262176 | tf_op jit(solution)/shard_map/all_to_all | solution.py:342
  177.2 3.9 %collective-permute-start.8 = (bf16[4,32,128]{2,1,0:T(8,128)(2,1)S(1)}, bf16[4,32,128]{2,1,0:T(8,128)(2,1)S(1)}, u32[]{:S(2)}, u32[]{:S(2)}) collective-permute-start(bf16[4,32,128]{2,1,0:T(8,128)(2,1)S(1)} %get-tuple-element.46), channel_id=1, source_target_pairs={{0,32},{32,0},{64,96},{96,64},{128,160},{160,128},{192,224},{224,1... | collective-permute-start | bytes 98312 | tf_op jit(solution)/shard_map/ppermute | solution.py:309
  183.9 4.0 %all-to-all-start.4 = ((bf16[16,64,128]{2,1,0:T(8,128)(2,1)}), bf16[16,64,128]{2,1,0:T(8,128)(2,1)S(1)}, u32[]{:S(2)}, u32[]{:S(2)}) async-start(bf16[16,64,128]{2,1,0:T(8,128)(2,1)} %broadcast_in_dim.2), calls=%async_computation.4 | async-start | bytes 524288 | tf_op jit(solution)/shard_map/all_to_all | solution.py:350
  188.0 11.8 %all-to-all-done.4 = bf16[16,64,128]{2,1,0:T(8,128)(2,1)S(1)} async-done(((bf16[16,64,128]{2,1,0:T(8,128)(2,1)}), bf16[16,64,128]{2,1,0:T(8,128)(2,1)S(1)}, u32[]{:S(2)}, u32[]{:S(2)}) %all-to-all-start.4) | async-done | bytes 262176 | tf_op jit(solution)/shard_map/all_to_all | solution.py:350
  199.8 9.3 %collective-permute-start.11 = (bf16[32,128]{1,0:T(8,128)(2,1)S(1)}, bf16[32,128]{1,0:T(8,128)(2,1)S(1)}, u32[]{:S(2)}, u32[]{:S(2)}) collective-permute-start(bf16[32,128]{1,0:T(8,128)(2,1)S(1)} %get-tuple-element.52), channel_id=1, source_target_pairs={{0,64},{32,96},{64,0},{96,32},{128,192},{160,224},{192,128},{224,1... | collective-permute-start | bytes 24584 | tf_op jit(solution)/shard_map/ppermute | solution.py:309
  211.1 5.2 %collective-permute-start.13 = (bf16[32,128]{1,0:T(8,128)(2,1)S(1)}, bf16[32,128]{1,0:T(8,128)(2,1)S(1)}, u32[]{:S(2)}, u32[]{:S(2)}) collective-permute-start(bf16[32,128]{1,0:T(8,128)(2,1)S(1)} %get-tuple-element.54), channel_id=1, source_target_pairs={{0,192},{32,224},{64,128},{96,160},{128,64},{160,96},{192,0},{224,... | collective-permute-start | bytes 24584 | tf_op jit(solution)/shard_map/ppermute | solution.py:309
  (77 shorter events, 25.8 us)
Async XLA Ops:
  7.2 71.5 %all-gather.6.cloned.1.call-start = ((), (), s32[]{:S(2)}) async-start(), calls=%async_computation.6 | async-start | bytes 4587520 | tf_op jit(solution)/shard_map/gather_weights/all_gather | solution.py:282
  40.9 33.5 %copy-start.8 = (bf16[256,128]{1,0:T(8,128)(2,1)S(1)}, bf16[256,128]{1,0:T(8,128)(2,1)}, u32[]{:S(2)}) copy-start(bf16[256,128]{1,0:T(8,128)(2,1)} %dense_ref.1) | copy-start | bytes 196612
  40.9 33.5 %all-to-all-start.1 = ((bf16[16,312,128]{2,1,0:T(8,128)(2,1)}), bf16[16,312,128]{2,1,0:T(8,128)(2,1)S(1)}, u32[]{:S(2)}, u32[]{:S(2)}) async-start(bf16[16,312,128]{2,1,0:T(8,128)(2,1)} %fetch.1), calls=%async_computation.1 | async-start | bytes 2555904 | tf_op jit(solution)/shard_map/all_to_all | solution.py:287
  44.7 70.8 %all-gather.4.cloned.1.call-start = ((), (), s32[]{:S(2)}) async-start(), calls=%async_computation.5 | async-start | bytes 1433600 | tf_op jit(solution)/shard_map/all_gather | solution.py:296
  88.1 27.5 %copy-start.4 = (bf16[1792,128]{1,0:T(8,128)(2,1)S(1)}, bf16[1792,128]{1,0:T(8,128)(2,1)}, u32[]{:S(2)}) copy-start(bf16[1792,128]{1,0:T(8,128)(2,1)} %down_ref.3) | copy-start | bytes 1376260
  88.1 27.5 %copy-start.6 = (bf16[128,1792]{1,0:T(8,128)(2,1)S(1)}, bf16[128,1792]{1,0:T(8,128)(2,1)}, u32[]{:S(2)}) copy-start(bf16[128,1792]{1,0:T(8,128)(2,1)} %up_ref.3) | copy-start | bytes 1376260
  88.1 47.5 %all-to-all-start.2 = ((bf16[16,312,128]{2,1,0:T(8,128)(2,1)}), bf16[16,312,128]{2,1,0:T(8,128)(2,1)S(1)}, u32[]{:S(2)}, u32[]{:S(2)}) async-start(bf16[16,312,128]{2,1,0:T(8,128)(2,1)} %get-tuple-element.35), calls=%async_computation.2 | async-start | bytes 2555904 | tf_op jit(solution)/shard_map/all_to_all | solution.py:305
  94.9 20.6 %collective-permute-start = (f32[80,128]{1,0:T(8,128)S(1)}, f32[80,128]{1,0:T(8,128)S(1)}, u32[]{:S(2)}, u32[]{:S(2)}) collective-permute-start(f32[80,128]{1,0:T(8,128)S(1)} %get-tuple-element.36.s0_ref), channel_id=1, source_target_pairs={{0,1},{1,0},{2,3},{3,2},{4,5},{5,4},{6,7},{7,6},{8,9},{9,8},{10,11... | collective-permute-start | bytes 122888 | tf_op jit(solution)/shard_map/ppermute | solution.py:309
  97.8 17.7 %collective-permute-start.1 = (f32[80,128]{1,0:T(8,128)S(1)}, f32[80,128]{1,0:T(8,128)S(1)}, u32[]{:S(2)}, u32[]{:S(2)}) collective-permute-start(f32[80,128]{1,0:T(8,128)S(1)} %get-tuple-element.36.s0_ref), channel_id=1, source_target_pairs={{0,2},{1,3},{2,0},{3,1},{4,6},{5,7},{6,4},{7,5},{8,10},{9,11},{10,... | collective-permute-start | bytes 122888 | tf_op jit(solution)/shard_map/ppermute | solution.py:309
  102.2 13.3 %collective-permute-start.2 = (f32[80,128]{1,0:T(8,128)S(1)}, f32[80,128]{1,0:T(8,128)S(1)}, u32[]{:S(2)}, u32[]{:S(2)}) collective-permute-start(f32[80,128]{1,0:T(8,128)S(1)} %get-tuple-element.36.s0_ref), channel_id=1, source_target_pairs={{0,3},{1,2},{2,1},{3,0},{4,7},{5,6},{6,5},{7,4},{8,11},{9,10},{10,... | collective-permute-start | bytes 122888 | tf_op jit(solution)/shard_map/ppermute | solution.py:309
  120.2 15.1 %collective-permute-start.3 = (bf16[4,16,32,128]{3,2,1,0:T(8,128)(2,1)S(1)}, bf16[4,16,32,128]{3,2,1,0:T(8,128)(2,1)S(1)}, u32[]{:S(2)}, u32[]{:S(2)}) collective-permute-start(bf16[4,16,32,128]{3,2,1,0:T(8,128)(2,1)S(1)} %get-tuple-element.38), channel_id=1, source_target_pairs={{0,4},{4,0},{8,12},{12,8},{16,20},{20,16},{24,28},{28,24},{1,5},{5... | collective-permute-start | bytes 1572872 | tf_op jit(solution)/shard_map/ppermute | solution.py:309
  135.5 24.9 %collective-permute-start.4 = (bf16[16,32,128]{2,1,0:T(8,128)(2,1)S(1)}, bf16[16,32,128]{2,1,0:T(8,128)(2,1)S(1)}, u32[]{:S(2)}, u32[]{:S(2)}) collective-permute-start(bf16[16,32,128]{2,1,0:T(8,128)(2,1)S(1)} %get-tuple-element.41), channel_id=1, source_target_pairs={{0,8},{4,12},{8,0},{12,4},{16,24},{20,28},{24,16},{28,20},{1,9},{5... | collective-permute-start | bytes 393224 | tf_op jit(solution)/shard_map/ppermute | solution.py:309
  139.8 20.7 %collective-permute-start.5 = (bf16[16,32,128]{2,1,0:T(8,128)(2,1)S(1)}, bf16[16,32,128]{2,1,0:T(8,128)(2,1)S(1)}, u32[]{:S(2)}, u32[]{:S(2)}) collective-permute-start(bf16[16,32,128]{2,1,0:T(8,128)(2,1)S(1)} %get-tuple-element.42), channel_id=1, source_target_pairs={{0,16},{4,20},{8,24},{12,28},{16,0},{20,4},{24,8},{28,12},{1,17},{... | collective-permute-start | bytes 393224 | tf_op jit(solution)/shard_map/ppermute | solution.py:309
  145.3 15.1 %collective-permute-start.6 = (bf16[16,32,128]{2,1,0:T(8,128)(2,1)S(1)}, bf16[16,32,128]{2,1,0:T(8,128)(2,1)S(1)}, u32[]{:S(2)}, u32[]{:S(2)}) collective-permute-start(bf16[16,32,128]{2,1,0:T(8,128)(2,1)S(1)} %get-tuple-element.43), channel_id=1, source_target_pairs={{0,24},{4,28},{8,16},{12,20},{16,8},{20,12},{24,0},{28,4},{1,25},{... | collective-permute-start | bytes 393224 | tf_op jit(solution)/shard_map/ppermute | solution.py:309
  151.6 20.5 %all-to-all-start.3 = ((bf16[16,64,128]{2,1,0:T(8,128)(2,1)}), bf16[16,64,128]{2,1,0:T(8,128)(2,1)S(1)}, u32[]{:S(2)}, u32[]{:S(2)}) async-start(bf16[16,64,128]{2,1,0:T(8,128)(2,1)} %bitcast.13), calls=%async_computation.3 | async-start | bytes 524288 | tf_op jit(solution)/shard_map/all_to_all | solution.py:342
  160.4 55.9 %copy-start.12 = (f32[1024,128]{1,0:T(8,128)S(1)}, f32[1024,128]{1,0:T(8,128)}, u32[]{:S(2)}) copy-start(f32[1024,128]{1,0:T(8,128)} %param.13) | copy-start | bytes 1572868
  172.1 11.0 %collective-permute-start.7 = (f32[64,128]{1,0:T(8,128)S(1)}, f32[64,128]{1,0:T(8,128)S(1)}, u32[]{:S(2)}, u32[]{:S(2)}) collective-permute-start(f32[64,128]{1,0:T(8,128)S(1)} %convert_reduce_fusion), channel_id=1, source_target_pairs={{0,2},{2,0},{1,3},{3,1},{4,6},{6,4},{5,7},{7,5},{8,10},{10,8},{9,1... | collective-permute-start | bytes 98312 | tf_op jit(solution)/shard_map/ppermute | solution.py:309
  174.7 13.2 %collective-permute-start.10 = (bf16[4,32,128]{2,1,0:T(8,128)(2,1)S(1)}, bf16[4,32,128]{2,1,0:T(8,128)(2,1)S(1)}, u32[]{:S(2)}, u32[]{:S(2)}) collective-permute-start(bf16[4,32,128]{2,1,0:T(8,128)(2,1)S(1)} %get-tuple-element.48), channel_id=1, source_target_pairs={{0,288},{32,256},{64,352},{96,320},{128,416},{160,384},{192,480},{... | collective-permute-start | bytes 98312 | tf_op jit(solution)/shard_map/ppermute | solution.py:309
  177.2 10.8 %collective-permute-start.8 = (bf16[4,32,128]{2,1,0:T(8,128)(2,1)S(1)}, bf16[4,32,128]{2,1,0:T(8,128)(2,1)S(1)}, u32[]{:S(2)}, u32[]{:S(2)}) collective-permute-start(bf16[4,32,128]{2,1,0:T(8,128)(2,1)S(1)} %get-tuple-element.46), channel_id=1, source_target_pairs={{0,32},{32,0},{64,96},{96,64},{128,160},{160,128},{192,224},{224,1... | collective-permute-start | bytes 98312 | tf_op jit(solution)/shard_map/ppermute | solution.py:309
  181.1 6.9 %collective-permute-start.9 = (bf16[4,32,128]{2,1,0:T(8,128)(2,1)S(1)}, bf16[4,32,128]{2,1,0:T(8,128)(2,1)S(1)}, u32[]{:S(2)}, u32[]{:S(2)}) collective-permute-start(bf16[4,32,128]{2,1,0:T(8,128)(2,1)S(1)} %get-tuple-element.47), channel_id=1, source_target_pairs={{0,256},{32,288},{64,320},{96,352},{128,384},{160,416},{192,448},{... | collective-permute-start | bytes 98312 | tf_op jit(solution)/shard_map/ppermute | solution.py:309
  183.9 15.9 %all-to-all-start.4 = ((bf16[16,64,128]{2,1,0:T(8,128)(2,1)}), bf16[16,64,128]{2,1,0:T(8,128)(2,1)S(1)}, u32[]{:S(2)}, u32[]{:S(2)}) async-start(bf16[16,64,128]{2,1,0:T(8,128)(2,1)} %broadcast_in_dim.2), calls=%async_computation.4 | async-start | bytes 524288 | tf_op jit(solution)/shard_map/all_to_all | solution.py:350
  199.8 17.6 %collective-permute-start.11 = (bf16[32,128]{1,0:T(8,128)(2,1)S(1)}, bf16[32,128]{1,0:T(8,128)(2,1)S(1)}, u32[]{:S(2)}, u32[]{:S(2)}) collective-permute-start(bf16[32,128]{1,0:T(8,128)(2,1)S(1)} %get-tuple-element.52), channel_id=1, source_target_pairs={{0,64},{32,96},{64,0},{96,32},{128,192},{160,224},{192,128},{224,1... | collective-permute-start | bytes 24584 | tf_op jit(solution)/shard_map/ppermute | solution.py:309
  209.2 8.3 %collective-permute-start.12 = (bf16[32,128]{1,0:T(8,128)(2,1)S(1)}, bf16[32,128]{1,0:T(8,128)(2,1)S(1)}, u32[]{:S(2)}, u32[]{:S(2)}) collective-permute-start(bf16[32,128]{1,0:T(8,128)(2,1)S(1)} %get-tuple-element.53), channel_id=1, source_target_pairs={{0,128},{32,160},{64,192},{96,224},{128,0},{160,32},{192,64},{224,... | collective-permute-start | bytes 24584 | tf_op jit(solution)/shard_map/ppermute | solution.py:309
  211.1 6.9 %collective-permute-start.13 = (bf16[32,128]{1,0:T(8,128)(2,1)S(1)}, bf16[32,128]{1,0:T(8,128)(2,1)S(1)}, u32[]{:S(2)}, u32[]{:S(2)}) collective-permute-start(bf16[32,128]{1,0:T(8,128)(2,1)S(1)} %get-tuple-element.54), channel_id=1, source_target_pairs={{0,192},{32,224},{64,128},{96,160},{128,64},{160,96},{192,0},{224,... | collective-permute-start | bytes 24584 | tf_op jit(solution)/shard_map/ppermute | solution.py:309
  (12 other events, 49.6 us)
Sparse Core Ops, SparseCore 0:
  17.7 59.6 all-gather.5
  80.1 35.3 all-gather.3

commit v3 on v2

--- a/solution.py
+++ b/solution.py
@@ -24,7 +24,8 @@
 RANK = 128
 GROUP = 14
 CHUNK = 32
-XROWS = 80
+EARLY = 4
+SPAN = POOL + E
 BLOCKS = DX // E
 BAGS = N * F
 LEARN = 0.5
@@ -33,6 +34,7 @@
 
 VMEM = pl.BlockSpec(memory_space=pltpu.VMEM)
 SMEM = pl.BlockSpec(memory_space=pltpu.SMEM)
+ANY = pl.BlockSpec(memory_space=pl.ANY)
 
 
 def iota(shape, axis):
@@ -43,13 +45,13 @@
     return lax.dot_general(a, b, (((ca,), (cb,)), ((), ())), preferred_element_type=F32)
 
 
-def call(kernel, outs, ins, name, scratch=(), limit=40, flops=0):
+def call(kernel, outs, ins, name, scratch=(), limit=40, flops=0, far=(), far_out=()):
     nbytes = sum(x.size * x.dtype.itemsize for x in ins)
     return pl.pallas_call(
         kernel,
         out_shape=outs,
-        in_specs=[SMEM if x.size < 8 else VMEM for x in ins],
-        out_specs=jax.tree.map(lambda _: VMEM, outs),
+        in_specs=[SMEM if x.size < 8 else ANY if i in far else VMEM for i, x in enumerate(ins)],
+        out_specs=[ANY if i in far_out else VMEM for i in range(len(outs))],
         scratch_shapes=scratch,
         compiler_params=pltpu.CompilerParams(vmem_limit_bytes=limit << 20),
         cost_estimate=pl.CostEstimate(flops=flops, bytes_accessed=nbytes, transcendentals=0),
@@ -58,8 +60,19 @@
 
 
 def index_kernel(
-    shard_ref, row_ref, len_ref, down_ref, up_ref, ids_ref, src_ref, src_t_ref, pack_ref
+    shard_hbm, row_hbm, len_hbm, down_ref, up_ref, ids_ref, src_ref, src_t_ref, pack_ref,
+    shard_ref, row_ref, len_ref, sems,
 ):
+    moves = [(shard_hbm, shard_ref), (row_hbm, row_ref), (len_hbm, len_ref)]
+    moves.append((down_ref, pack_ref.at[pl.ds(0, DX), :]))
+    for j in range(BLOCKS):
+        moves.append((up_ref.at[:, pl.ds(j * E, E)], pack_ref.at[pl.ds(DX + j * E, E), :]))
+    moves = [pltpu.make_async_copy(a, b, sems.at[i]) for i, (a, b) in enumerate(moves)]
+    for move in moves:
+        move.start()
+    for move in moves[:3]:
+        move.wait()
+
     def spread(values):
         parts = []
         for j in range(BAG):
@@ -67,9 +80,6 @@
             parts.append(dot(pick, values.astype(F32).astype(BF)))
         return jnp.concatenate(parts, axis=1)
 
-    for j in range(DX // E):
-        pack_ref[j] = down_ref[j * E : (j + 1) * E, :]
-        pack_ref[DX // E + j] = up_ref[:, j * E : (j + 1) * E]
     shard = spread(shard_ref[...].reshape(LOOK, N))
     rows = row_ref[...]
     row_lo, row_hi = spread(rows & 255), spread(rows >> 8)
@@ -108,6 +118,8 @@
     ids_ref[...] = ids.astype(I32)
     src_ref[...] = src.astype(I32) - 1
     src_t_ref[...] = src_t.astype(I32) - 1
+    for move in moves[3:]:
+        move.wait()
 
 
 def fetch_kernel(ids_ref, table_ref, out_ref):
@@ -119,10 +131,24 @@
         out_ref[s] = dot(pick, table).astype(BF)
 
 
-def pool_kernel(where_ref, rows_ref, src_ref, dense_ref, out_ref, acc_ref):
+def main_kernel(
+    where_ref, rows_ref, src_ref, dense_ref, pack_ref, bias_ref, head_ref, label_ref,
+    feedback_ref, src_t_ref, carried_ref, send_ref, span_ref,
+    acc_ref, x_ref, down_ref, up_ref, small_ref, sems,
+):
+    moves = []
+    for k in range(TP):
+        block = pl.ds(k * RANK, RANK)
+        moves.append((pack_ref.at[k, pl.ds(0, DX), :], down_ref.at[:, block]))
+        for j in range(BLOCKS):
+            lanes = pl.ds(j * E, E)
+            moves.append((pack_ref.at[k, pl.ds(DX + j * E, E), :], up_ref.at[block, lanes]))
+    moves = [pltpu.make_async_copy(a, b, sems.at[i]) for i, (a, b) in enumerate(moves)]
+    for move in moves:
+        move.start()
+
     first = pl.multiple_of(where_ref[0] * N, N)
-    out_ref[0:N, 0:E] = dense_ref[pl.ds(first, N), :]
-    out_ref[N:, :] = jnp.zeros((XROWS - N, DX), BF)
+    x_ref[:, 0:E] = dense_ref[pl.ds(first, N), :]
     bags = iota((BAGS, CAP), 0)
     for s in range(SHARDS):
         pick = jnp.where(bags == src_ref[s : s + 1, :], 1.0, 0.0).astype(BF)
@@ -132,20 +158,12 @@
         else:
             acc_ref[...] += term
     for f in range(F):
-        out_ref[0:N, (f + 1) * E : (f + 2) * E] = acc_ref[f * N : (f + 1) * N, :].astype(BF)
-
-
-def dense_kernel(
-    where_ref, x_ref, pack_ref, bias_ref, head_ref, label_ref, feedback_ref, src_t_ref,
-    carried_ref, send_ref, small_ref, down_ref, up_ref,
-):
-    first = pl.multiple_of(where_ref[0] * N, N)
-    for k in range(TP):
-        block = slice(k * RANK, (k + 1) * RANK)
-        for j in range(BLOCKS):
-            down_ref[j * E : (j + 1) * E, block] = pack_ref[k, j]
-            up_ref[block, j * E : (j + 1) * E] = pack_ref[k, BLOCKS + j]
-    x = x_ref[0:N, :]
+        pooled = acc_ref[f * N : (f + 1) * N, :].astype(BF)
+        x_ref[:, (f + 1) * E : (f + 2) * E] = pooled
+        span_ref[:, f * E : (f + 1) * E] = pooled
+    for move in moves:
+        move.wait()
+    x = x_ref[...]
     hidden = dot(x, down_ref[...]).astype(BF)
     up = up_ref[...]
     crossed = dot(hidden, up)
@@ -166,32 +184,46 @@
     for s in range(SHARDS):
         pick = jnp.where(src_t_ref[:, s : s + 1] == bags, 1.0, 0.0).astype(BF)
         send_ref[s] = dot(pick, by_bag).astype(BF)
-    small_ref[0:N, :] = jnp.broadcast_to(grad_logit, (N, E))
     grad_head = jnp.sum(grad_logit * x_next, axis=0, keepdims=True)
-    for j in range(DX // E):
-        small_ref[N + j : N + j + 1, :] = grad_head[:, j * E : (j + 1) * E]
-    small_ref[N + DX // E :, :] = jnp.zeros((2, E), F32)
-
-
-def grads_kernel(
-    where_ref, x_ref, down_ref, up_ref, head_ref, s0_ref, s1_ref, s2_ref, s3_ref,
-    keep_ref, send_ref, logit_ref, down_grad_ref, up_grad_ref, stage_ref,
-):
+    small_ref[...] = jnp.zeros((N, E), F32)
+    for j in range(BLOCKS):
+        part = grad_head[:, j * E : (j + 1) * E]
+        high = part.astype(BF).astype(F32)
+        small_ref[j : j + 1, :] = high
+        small_ref[BLOCKS + j : BLOCKS + j + 1, :] = part - high
+    diagonal = iota((N, N), 0) == iota((N, N), 1)
+    part = jnp.sum(jnp.where(diagonal, grad_logit, 0.0), axis=0, keepdims=True)
+    high = part.astype(BF).astype(F32)
+    small_ref[2 * BLOCKS : 2 * BLOCKS + 1, 0:N] = high
+    small_ref[2 * BLOCKS + 1 : 2 * BLOCKS + 2, 0:N] = part - high
+    span_ref[:, POOL:] = small_ref[...].astype(BF)
+
+
+def grads_kernel(where_ref, s0_ref, s1_ref, s2_ref, s3_ref, dense_ref, down_ref, up_ref, head_ref, *rest):
+    outs, (x_ref, logit_ref, down_grad_ref, up_grad_ref, stage_ref) = rest[:DP], rest[DP:]
     t, y, u = where_ref[0], where_ref[1], where_ref[2]
+    x_ref[:, 0:E] = dense_ref[...]
+    diagonal = iota((N, N), 0) == iota((N, N), 1)
+    heads = []
     for m, ref in enumerate((s0_ref, s1_ref, s2_ref, s3_ref)):
-        logit_ref[pl.ds(pl.multiple_of((t ^ m) * N, N), N), :] = ref[0:N, :]
-    x = jnp.concatenate([x_ref[XROWS * k : XROWS * k + N, :] for k in range(TP)], axis=0)
+        rows = pl.ds(pl.multiple_of((t ^ m) * N, N), N)
+        x_ref[rows, E:] = ref[:, :POOL]
+        tail = ref[:, POOL:].astype(F32)
+        heads.append(tail[0:BLOCKS] + tail[BLOCKS : 2 * BLOCKS])
+        row = tail[2 * BLOCKS : 2 * BLOCKS + 1, 0:N] + tail[2 * BLOCKS + 1 : 2 * BLOCKS + 2, 0:N]
+        logit_ref[rows, :] = jnp.sum(jnp.where(diagonal, row, 0.0), axis=1, keepdims=True)
+    heads = (heads[0] + heads[1]) + (heads[2] + heads[3])
+    x = x_ref[...]
+    grad_logit = logit_ref[...]
     xf = x.astype(F32)
     hidden = dot(x, down_ref[...]).astype(BF)
-    cross = logit_ref[:, 0:1] * head_ref[...] * xf
+    cross = grad_logit * head_ref[...] * xf
     grad_bias = jnp.sum(cross, axis=0, keepdims=True)
     grad_cross = cross.astype(BF)
     grad_hidden = dot(grad_cross, up_ref[...], 1, 1).astype(BF)
     down_grad_ref[...] = dot(x, grad_hidden, 0, 0).astype(BF)
     up_grad_ref[...] = dot(grad_cross, hidden, 0, 0).astype(BF)
 
-    tail = slice(N, N + DX // E)
-    heads = (s0_ref[tail, :] + s1_ref[tail, :]) + (s2_ref[tail, :] + s3_ref[tail, :])
     grad_head = jnp.concatenate([heads[j : j + 1, :] for j in range(DX // E)], axis=1)
     groups = DX // GROUP
     r = iota((groups, DX), 1) - GROUP * iota((groups, DX), 0)
@@ -231,10 +263,9 @@
         w = u ^ e
         place = ((w >> 3) & 1) * 8 + (w & 1) * 4 + ((w >> 1) & 3)
         for k in range(DP):
-            v = y ^ k
-            stage_ref[v & 1, v >> 1, place] = got[CHUNK * k : CHUNK * (k + 1)]
-    keep_ref[...] = stage_ref[0]
-    send_ref[...] = stage_ref[1]
+            stage_ref[y ^ k, place] = got[CHUNK * k : CHUNK * (k + 1)]
+    for m in range(DP):
+        outs[m][...] = stage_ref[m]
 
 
 def scatter_kernel(ids_ref, rows_ref, out_ref, acc_ref):
@@ -272,35 +303,47 @@
             sds((SHARDS, CAP), I32),
             sds((SHARDS, CAP), I32),
             sds((CAP, SHARDS), I32),
-            sds((2 * BLOCKS, E, E), BF),
+            sds((2 * DX, E), BF),
         ),
         (row_shard.transpose(1, 2, 0), local_row.T, bag_length.T, cross_down, cross_up),
         "index",
+        scratch=[
+            pltpu.VMEM((LOOK, 1, N), I32),
+            pltpu.VMEM((LOOK, N), I32),
+            pltpu.VMEM((F, N), I32),
+            pltpu.SemaphoreType.DMA((4 + BLOCKS,)),
+        ],
         flops=400_000_000,
+        limit=56,
+        far=range(5),
+        far_out=(3,),
     )
     with jax.named_scope("gather_weights"):
         pack_all = lax.all_gather(pack, TPA, axis=0, tiled=False)
     ids = lax.all_to_all(ids, EMB, split_axis=0, concat_axis=0, tiled=True)
-    fetched = call(
-        fetch_kernel, sds((SHARDS, CAP, E), BF), (ids, emb_table), "fetch", flops=1_300_000_000
+    (fetched,) = call(
+        fetch_kernel, [sds((SHARDS, CAP, E), BF)], (ids, emb_table), "fetch", flops=1_300_000_000
     )
     returned = lax.all_to_all(fetched, EMB, split_axis=0, concat_axis=0, tiled=True)
-    x = call(
-        pool_kernel,
-        sds((XROWS, DX), BF),
-        (where, returned, src, dense_input),
-        "pool",
-        scratch=[pltpu.VMEM((BAGS, E), F32)],
-        flops=1_060_000_000,
-    )
-    x_all = lax.all_gather(x, TPA, axis=0, tiled=True)
-    carried, send, small = call(
-        dense_kernel,
-        (sds((N, POOL), F32), sds((SHARDS, CAP, E), BF), sds((N + 16, E), F32)),
-        (where, x, pack_all, bias, head, labels.reshape(DENSE, 1), feedback, src_t),
-        "dense",
-        scratch=[pltpu.VMEM((DX, TP * RANK), BF), pltpu.VMEM((TP * RANK, DX), BF)],
-        flops=1_500_000_000,
+    carried, send, span = call(
+        main_kernel,
+        (sds((N, POOL), F32), sds((SHARDS, CAP, E), BF), sds((N, SPAN), BF)),
+        (
+            where, returned, src, dense_input, pack_all, bias, head, labels.reshape(DENSE, 1),
+            feedback, src_t,
+        ),
+        "main",
+        scratch=[
+            pltpu.VMEM((BAGS, E), F32),
+            pltpu.VMEM((N, DX), BF),
+            pltpu.VMEM((DX, TP * RANK), BF),
+            pltpu.VMEM((TP * RANK, DX), BF),
+            pltpu.VMEM((N, E), F32),
+            pltpu.SemaphoreType.DMA((TP * (1 + BLOCKS),)),
+        ],
+        flops=2_600_000_000,
+        limit=56,
+        far=(4,),
     )
     arrived = lax.all_to_all(send, EMB, split_axis=0, concat_axis=0, tiled=True)
 
@@ -308,35 +351,34 @@
         size = lax.axis_size(axes)
         return lax.ppermute(value, axes, [(i, i ^ mask) for i in range(size)])
 
-    s1 = partner(small, TPA, 1)
-    s2 = partner(small, TPA, 2)
-    s3 = partner(small, TPA, 3)
-    keep, give = call(
+    spans = [span] + [partner(span, TPA, m) for m in range(1, TP)]
+    part = call(
         grads_kernel,
-        [sds((DP // 2, SHARDS, CHUNK, E), BF)] * 2,
-        (where, x_all, cross_down, cross_up, head, small, s1, s2, s3),
+        [sds((SHARDS, CHUNK, E), BF)] * DP,
+        (where, *spans, dense_input, cross_down, cross_up, head),
         "grads",
         scratch=[
-            pltpu.VMEM((DENSE, E), F32),
+            pltpu.VMEM((DENSE, DX), BF),
+            pltpu.VMEM((DENSE, 1), F32),
             pltpu.VMEM((DX, RANK), BF),
             pltpu.VMEM((DX, RANK), BF),
-            pltpu.VMEM((2, DP // 2, SHARDS, CHUNK, E), BF),
+            pltpu.VMEM((DP, SHARDS, CHUNK, E), BF),
         ],
         flops=1_000_000_000,
     )
-    got = partner(give, "y", 1)
-    part = [keep[m].astype(F32) + got[m].astype(F32) for m in range(DP // 2)]
-    part = [part[0]] + [p.astype(BF) for p in part[1:]]
-    arrived, *part = lax.optimization_barrier((arrived, *part))
-    part = part[:1] + [partner(part[m], "y", 2 * m) for m in range(1, DP // 2)]
-    row_grad = call(
+    early = [partner(part[m], "y", m) for m in range(1, EARLY)]
+    arrived, *early = lax.optimization_barrier((arrived, *early))
+    (row_grad,) = call(
         scatter_kernel,
-        sds((ROWS, E), BF),
+        [sds((ROWS, E), BF)],
         (ids, arrived),
         "scatter",
         scratch=[pltpu.VMEM((ROWS, E), F32)],
         flops=1_300_000_000,
     )
+    row_grad, *late = lax.optimization_barrier((row_grad, *part[EARLY:]))
+    late = [partner(v, "y", m) for m, v in enumerate(late, EARLY)]
+    part = [part[0], *early, *late]
     owners = ("y", "core")
     pieces = 2 * DP
     by_y = lax.all_to_all(row_grad, owners, split_axis=0, concat_axis=0, tiled=True)

time: 227 us -> 262 us (1.15)
  Pallas kernels: 29.3 us -> 52.5 us
  starting transfers between devices: 76.2 us -> 92.3 us
  local copies, waits for them, and re-layouts: 9.68 us -> 6.26 us
    pallas_call x6 -> x5, Pallas kernels: 29.3 us -> 52.5 us  [call(): pl.pallas_call(kernel, out_shape=outs, in_specs=[SMEM if x.size < 8 else...]
    ppermute x14 -> x17, waiting for transfers between devices: 12.6 us -> 29.7 us  [partner(): return lax.ppermute(value, axes, [(i, i ^ mask) for i in range(size)])]
    ppermute x14 -> x17, starting transfers between devices: 52.4 us -> 63.9 us  [partner(): return lax.ppermute(value, axes, [(i, i ^ mask) for i in range(size)])]
    all_gather x1 -> x0, waiting for transfers between devices: 10.7 us -> none  [local(): x_all = lax.all_gather(x, TPA, axis=0, tiled=True)]
    all_to_all x1, waiting for transfers between devices: 11.6 us -> 3.82 us  [local(): lax.all_to_all(row_grad, owners, split_axis=0, concat_axis=0, tiled=True)]
    unnamed x33 -> x29, local copies, waits for them, and re-layouts: 7.54 us -> 1.55 us
    all_to_all x1, starting transfers between devices: 4.03 us -> 6.96 us  [local(): lax.all_to_all(spread, owners, split_axis=0, concat_axis=0, tiled=True)]
  transfers between devices with their start and end apart: 20 -> 22, of which waited for: 7 -> 11; matrix products, arithmetic and copies ran while one was open for 1% -> 2% of each run, Pallas kernels for 10% -> 3%
where the time goes in v3:
time: 262 us; the launch traced here: 261 us
  starting transfers between devices  92.3 us (35%)
  waiting for transfers between devices  74.3 us (28%)
  Pallas kernels  52.5 us (20%)
  blocking collectives  19 us (7%)
  between operations  14.5 us (6%)
  local copies, waits for them, and re-layouts  6.26 us (2%)
    ppermute x17, starting transfers between devices, partner(): return lax.ppermute(value, axes, [(i, i ^ mask) for i in range(size)])  63.9 us
    pallas_call x5, Pallas kernels, call(): pl.pallas_call(kernel, out_shape=outs, in_specs=[SMEM if x.size < 8 else...  52.5 us
    ppermute x17, waiting for transfers between devices, partner(): return lax.ppermute(value, axes, [(i, i ^ mask) for i in range(size)])  29.7 us
    all_to_all x1, waiting for transfers between devices, local(): lax.all_to_all(fetched, EMB, split_axis=0, concat_axis=0, tiled=True)  26.9 us
    all_to_all x1, blocking collectives, local(): ids = lax.all_to_all(ids, EMB, split_axis=0, concat_axis=0, tiled=True)  19 us
    all_to_all x1, waiting for transfers between devices, local(): lax.all_to_all(spread, owners, split_axis=0, concat_axis=0, tiled=True)  11.6 us
    all_to_all x1, starting transfers between devices, local(): lax.all_to_all(row_grad, owners, split_axis=0, concat_axis=0, tiled=True)  9.16 us
    all_to_all x1, starting transfers between devices, local(): arrived = lax.all_to_all(send, EMB, split_axis=0, concat_axis=0, tiled=True)  8.23 us
  transfers between devices with their start and end apart: 22, of which 11 were waited for; matrix products, arithmetic and copies ran while one was open for 2% of the time, Pallas kernels for 3%

profile of v3, /device:TPU:1, one launch (start us, length us, event | category | flops | bytes accessed | tf_op | source)
XLA Modules:
  0.0 260.7 jit_solution(15718741201789785512)
XLA Ops:
  7.2 29.7 %index.1 = (s32[16,312]{1,0:T(8,128)}, s32[16,312]{1,0:T(8,128)}, s32[312,16]{1,0:T(8,128)}, bf16[3584,128]{1,0:T(8,128)(2,1)}) custom-call(s32[52,1,64]{2,1,0:T(1,128)} %bitcast.38, s32[52,64]{1,0:T(8,128)} %bitcast.37, s32[13,64]{1,0:T(8,128)} %bitcast.39, bf16[1792,128]{1,0:T(8,128)(2,1)} %down_ref.3, bf16[128,1792]{1,0:T(8,128)(2,1)} %up_ref.3), custom_call_target="tpu_custom_call" | custom-call | flops 400000000 | bytes 947456 | tf_op jit(solution)/shard_map/index/pallas_call | solution.py:50
  37.8 19.0 %all_to_all.42 = s32[16,1,312]{2,1,0:T(1,128)S(1)} all-to-all(s32[16,1,312]{2,1,0:T(1,128)S(1)} %copy.20), channel_id=1, replica_groups=mesh['xl'=2,'z'=8,'y'=8,'xh'=2,'core'=2] {'xl','z'}, dimensions={0} | all-to-all | bytes 39936 | tf_op jit(solution)/shard_map/all_to_all | solution.py:323
  56.8 4.2 %fetch.1 = bf16[16,312,128]{2,1,0:T(8,128)(2,1)} custom-call(s32[16,312]{1,0:T(8,128)S(1)} %bitcast.31, f32[1024,128]{1,0:T(8,128)S(1)} %copy-done), custom_call_target="tpu_custom_call" | custom-call | flops 1300000000 | bytes 544256 | tf_op jit(solution)/shard_map/fetch/pallas_call | solution.py:50
  61.0 4.0 %all-to-all-start.1 = ((bf16[16,312,128]{2,1,0:T(8,128)(2,1)}), bf16[16,312,128]{2,1,0:T(8,128)(2,1)S(1)}, u32[]{:S(2)}, u32[]{:S(2)}) async-start(bf16[16,312,128]{2,1,0:T(8,128)(2,1)} %fetch.1), calls=%async_computation.1 | async-start | bytes 2555904 | tf_op jit(solution)/shard_map/all_to_all | solution.py:327
  67.6 26.9 %all-to-all-done.1.rows_ref = bf16[16,312,128]{2,1,0:T(8,128)(2,1)S(1)} async-done(((bf16[16,312,128]{2,1,0:T(8,128)(2,1)}), bf16[16,312,128]{2,1,0:T(8,128)(2,1)S(1)}, u32[]{:S(2)}, u32[]{:S(2)}) %all-to-all-start.1) | async-done | bytes 1277984 | tf_op jit(solution)/shard_map/all_to_all | solution.py:327
  96.7 10.9 %main.1 = (f32[64,1664]{1,0:T(8,128)}, bf16[16,312,128]{2,1,0:T(8,128)(2,1)}, bf16[64,1792]{1,0:T(8,128)(2,1)}) custom-call(s32[3]{0:T(128)} %pad_add_fusion.where_ref, bf16[16,312,128]{2,1,0:T(8,128)(2,1)} %copy-done.9, s32[16,312]{1,0:T(8,128)} %get-tuple-element.42.src_ref, bf16[256,128]{1,0:T(8,128)(2,1)} %dense_ref.3, bf16[4,3584,128]{2,1,0:T(8,128)(2,1)} %bitcast.36, ...), custom_call_target="tpu_custom_call" | custom-call | flops 2600000000 | bytes 5494796 | tf_op jit(solution)/shard_map/main/pallas_call | solution.py:50
  107.8 8.2 %all-to-all-start.2 = ((bf16[16,312,128]{2,1,0:T(8,128)(2,1)}), bf16[16,312,128]{2,1,0:T(8,128)(2,1)S(1)}, u32[]{:S(2)}, u32[]{:S(2)}) async-start(bf16[16,312,128]{2,1,0:T(8,128)(2,1)} %get-tuple-element.45), calls=%async_computation.2 | async-start | bytes 2555904 | tf_op jit(solution)/shard_map/all_to_all | solution.py:348
  116.0 4.1 %collective-permute-start.2 = (bf16[64,1792]{1,0:T(8,128)(2,1)S(1)}, bf16[64,1792]{1,0:T(8,128)(2,1)S(1)}, u32[]{:S(2)}, u32[]{:S(2)}) collective-permute-start(bf16[64,1792]{1,0:T(8,128)(2,1)S(1)} %copy-done.5), channel_id=1, source_target_pairs={{0,3},{1,2},{2,1},{3,0},{4,7},{5,6},{6,5},{7,4},{8,11},{9,10},{10,... | collective-permute-start | bytes 688136 | tf_op jit(solution)/shard_map/ppermute | solution.py:352
  125.4 5.5 %collective-permute-done.2.s3_ref = bf16[64,1792]{1,0:T(8,128)(2,1)S(1)} collective-permute-done((bf16[64,1792]{1,0:T(8,128)(2,1)S(1)}, bf16[64,1792]{1,0:T(8,128)(2,1)S(1)}, u32[]{:S(2)}, u32[]{:S(2)}) %collective-permute-start.2) | collective-permute-done | bytes 229408 | tf_op jit(solution)/shard_map/ppermute | solution.py:352
  130.9 9.5 %collective-permute-done.1.s2_ref = bf16[64,1792]{1,0:T(8,128)(2,1)S(1)} collective-permute-done((bf16[64,1792]{1,0:T(8,128)(2,1)S(1)}, bf16[64,1792]{1,0:T(8,128)(2,1)S(1)}, u32[]{:S(2)}, u32[]{:S(2)}) %collective-permute-start.1) | collective-permute-done | bytes 229408 | tf_op jit(solution)/shard_map/ppermute | solution.py:352
  148.5 4.0 %collective-permute-start.4 = (bf16[16,32,128]{2,1,0:T(8,128)(2,1)S(1)}, bf16[16,32,128]{2,1,0:T(8,128)(2,1)S(1)}, u32[]{:S(2)}, u32[]{:S(2)}) collective-permute-start(bf16[16,32,128]{2,1,0:T(8,128)(2,1)S(1)} %get-tuple-element.48), channel_id=1, source_target_pairs={{0,8},{4,12},{8,0},{12,4},{16,24},{20,28},{24,16},{28,20},{1,9},{5... | collective-permute-start | bytes 393224 | tf_op jit(solution)/shard_map/ppermute | solution.py:352
  160.3 4.2 %scatter.1 = bf16[1024,128]{1,0:T(8,128)(2,1)} custom-call(s32[16,312]{1,0:T(8,128)S(1)} %bitcast.32, bf16[16,312,128]{2,1,0:T(8,128)(2,1)S(1)} %all-to-all-done.2.rows_ref), custom_call_target="tpu_custom_call" | custom-call | flops 1300000000 | bytes 1297920 | tf_op jit(solution)/shard_map/scatter/pallas_call | solution.py:50
  164.5 7.2 %collective-permute-start.6 = (bf16[16,32,128]{2,1,0:T(8,128)(2,1)S(1)}, bf16[16,32,128]{2,1,0:T(8,128)(2,1)S(1)}, u32[]{:S(2)}, u32[]{:S(2)}) collective-permute-start(bf16[16,32,128]{2,1,0:T(8,128)(2,1)S(1)} %copy-done.7), channel_id=1, source_target_pairs={{0,16},{4,20},{8,24},{12,28},{16,0},{20,4},{24,8},{28,12},{1,17},{... | collective-permute-start | bytes 393224 | tf_op jit(solution)/shard_map/ppermute | solution.py:352
  171.7 5.2 %collective-permute-start.7 = (bf16[16,32,128]{2,1,0:T(8,128)(2,1)S(1)}, bf16[16,32,128]{2,1,0:T(8,128)(2,1)S(1)}, u32[]{:S(2)}, u32[]{:S(2)}) collective-permute-start(bf16[16,32,128]{2,1,0:T(8,128)(2,1)S(1)} %get-tuple-element.61), channel_id=1, source_target_pairs={{0,20},{4,16},{8,28},{12,24},{16,4},{20,0},{24,12},{28,8},{1,21},{... | collective-permute-start | bytes 393224 | tf_op jit(solution)/shard_map/ppermute | solution.py:352
  178.8 4.5 %collective-permute-start.9 = (bf16[16,32,128]{2,1,0:T(8,128)(2,1)S(1)}, bf16[16,32,128]{2,1,0:T(8,128)(2,1)S(1)}, u32[]{:S(2)}, u32[]{:S(2)}) collective-permute-start(bf16[16,32,128]{2,1,0:T(8,128)(2,1)S(1)} %get-tuple-element.63), channel_id=1, source_target_pairs={{0,28},{4,24},{8,20},{12,16},{16,12},{20,8},{24,4},{28,0},{1,29},{... | collective-permute-start | bytes 393224 | tf_op jit(solution)/shard_map/ppermute | solution.py:352
  183.3 9.2 %all-to-all-start.3 = ((bf16[16,64,128]{2,1,0:T(8,128)(2,1)}), bf16[16,64,128]{2,1,0:T(8,128)(2,1)S(1)}, u32[]{:S(2)}, u32[]{:S(2)}) async-start(bf16[16,64,128]{2,1,0:T(8,128)(2,1)} %bitcast.9), calls=%async_computation.3 | async-start | bytes 524288 | tf_op jit(solution)/shard_map/all_to_all | solution.py:384
  193.2 5.3 %collective-permute-done.9 = bf16[16,32,128]{2,1,0:T(8,128)(2,1)S(1)} collective-permute-done((bf16[16,32,128]{2,1,0:T(8,128)(2,1)S(1)}, bf16[16,32,128]{2,1,0:T(8,128)(2,1)S(1)}, u32[]{:S(2)}, u32[]{:S(2)}) %collective-permute-start.9) | collective-permute-done | bytes 131104 | tf_op jit(solution)/shard_map/ppermute | solution.py:352
  198.6 3.8 %all-to-all-done.3 = bf16[16,64,128]{2,1,0:T(8,128)(2,1)S(1)} async-done(((bf16[16,64,128]{2,1,0:T(8,128)(2,1)}), bf16[16,64,128]{2,1,0:T(8,128)(2,1)S(1)}, u32[]{:S(2)}, u32[]{:S(2)}) %all-to-all-start.3) | async-done | bytes 262176 | tf_op jit(solution)/shard_map/all_to_all | solution.py:384
  202.5 4.3 %collective-permute-start.10 = (f32[64,128]{1,0:T(8,128)S(1)}, f32[64,128]{1,0:T(8,128)S(1)}, u32[]{:S(2)}, u32[]{:S(2)}) collective-permute-start(f32[64,128]{1,0:T(8,128)S(1)} %convert_reduce_fusion), channel_id=1, source_target_pairs={{0,2},{2,0},{1,3},{3,1},{4,6},{6,4},{5,7},{7,5},{8,10},{10,8},{9,1... | collective-permute-start | bytes 98312 | tf_op jit(solution)/shard_map/ppermute | solution.py:352
  206.7 4.6 %collective-permute-start.11 = (bf16[4,32,128]{2,1,0:T(8,128)(2,1)S(1)}, bf16[4,32,128]{2,1,0:T(8,128)(2,1)S(1)}, u32[]{:S(2)}, u32[]{:S(2)}) collective-permute-start(bf16[4,32,128]{2,1,0:T(8,128)(2,1)S(1)} %get-tuple-element.66), channel_id=1, source_target_pairs={{0,32},{32,0},{64,96},{96,64},{128,160},{160,128},{192,224},{224,1... | collective-permute-start | bytes 98312 | tf_op jit(solution)/shard_map/ppermute | solution.py:352
  217.1 7.0 %all-to-all-start.4 = ((bf16[16,64,128]{2,1,0:T(8,128)(2,1)}), bf16[16,64,128]{2,1,0:T(8,128)(2,1)S(1)}, u32[]{:S(2)}, u32[]{:S(2)}) async-start(bf16[16,64,128]{2,1,0:T(8,128)(2,1)} %broadcast_in_dim.2), calls=%async_computation.4 | async-start | bytes 524288 | tf_op jit(solution)/shard_map/all_to_all | solution.py:392
  224.2 11.6 %all-to-all-done.4 = bf16[16,64,128]{2,1,0:T(8,128)(2,1)S(1)} async-done(((bf16[16,64,128]{2,1,0:T(8,128)(2,1)}), bf16[16,64,128]{2,1,0:T(8,128)(2,1)S(1)}, u32[]{:S(2)}, u32[]{:S(2)}) %all-to-all-start.4) | async-done | bytes 262176 | tf_op jit(solution)/shard_map/all_to_all | solution.py:392
  235.8 5.1 %collective-permute-start.14 = (bf16[32,128]{1,0:T(8,128)(2,1)S(1)}, bf16[32,128]{1,0:T(8,128)(2,1)S(1)}, u32[]{:S(2)}, u32[]{:S(2)}) collective-permute-start(bf16[32,128]{1,0:T(8,128)(2,1)S(1)} %get-tuple-element.72), channel_id=1, source_target_pairs={{0,64},{32,96},{64,0},{96,32},{128,192},{160,224},{192,128},{224,1... | collective-permute-start | bytes 24584 | tf_op jit(solution)/shard_map/ppermute | solution.py:352
  240.9 5.3 %collective-permute-start.15 = (bf16[32,128]{1,0:T(8,128)(2,1)S(1)}, bf16[32,128]{1,0:T(8,128)(2,1)S(1)}, u32[]{:S(2)}, u32[]{:S(2)}) collective-permute-start(bf16[32,128]{1,0:T(8,128)(2,1)S(1)} %get-tuple-element.73), channel_id=1, source_target_pairs={{0,128},{32,160},{64,192},{96,224},{128,0},{160,32},{192,64},{224,... | collective-permute-start | bytes 24584 | tf_op jit(solution)/shard_map/ppermute | solution.py:352
  (74 shorter events, 43.1 us)
Async XLA Ops:
  7.2 89.6 %all-gather.3.cloned.1.call-start = ((), (), s32[]{:S(2)}) async-start(), calls=%async_computation.5 | async-start | bytes 4587520 | tf_op jit(solution)/shard_map/gather_weights/all_gather | solution.py:322
  7.2 49.6 %copy-start = (f32[1024,128]{1,0:T(8,128)S(1)}, f32[1024,128]{1,0:T(8,128)}, u32[]{:S(2)}) copy-start(f32[1024,128]{1,0:T(8,128)} %table_ref.1) | copy-start | bytes 1572868
  61.0 33.5 %all-to-all-start.1 = ((bf16[16,312,128]{2,1,0:T(8,128)(2,1)}), bf16[16,312,128]{2,1,0:T(8,128)(2,1)S(1)}, u32[]{:S(2)}, u32[]{:S(2)}) async-start(bf16[16,312,128]{2,1,0:T(8,128)(2,1)} %fetch.1), calls=%async_computation.1 | async-start | bytes 2555904 | tf_op jit(solution)/shard_map/all_to_all | solution.py:327
  107.8 52.6 %all-to-all-start.2 = ((bf16[16,312,128]{2,1,0:T(8,128)(2,1)}), bf16[16,312,128]{2,1,0:T(8,128)(2,1)S(1)}, u32[]{:S(2)}, u32[]{:S(2)}) async-start(bf16[16,312,128]{2,1,0:T(8,128)(2,1)} %get-tuple-element.45), calls=%async_computation.2 | async-start | bytes 2555904 | tf_op jit(solution)/shard_map/all_to_all | solution.py:348
  116.0 14.9 %collective-permute-start.2 = (bf16[64,1792]{1,0:T(8,128)(2,1)S(1)}, bf16[64,1792]{1,0:T(8,128)(2,1)S(1)}, u32[]{:S(2)}, u32[]{:S(2)}) collective-permute-start(bf16[64,1792]{1,0:T(8,128)(2,1)S(1)} %copy-done.5), channel_id=1, source_target_pairs={{0,3},{1,2},{2,1},{3,0},{4,7},{5,6},{6,5},{7,4},{8,11},{9,10},{10,... | collective-permute-start | bytes 688136 | tf_op jit(solution)/shard_map/ppermute | solution.py:352
  120.1 20.3 %collective-permute-start.1 = (bf16[64,1792]{1,0:T(8,128)(2,1)S(1)}, bf16[64,1792]{1,0:T(8,128)(2,1)S(1)}, u32[]{:S(2)}, u32[]{:S(2)}) collective-permute-start(bf16[64,1792]{1,0:T(8,128)(2,1)S(1)} %copy-done.5), channel_id=1, source_target_pairs={{0,2},{1,3},{2,0},{3,1},{4,6},{5,7},{6,4},{7,5},{8,10},{9,11},{10,... | collective-permute-start | bytes 688136 | tf_op jit(solution)/shard_map/ppermute | solution.py:352
  123.2 17.1 %collective-permute-start = (bf16[64,1792]{1,0:T(8,128)(2,1)S(1)}, bf16[64,1792]{1,0:T(8,128)(2,1)S(1)}, u32[]{:S(2)}, u32[]{:S(2)}) collective-permute-start(bf16[64,1792]{1,0:T(8,128)(2,1)S(1)} %copy-done.5), channel_id=1, source_target_pairs={{0,1},{1,0},{2,3},{3,2},{4,5},{5,4},{6,7},{7,6},{8,9},{9,8},{10,11... | collective-permute-start | bytes 688136 | tf_op jit(solution)/shard_map/ppermute | solution.py:352
  145.4 9.7 %collective-permute-start.3 = (bf16[16,32,128]{2,1,0:T(8,128)(2,1)S(1)}, bf16[16,32,128]{2,1,0:T(8,128)(2,1)S(1)}, u32[]{:S(2)}, u32[]{:S(2)}) collective-permute-start(bf16[16,32,128]{2,1,0:T(8,128)(2,1)S(1)} %get-tuple-element.47), channel_id=1, source_target_pairs={{0,4},{4,0},{8,12},{12,8},{16,20},{20,16},{24,28},{28,24},{1,5},{5... | collective-permute-start | bytes 393224 | tf_op jit(solution)/shard_map/ppermute | solution.py:352
  148.5 10.3 %collective-permute-start.4 = (bf16[16,32,128]{2,1,0:T(8,128)(2,1)S(1)}, bf16[16,32,128]{2,1,0:T(8,128)(2,1)S(1)}, u32[]{:S(2)}, u32[]{:S(2)}) collective-permute-start(bf16[16,32,128]{2,1,0:T(8,128)(2,1)S(1)} %get-tuple-element.48), channel_id=1, source_target_pairs={{0,8},{4,12},{8,0},{12,4},{16,24},{20,28},{24,16},{28,20},{1,9},{5... | collective-permute-start | bytes 393224 | tf_op jit(solution)/shard_map/ppermute | solution.py:352
  152.6 7.7 %collective-permute-start.5 = (bf16[16,32,128]{2,1,0:T(8,128)(2,1)S(1)}, bf16[16,32,128]{2,1,0:T(8,128)(2,1)S(1)}, u32[]{:S(2)}, u32[]{:S(2)}) collective-permute-start(bf16[16,32,128]{2,1,0:T(8,128)(2,1)S(1)} %get-tuple-element.49), channel_id=1, source_target_pairs={{0,12},{4,8},{8,4},{12,0},{16,28},{20,24},{24,20},{28,16},{1,13},{... | collective-permute-start | bytes 393224 | tf_op jit(solution)/shard_map/ppermute | solution.py:352
  164.5 28.0 %collective-permute-start.6 = (bf16[16,32,128]{2,1,0:T(8,128)(2,1)S(1)}, bf16[16,32,128]{2,1,0:T(8,128)(2,1)S(1)}, u32[]{:S(2)}, u32[]{:S(2)}) collective-permute-start(bf16[16,32,128]{2,1,0:T(8,128)(2,1)S(1)} %copy-done.7), channel_id=1, source_target_pairs={{0,16},{4,20},{8,24},{12,28},{16,0},{20,4},{24,8},{28,12},{1,17},{... | collective-permute-start | bytes 393224 | tf_op jit(solution)/shard_map/ppermute | solution.py:352
  171.7 20.8 %collective-permute-start.7 = (bf16[16,32,128]{2,1,0:T(8,128)(2,1)S(1)}, bf16[16,32,128]{2,1,0:T(8,128)(2,1)S(1)}, u32[]{:S(2)}, u32[]{:S(2)}) collective-permute-start(bf16[16,32,128]{2,1,0:T(8,128)(2,1)S(1)} %get-tuple-element.61), channel_id=1, source_target_pairs={{0,20},{4,16},{8,28},{12,24},{16,4},{20,0},{24,12},{28,8},{1,21},{... | collective-permute-start | bytes 393224 | tf_op jit(solution)/shard_map/ppermute | solution.py:352
  176.9 16.3 %collective-permute-start.8 = (bf16[16,32,128]{2,1,0:T(8,128)(2,1)S(1)}, bf16[16,32,128]{2,1,0:T(8,128)(2,1)S(1)}, u32[]{:S(2)}, u32[]{:S(2)}) collective-permute-start(bf16[16,32,128]{2,1,0:T(8,128)(2,1)S(1)} %get-tuple-element.62), channel_id=1, source_target_pairs={{0,24},{4,28},{8,16},{12,20},{16,8},{20,12},{24,0},{28,4},{1,25},{... | collective-permute-start | bytes 393224 | tf_op jit(solution)/shard_map/ppermute | solution.py:352
  178.8 19.6 %collective-permute-start.9 = (bf16[16,32,128]{2,1,0:T(8,128)(2,1)S(1)}, bf16[16,32,128]{2,1,0:T(8,128)(2,1)S(1)}, u32[]{:S(2)}, u32[]{:S(2)}) collective-permute-start(bf16[16,32,128]{2,1,0:T(8,128)(2,1)S(1)} %get-tuple-element.63), channel_id=1, source_target_pairs={{0,28},{4,24},{8,20},{12,16},{16,12},{20,8},{24,4},{28,0},{1,29},{... | collective-permute-start | bytes 393224 | tf_op jit(solution)/shard_map/ppermute | solution.py:352
  183.3 19.1 %all-to-all-start.3 = ((bf16[16,64,128]{2,1,0:T(8,128)(2,1)}), bf16[16,64,128]{2,1,0:T(8,128)(2,1)S(1)}, u32[]{:S(2)}, u32[]{:S(2)}) async-start(bf16[16,64,128]{2,1,0:T(8,128)(2,1)} %bitcast.9), calls=%async_computation.3 | async-start | bytes 524288 | tf_op jit(solution)/shard_map/all_to_all | solution.py:384
  198.6 49.5 %copy-start.10 = (f32[1024,128]{1,0:T(8,128)S(1)}, f32[1024,128]{1,0:T(8,128)}, u32[]{:S(2)}) copy-start(f32[1024,128]{1,0:T(8,128)} %param.13) | copy-start | bytes 1572868
  202.5 13.9 %collective-permute-start.10 = (f32[64,128]{1,0:T(8,128)S(1)}, f32[64,128]{1,0:T(8,128)S(1)}, u32[]{:S(2)}, u32[]{:S(2)}) collective-permute-start(f32[64,128]{1,0:T(8,128)S(1)} %convert_reduce_fusion), channel_id=1, source_target_pairs={{0,2},{2,0},{1,3},{3,1},{4,6},{6,4},{5,7},{7,5},{8,10},{10,8},{9,1... | collective-permute-start | bytes 98312 | tf_op jit(solution)/shard_map/ppermute | solution.py:352
  206.7 17.4 %collective-permute-start.11 = (bf16[4,32,128]{2,1,0:T(8,128)(2,1)S(1)}, bf16[4,32,128]{2,1,0:T(8,128)(2,1)S(1)}, u32[]{:S(2)}, u32[]{:S(2)}) collective-permute-start(bf16[4,32,128]{2,1,0:T(8,128)(2,1)S(1)} %get-tuple-element.66), channel_id=1, source_target_pairs={{0,32},{32,0},{64,96},{96,64},{128,160},{160,128},{192,224},{224,1... | collective-permute-start | bytes 98312 | tf_op jit(solution)/shard_map/ppermute | solution.py:352
  211.3 12.8 %collective-permute-start.12 = (bf16[4,32,128]{2,1,0:T(8,128)(2,1)S(1)}, bf16[4,32,128]{2,1,0:T(8,128)(2,1)S(1)}, u32[]{:S(2)}, u32[]{:S(2)}) collective-permute-start(bf16[4,32,128]{2,1,0:T(8,128)(2,1)S(1)} %get-tuple-element.67), channel_id=1, source_target_pairs={{0,256},{32,288},{64,320},{96,352},{128,384},{160,416},{192,448},{... | collective-permute-start | bytes 98312 | tf_op jit(solution)/shard_map/ppermute | solution.py:352
  213.8 10.3 %collective-permute-start.13 = (bf16[4,32,128]{2,1,0:T(8,128)(2,1)S(1)}, bf16[4,32,128]{2,1,0:T(8,128)(2,1)S(1)}, u32[]{:S(2)}, u32[]{:S(2)}) collective-permute-start(bf16[4,32,128]{2,1,0:T(8,128)(2,1)S(1)} %get-tuple-element.68), channel_id=1, source_target_pairs={{0,288},{32,256},{64,352},{96,320},{128,416},{160,384},{192,480},{... | collective-permute-start | bytes 98312 | tf_op jit(solution)/shard_map/ppermute | solution.py:352
  217.1 18.7 %all-to-all-start.4 = ((bf16[16,64,128]{2,1,0:T(8,128)(2,1)}), bf16[16,64,128]{2,1,0:T(8,128)(2,1)S(1)}, u32[]{:S(2)}, u32[]{:S(2)}) async-start(bf16[16,64,128]{2,1,0:T(8,128)(2,1)} %broadcast_in_dim.2), calls=%async_computation.4 | async-start | bytes 524288 | tf_op jit(solution)/shard_map/all_to_all | solution.py:392
  235.8 13.4 %collective-permute-start.14 = (bf16[32,128]{1,0:T(8,128)(2,1)S(1)}, bf16[32,128]{1,0:T(8,128)(2,1)S(1)}, u32[]{:S(2)}, u32[]{:S(2)}) collective-permute-start(bf16[32,128]{1,0:T(8,128)(2,1)S(1)} %get-tuple-element.72), channel_id=1, source_target_pairs={{0,64},{32,96},{64,0},{96,32},{128,192},{160,224},{192,128},{224,1... | collective-permute-start | bytes 24584 | tf_op jit(solution)/shard_map/ppermute | solution.py:352
  240.9 8.3 %collective-permute-start.15 = (bf16[32,128]{1,0:T(8,128)(2,1)S(1)}, bf16[32,128]{1,0:T(8,128)(2,1)S(1)}, u32[]{:S(2)}, u32[]{:S(2)}) collective-permute-start(bf16[32,128]{1,0:T(8,128)(2,1)S(1)} %get-tuple-element.73), channel_id=1, source_target_pairs={{0,128},{32,160},{64,192},{96,224},{128,0},{160,32},{192,64},{224,... | collective-permute-start | bytes 24584 | tf_op jit(solution)/shard_map/ppermute | solution.py:352
  246.2 6.5 %collective-permute-start.16 = (bf16[32,128]{1,0:T(8,128)(2,1)S(1)}, bf16[32,128]{1,0:T(8,128)(2,1)S(1)}, u32[]{:S(2)}, u32[]{:S(2)}) collective-permute-start(bf16[32,128]{1,0:T(8,128)(2,1)S(1)} %get-tuple-element.74), channel_id=1, source_target_pairs={{0,192},{32,224},{64,128},{96,160},{128,64},{160,96},{192,0},{224,... | collective-permute-start | bytes 24584 | tf_op jit(solution)/shard_map/ppermute | solution.py:352
  (12 other events, 168.6 us)
Sparse Core Ops, SparseCore 0:
  37.1 59.5 all-gather.2

commit v4 on v3

--- a/solution.py
+++ b/solution.py
@@ -24,8 +24,6 @@
 RANK = 128
 GROUP = 14
 CHUNK = 32
-EARLY = 4
-SPAN = POOL + E
 BLOCKS = DX // E
 BAGS = N * F
 LEARN = 0.5
@@ -45,13 +43,13 @@
     return lax.dot_general(a, b, (((ca,), (cb,)), ((), ())), preferred_element_type=F32)
 
 
-def call(kernel, outs, ins, name, scratch=(), limit=40, flops=0, far=(), far_out=()):
+def call(kernel, outs, ins, name, scratch=(), limit=40, flops=0, far=()):
     nbytes = sum(x.size * x.dtype.itemsize for x in ins)
     return pl.pallas_call(
         kernel,
         out_shape=outs,
         in_specs=[SMEM if x.size < 8 else ANY if i in far else VMEM for i, x in enumerate(ins)],
-        out_specs=[ANY if i in far_out else VMEM for i in range(len(outs))],
+        out_specs=[VMEM] * len(outs),
         scratch_shapes=scratch,
         compiler_params=pltpu.CompilerParams(vmem_limit_bytes=limit << 20),
         cost_estimate=pl.CostEstimate(flops=flops, bytes_accessed=nbytes, transcendentals=0),
@@ -60,13 +58,11 @@
 
 
 def index_kernel(
-    shard_hbm, row_hbm, len_hbm, down_ref, up_ref, ids_ref, src_ref, src_t_ref, pack_ref,
-    shard_ref, row_ref, len_ref, sems,
+    shard_hbm, row_hbm, len_hbm, down_hbm, up_hbm, ids_ref, src_ref, src_t_ref, pack_ref,
+    shard_ref, row_ref, len_ref, up_ref, sems,
 ):
     moves = [(shard_hbm, shard_ref), (row_hbm, row_ref), (len_hbm, len_ref)]
-    moves.append((down_ref, pack_ref.at[pl.ds(0, DX), :]))
-    for j in range(BLOCKS):
-        moves.append((up_ref.at[:, pl.ds(j * E, E)], pack_ref.at[pl.ds(DX + j * E, E), :]))
+    moves += [(down_hbm, pack_ref.at[pl.ds(0, DX), :]), (up_hbm, up_ref)]
     moves = [pltpu.make_async_copy(a, b, sems.at[i]) for i, (a, b) in enumerate(moves)]
     for move in moves:
         move.start()
@@ -120,6 +116,8 @@
     src_t_ref[...] = src_t.astype(I32) - 1
     for move in moves[3:]:
         move.wait()
+    for j in range(BLOCKS):
+        pack_ref[DX + j * E : DX + (j + 1) * E, :] = up_ref[:, j * E : (j + 1) * E]
 
 
 def fetch_kernel(ids_ref, table_ref, out_ref):
@@ -131,11 +129,7 @@
         out_ref[s] = dot(pick, table).astype(BF)
 
 
-def main_kernel(
-    where_ref, rows_ref, src_ref, dense_ref, pack_ref, bias_ref, head_ref, label_ref,
-    feedback_ref, src_t_ref, carried_ref, send_ref, span_ref,
-    acc_ref, x_ref, down_ref, up_ref, small_ref, sems,
-):
+def start_weights(pack_ref, down_ref, up_ref, sems):
     moves = []
     for k in range(TP):
         block = pl.ds(k * RANK, RANK)
@@ -146,9 +140,21 @@
     moves = [pltpu.make_async_copy(a, b, sems.at[i]) for i, (a, b) in enumerate(moves)]
     for move in moves:
         move.start()
-
-    first = pl.multiple_of(where_ref[0] * N, N)
-    x_ref[:, 0:E] = dense_ref[pl.ds(first, N), :]
+    return moves
+
+
+def forward(x, down, up, bias, head, labels):
+    hidden = dot(x, down).astype(BF)
+    crossed = dot(hidden, up)
+    xf = x.astype(F32)
+    x_next = xf * (crossed + bias) + xf
+    logits = jnp.sum(x_next * head, axis=1, keepdims=True)
+    grad_logit = jax.nn.sigmoid(logits) - labels.astype(F32)
+    grad_next = grad_logit * head
+    return hidden, crossed, xf, x_next, grad_logit, grad_next, grad_next * xf
+
+
+def pool_kernel(rows_ref, src_ref, pooled_ref, acc_ref):
     bags = iota((BAGS, CAP), 0)
     for s in range(SHARDS):
         pick = jnp.where(bags == src_ref[s : s + 1, :], 1.0, 0.0).astype(BF)
@@ -158,22 +164,23 @@
         else:
             acc_ref[...] += term
     for f in range(F):
-        pooled = acc_ref[f * N : (f + 1) * N, :].astype(BF)
-        x_ref[:, (f + 1) * E : (f + 2) * E] = pooled
-        span_ref[:, f * E : (f + 1) * E] = pooled
+        pooled_ref[:, f * E : (f + 1) * E] = acc_ref[f * N : (f + 1) * N, :].astype(BF)
+
+
+def main_kernel(
+    where_ref, pooled_ref, dense_ref, pack_ref, bias_ref, head_ref, label_ref, feedback_ref,
+    src_t_ref, carried_ref, send_ref, down_ref, up_ref, sems,
+):
+    moves = start_weights(pack_ref, down_ref, up_ref, sems)
+    first = pl.multiple_of(where_ref[0] * N, N)
+    x = jnp.concatenate([dense_ref[pl.ds(first, N), :], pooled_ref[...]], axis=1)
     for move in moves:
         move.wait()
-    x = x_ref[...]
-    hidden = dot(x, down_ref[...]).astype(BF)
-    up = up_ref[...]
-    crossed = dot(hidden, up)
-    xf = x.astype(F32)
-    bias, head = bias_ref[...], head_ref[...]
-    x_next = xf * (crossed + bias) + xf
-    logits = jnp.sum(x_next * head, axis=1, keepdims=True)
-    grad_logit = jax.nn.sigmoid(logits) - label_ref[pl.ds(first, N), :].astype(F32)
-    grad_next = grad_logit * head
-    grad_cross = (grad_next * xf).astype(BF)
+    up, bias, head = up_ref[...], bias_ref[...], head_ref[...]
+    _, crossed, _, _, _, grad_next, cross = forward(
+        x, down_ref[...], up, bias, head, label_ref[pl.ds(first, N), :]
+    )
+    grad_cross = cross.astype(BF)
     grad_hidden = dot(grad_cross, up, 1, 1).astype(BF)
     back = dot(grad_hidden, down_ref[E:, :], 1, 1)
     carried = grad_next[:, E:] * (crossed[:, E:] + bias[:, E:] + 1.0) + back + feedback_ref[...]
@@ -184,47 +191,34 @@
     for s in range(SHARDS):
         pick = jnp.where(src_t_ref[:, s : s + 1] == bags, 1.0, 0.0).astype(BF)
         send_ref[s] = dot(pick, by_bag).astype(BF)
+
+
+def grads_kernel(
+    where_ref, s0_ref, s1_ref, s2_ref, s3_ref, dense_ref, pack_ref, bias_ref, head_ref, label_ref,
+    out_ref, x_ref, down_ref, up_ref, hidden_ref, down_grad_ref, up_grad_ref, sems,
+):
+    moves = start_weights(pack_ref, down_ref, up_ref, sems)
+    t = where_ref[0]
+    x_ref[:, 0:E] = dense_ref[...]
+    for m, ref in enumerate((s0_ref, s1_ref, s2_ref, s3_ref)):
+        x_ref[pl.ds(pl.multiple_of((t ^ m) * N, N), N), E:] = ref[...]
+    x = x_ref[...]
+    for move in moves:
+        move.wait()
+    hidden, _, _, x_next, grad_logit, _, cross = forward(
+        x, down_ref[...], up_ref[...], bias_ref[...], head_ref[...], label_ref[...]
+    )
+    for k in range(TP):
+        hidden_ref[k] = hidden[:, k * RANK : (k + 1) * RANK]
+    hidden = hidden_ref[t]
+    up = up_ref[pl.ds(pl.multiple_of(t * RANK, RANK), RANK), :]
+    grad_cross = cross.astype(BF)
+    grad_bias = jnp.sum(cross, axis=0, keepdims=True)
     grad_head = jnp.sum(grad_logit * x_next, axis=0, keepdims=True)
-    small_ref[...] = jnp.zeros((N, E), F32)
-    for j in range(BLOCKS):
-        part = grad_head[:, j * E : (j + 1) * E]
-        high = part.astype(BF).astype(F32)
-        small_ref[j : j + 1, :] = high
-        small_ref[BLOCKS + j : BLOCKS + j + 1, :] = part - high
-    diagonal = iota((N, N), 0) == iota((N, N), 1)
-    part = jnp.sum(jnp.where(diagonal, grad_logit, 0.0), axis=0, keepdims=True)
-    high = part.astype(BF).astype(F32)
-    small_ref[2 * BLOCKS : 2 * BLOCKS + 1, 0:N] = high
-    small_ref[2 * BLOCKS + 1 : 2 * BLOCKS + 2, 0:N] = part - high
-    span_ref[:, POOL:] = small_ref[...].astype(BF)
-
-
-def grads_kernel(where_ref, s0_ref, s1_ref, s2_ref, s3_ref, dense_ref, down_ref, up_ref, head_ref, *rest):
-    outs, (x_ref, logit_ref, down_grad_ref, up_grad_ref, stage_ref) = rest[:DP], rest[DP:]
-    t, y, u = where_ref[0], where_ref[1], where_ref[2]
-    x_ref[:, 0:E] = dense_ref[...]
-    diagonal = iota((N, N), 0) == iota((N, N), 1)
-    heads = []
-    for m, ref in enumerate((s0_ref, s1_ref, s2_ref, s3_ref)):
-        rows = pl.ds(pl.multiple_of((t ^ m) * N, N), N)
-        x_ref[rows, E:] = ref[:, :POOL]
-        tail = ref[:, POOL:].astype(F32)
-        heads.append(tail[0:BLOCKS] + tail[BLOCKS : 2 * BLOCKS])
-        row = tail[2 * BLOCKS : 2 * BLOCKS + 1, 0:N] + tail[2 * BLOCKS + 1 : 2 * BLOCKS + 2, 0:N]
-        logit_ref[rows, :] = jnp.sum(jnp.where(diagonal, row, 0.0), axis=1, keepdims=True)
-    heads = (heads[0] + heads[1]) + (heads[2] + heads[3])
-    x = x_ref[...]
-    grad_logit = logit_ref[...]
-    xf = x.astype(F32)
-    hidden = dot(x, down_ref[...]).astype(BF)
-    cross = grad_logit * head_ref[...] * xf
-    grad_bias = jnp.sum(cross, axis=0, keepdims=True)
-    grad_cross = cross.astype(BF)
-    grad_hidden = dot(grad_cross, up_ref[...], 1, 1).astype(BF)
+    grad_hidden = dot(grad_cross, up, 1, 1).astype(BF)
     down_grad_ref[...] = dot(x, grad_hidden, 0, 0).astype(BF)
     up_grad_ref[...] = dot(grad_cross, hidden, 0, 0).astype(BF)
 
-    grad_head = jnp.concatenate([heads[j : j + 1, :] for j in range(DX // E)], axis=1)
     groups = DX // GROUP
     r = iota((groups, DX), 1) - GROUP * iota((groups, DX), 0)
     own = (r >= 0) & (r < GROUP)
@@ -260,12 +254,8 @@
             axis=0,
         )
         got = dot(select, block_rows).astype(BF)
-        w = u ^ e
-        place = ((w >> 3) & 1) * 8 + (w & 1) * 4 + ((w >> 1) & 3)
         for k in range(DP):
-            stage_ref[y ^ k, place] = got[CHUNK * k : CHUNK * (k + 1)]
-    for m in range(DP):
-        outs[m][...] = stage_ref[m]
+            out_ref[k, e] = got[CHUNK * k : CHUNK * (k + 1)]
 
 
 def scatter_kernel(ids_ref, rows_ref, out_ref, acc_ref):
@@ -280,11 +270,9 @@
     out_ref[...] = acc_ref[...].astype(BF)
 
 
-def total(parts):
-    parts = [p.astype(F32) for p in parts]
-    while len(parts) > 1:
-        parts = [a + b for a, b in zip(parts[::2], parts[1::2])]
-    return parts[0]
+def partner(value, axes, mask):
+    size = lax.axis_size(axes)
+    return lax.ppermute(value, axes, [(i, i ^ mask) for i in range(size)])
 
 
 def sds(shape, dtype):
@@ -296,6 +284,7 @@
     cross_down, cross_up, cross_bias, head_weight,
 ):
     bias, head = cross_bias.reshape(1, DX), head_weight.reshape(1, DX)
+    label = labels.reshape(DENSE, 1)
     where = jnp.stack([lax.axis_index(TPA), lax.axis_index("y"), lax.axis_index(EMB)]).astype(I32)
     ids, src, src_t, pack = call(
         index_kernel,
@@ -311,12 +300,12 @@
             pltpu.VMEM((LOOK, 1, N), I32),
             pltpu.VMEM((LOOK, N), I32),
             pltpu.VMEM((F, N), I32),
-            pltpu.SemaphoreType.DMA((4 + BLOCKS,)),
+            pltpu.VMEM((RANK, DX), BF),
+            pltpu.SemaphoreType.DMA((5,)),
         ],
         flops=400_000_000,
         limit=56,
         far=range(5),
-        far_out=(3,),
     )
     with jax.named_scope("gather_weights"):
         pack_all = lax.all_gather(pack, TPA, axis=0, tiled=False)
@@ -325,49 +314,55 @@
         fetch_kernel, [sds((SHARDS, CAP, E), BF)], (ids, emb_table), "fetch", flops=1_300_000_000
     )
     returned = lax.all_to_all(fetched, EMB, split_axis=0, concat_axis=0, tiled=True)
-    carried, send, span = call(
+    (pooled,) = call(
+        pool_kernel,
+        [sds((N, POOL), BF)],
+        (returned, src),
+        "pool",
+        scratch=[pltpu.VMEM((BAGS, E), F32)],
+        flops=1_060_000_000,
+    )
+    far = partner(pooled, "xh", 1)
+    carried, send = call(
         main_kernel,
-        (sds((N, POOL), F32), sds((SHARDS, CAP, E), BF), sds((N, SPAN), BF)),
-        (
-            where, returned, src, dense_input, pack_all, bias, head, labels.reshape(DENSE, 1),
-            feedback, src_t,
-        ),
+        (sds((N, POOL), F32), sds((SHARDS, CAP, E), BF)),
+        (where, pooled, dense_input, pack_all, bias, head, label, feedback, src_t),
         "main",
         scratch=[
-            pltpu.VMEM((BAGS, E), F32),
-            pltpu.VMEM((N, DX), BF),
             pltpu.VMEM((DX, TP * RANK), BF),
             pltpu.VMEM((TP * RANK, DX), BF),
-            pltpu.VMEM((N, E), F32),
             pltpu.SemaphoreType.DMA((TP * (1 + BLOCKS),)),
         ],
-        flops=2_600_000_000,
+        flops=10_000_000_000,
         limit=56,
-        far=(4,),
-    )
+        far=(3,),
+    )
+    far, again, send = lax.optimization_barrier((far, pooled, send))
     arrived = lax.all_to_all(send, EMB, split_axis=0, concat_axis=0, tiled=True)
 
-    def partner(value, axes, mask):
-        size = lax.axis_size(axes)
-        return lax.ppermute(value, axes, [(i, i ^ mask) for i in range(size)])
-
-    spans = [span] + [partner(span, TPA, m) for m in range(1, TP)]
-    part = call(
+    near, far_near = partner(again, "core", 1), partner(far, "core", 1)
+    (part,) = call(
         grads_kernel,
-        [sds((SHARDS, CHUNK, E), BF)] * DP,
-        (where, *spans, dense_input, cross_down, cross_up, head),
+        [sds((DP, SHARDS, CHUNK, E), BF)],
+        (where, pooled, near, far, far_near, dense_input, pack_all, bias, head, label),
         "grads",
         scratch=[
             pltpu.VMEM((DENSE, DX), BF),
-            pltpu.VMEM((DENSE, 1), F32),
+            pltpu.VMEM((DX, TP * RANK), BF),
+            pltpu.VMEM((TP * RANK, DX), BF),
+            pltpu.VMEM((TP, DENSE, RANK), BF),
             pltpu.VMEM((DX, RANK), BF),
             pltpu.VMEM((DX, RANK), BF),
-            pltpu.VMEM((DP, SHARDS, CHUNK, E), BF),
+            pltpu.SemaphoreType.DMA((TP * (1 + BLOCKS),)),
         ],
-        flops=1_000_000_000,
-    )
-    early = [partner(part[m], "y", m) for m in range(1, EARLY)]
-    arrived, *early = lax.optimization_barrier((arrived, *early))
+        flops=2_000_000_000,
+        limit=56,
+        far=(6,),
+    )
+    arrived, part = lax.optimization_barrier((arrived, part))
+    over_y = lax.psum_scatter(
+        part.reshape(DP * SHARDS * CHUNK, E), "y", scatter_dimension=0, tiled=True
+    )
     (row_grad,) = call(
         scatter_kernel,
         [sds((ROWS, E), BF)],
@@ -376,28 +371,20 @@
         scratch=[pltpu.VMEM((ROWS, E), F32)],
         flops=1_300_000_000,
     )
-    row_grad, *late = lax.optimization_barrier((row_grad, *part[EARLY:]))
-    late = [partner(v, "y", m) for m, v in enumerate(late, EARLY)]
-    part = [part[0], *early, *late]
     owners = ("y", "core")
     pieces = 2 * DP
     by_y = lax.all_to_all(row_grad, owners, split_axis=0, concat_axis=0, tiled=True)
-    over_y = total(part)
-    part = [over_y[0:4]] + [over_y[4 * c : 4 * c + 4].astype(BF) for c in (1, 2, 3)]
-    by_y, *part = lax.optimization_barrier((by_y, *part))
-    part = part[:1] + [partner(part[c], EMB, mask) for c, mask in ((1, 1), (2, 8), (3, 9))]
     mine = jnp.sum(by_y.reshape(pieces, ROWS // pieces, E).astype(F32), axis=0)
     mine = (mine + partner(mine, "xh", 1)).astype(BF)
+    over_y = over_y.reshape(SHARDS, CHUNK, E)
+    over_all = lax.all_to_all(over_y, EMB, split_axis=0, concat_axis=0, tiled=True)
     spread = jnp.broadcast_to(mine[None], (pieces, ROWS // pieces, E)).reshape(ROWS, E)
+    spread, over_all = lax.optimization_barrier((spread, over_all))
     full = lax.all_to_all(spread, owners, split_axis=0, concat_axis=0, tiled=True)
-    over_pair = total(part)
-    part = [over_pair[0]] + [over_pair[i].astype(BF) for i in (1, 2, 3)]
-    full, *part = lax.optimization_barrier((full, *part))
-    part = part[:1] + [partner(part[i], EMB, 2 * i) for i in (1, 2, 3)]
     full = full.astype(F32)
     accum_new = row_accum + full * full
     table_new = emb_table - LEARN * full / jnp.sqrt(accum_new)
-    grads = total(part)
+    grads = jnp.sum(over_all.astype(F32), axis=0)
     grad_down = grads[0:GROUP]
     grad_up = grads[GROUP : 2 * GROUP].T
     grad_head = grads[2 * GROUP, 0:GROUP]

time: 262 us -> 211 us (0.81)
  starting transfers between devices: 92.3 us -> 41.8 us
  blocking collectives: 19 us -> 42.6 us
  Pallas kernels: 52.5 us -> 35.9 us
  waiting for transfers between devices: 74.3 us -> 68.5 us
    ppermute x17 -> x4, starting transfers between devices: 63.9 us -> 13.3 us  [partner(): return lax.ppermute(value, axes, [(i, i ^ mask) for i in range(size)])]
    ppermute x17 -> x4, waiting for transfers between devices: 29.7 us -> 1.42 us  [partner(): return lax.ppermute(value, axes, [(i, i ^ mask) for i in range(size)])]
    all_to_all x0 -> x1, blocking collectives: none -> 23.6 us  [local(): lax.all_to_all(row_grad, owners, split_axis=0, concat_axis=0, tiled=True)]
    pallas_call x5 -> x6, Pallas kernels: 52.5 us -> 35.9 us  [call(): pl.pallas_call(kernel, out_shape=outs, in_specs=[SMEM if x.size < 8 else...]
    all_to_all x1, waiting for transfers between devices: 0.01 us -> 14.2 us  [local(): arrived = lax.all_to_all(send, EMB, split_axis=0, concat_axis=0, tiled=True)]
    reduce_scatter x0 -> x1, waiting for transfers between devices: none -> 7.89 us  [local(): lax.psum_scatter(part.reshape(DP * SHARDS * CHUNK, E), 'y', scatter_dimen...]
    all_to_all x1, starting transfers between devices: 6.96 us -> 10.7 us  [local(): lax.all_to_all(spread, owners, split_axis=0, concat_axis=0, tiled=True)]
    all_to_all x1, waiting for transfers between devices: 3.82 us -> 7.49 us  [local(): lax.all_to_all(over_y, EMB, split_axis=0, concat_axis=0, tiled=True)]
  transfers between devices with their start and end apart: 22 -> 10, of which waited for: 11 -> 6; matrix products, arithmetic and copies ran while one was open for 2% -> 2% of each run, Pallas kernels for 3% -> 14%
where the time goes in v4:
time: 211 us; the launch traced here: 210 us
  waiting for transfers between devices  68.5 us (32%)
  blocking collectives  42.6 us (20%)
  starting transfers between devices  41.8 us (20%)
  Pallas kernels  35.9 us (17%)
  between operations  14.3 us (7%)
  local copies, waits for them, and re-layouts  5.45 us (3%)
    pallas_call x6, Pallas kernels, call(): pl.pallas_call(kernel, out_shape=outs, in_specs=[SMEM if x.size < 8 else...  35.9 us
    all_to_all x1, waiting for transfers between devices, local(): lax.all_to_all(fetched, EMB, split_axis=0, concat_axis=0, tiled=True)  27 us
    all_to_all x1, blocking collectives, local(): lax.all_to_all(row_grad, owners, split_axis=0, concat_axis=0, tiled=True)  23.6 us
    all_to_all x1, blocking collectives, local(): ids = lax.all_to_all(ids, EMB, split_axis=0, concat_axis=0, tiled=True)  19 us
    all_to_all x1, waiting for transfers between devices, local(): arrived = lax.all_to_all(send, EMB, split_axis=0, concat_axis=0, tiled=True)  14.2 us
    ppermute x4, starting transfers between devices, partner(): return lax.ppermute(value, axes, [(i, i ^ mask) for i in range(size)])  13.3 us
    all_to_all x1, starting transfers between devices, local(): lax.all_to_all(spread, owners, split_axis=0, concat_axis=0, tiled=True)  10.7 us
    all_to_all x1, waiting for transfers between devices, local(): lax.all_to_all(spread, owners, split_axis=0, concat_axis=0, tiled=True)  10.5 us
  transfers between devices with their start and end apart: 10, of which 6 were waited for; matrix products, arithmetic and copies ran while one was open for 2% of the time, Pallas kernels for 14%

profile of v4, /device:TPU:1, one launch (start us, length us, event | category | flops | bytes accessed | tf_op | source)
XLA Modules:
  0.0 210.5 jit_solution(14516195028580992207)
XLA Ops:
  7.2 7.1 %index.1 = (s32[16,312]{1,0:T(8,128)}, s32[16,312]{1,0:T(8,128)}, s32[312,16]{1,0:T(8,128)}, bf16[3584,128]{1,0:T(8,128)(2,1)}) custom-call(s32[52,1,64]{2,1,0:T(1,128)} %bitcast.40, s32[52,64]{1,0:T(8,128)} %bitcast.39, s32[13,64]{1,0:T(8,128)} %bitcast.41, bf16[1792,128]{1,0:T(8,128)(2,1)} %down_hbm.1, bf16[128,1792]{1,0:T(8,128)(2,1)} %up_hbm.1), custom_call_target="tpu_custom_call" | custom-call | flops 400000000 | bytes 947456 | tf_op jit(solution)/shard_map/index/pallas_call | solution.py:48
  15.2 19.0 %all_to_all.44 = s32[16,1,312]{2,1,0:T(1,128)S(1)} all-to-all(s32[16,1,312]{2,1,0:T(1,128)S(1)} %copy.21), channel_id=1, replica_groups=mesh['xl'=2,'z'=8,'y'=8,'xh'=2,'core'=2] {'xl','z'}, dimensions={0} | all-to-all | bytes 39936 | tf_op jit(solution)/shard_map/all_to_all | solution.py:312
  34.2 4.1 %fetch.1 = bf16[16,312,128]{2,1,0:T(8,128)(2,1)} custom-call(s32[16,312]{1,0:T(8,128)S(1)} %bitcast.31, f32[1024,128]{1,0:T(8,128)S(1)} %copy-done), custom_call_target="tpu_custom_call" | custom-call | flops 1300000000 | bytes 544256 | tf_op jit(solution)/shard_map/fetch/pallas_call | solution.py:48
  38.3 3.8 %all-to-all-start.1 = ((bf16[16,312,128]{2,1,0:T(8,128)(2,1)}), bf16[16,312,128]{2,1,0:T(8,128)(2,1)S(1)}, u32[]{:S(2)}, u32[]{:S(2)}) async-start(bf16[16,312,128]{2,1,0:T(8,128)(2,1)} %fetch.1), calls=%async_computation.1 | async-start | bytes 2555904 | tf_op jit(solution)/shard_map/all_to_all | solution.py:316
  43.4 0.8 copy.22.label_ref
  44.9 27.0 %all-to-all-done.1.rows_ref = bf16[16,312,128]{2,1,0:T(8,128)(2,1)S(1)} async-done(((bf16[16,312,128]{2,1,0:T(8,128)(2,1)}), bf16[16,312,128]{2,1,0:T(8,128)(2,1)S(1)}, u32[]{:S(2)}, u32[]{:S(2)}) %all-to-all-start.1) | async-done | bytes 1277984 | tf_op jit(solution)/shard_map/all_to_all | solution.py:316
  71.8 2.8 %pool.1.pooled_ref.s0_ref = bf16[64,1664]{1,0:T(8,128)(2,1)S(1)} custom-call(bf16[16,312,128]{2,1,0:T(8,128)(2,1)S(1)} %all-to-all-done.1.rows_ref, s32[16,312]{1,0:T(8,128)S(1)} %copy-done.3), custom_call_target="tpu_custom_call" | custom-call | flops 1060000000 | bytes 1297920 | tf_op jit(solution)/shard_map/pool/pallas_call | solution.py:48
  74.7 4.5 %collective-permute-start = (bf16[64,1664]{1,0:T(8,128)(2,1)S(1)}, bf16[64,1664]{1,0:T(8,128)(2,1)S(1)}, u32[]{:S(2)}, u32[]{:S(2)}) collective-permute-start(bf16[64,1664]{1,0:T(8,128)(2,1)S(1)} %pool.1.pooled_ref.s0_ref), channel_id=1, source_target_pairs={{0,2},{2,0},{1,3},{3,1},{4,6},{6,4},{5,7},{7,5},{8,10},{10,8},{9,1... | collective-permute-start | bytes 638984 | tf_op jit(solution)/shard_map/ppermute | solution.py:275
  79.3 9.6 %main.1 = (f32[64,1664]{1,0:T(8,128)}, bf16[16,312,128]{2,1,0:T(8,128)(2,1)}) custom-call(s32[3]{0:T(128)} %pad_add_fusion.where_ref, bf16[64,1664]{1,0:T(8,128)(2,1)} %copy-done.1, bf16[256,128]{1,0:T(8,128)(2,1)} %dense_ref.3, bf16[4,3584,128]{2,1,0:T(8,128)(2,1)} %bitcast.37, f32[1,1792]{1,0:T(1,128)} %reshape.45.bias_ref, f32[1,1792]{1,0:T(1,128)} %reshape.46.head_ref, ...), custom_call_target="tpu_custom_call" | custom-call | flops 10000000000 | bytes 4409868 | tf_op jit(solution)/shard_map/main/pallas_call | solution.py:48
  88.9 6.3 %all-to-all-start.2 = ((bf16[16,312,128]{2,1,0:T(8,128)(2,1)}), bf16[16,312,128]{2,1,0:T(8,128)(2,1)S(1)}, u32[]{:S(2)}, u32[]{:S(2)}) async-start(bf16[16,312,128]{2,1,0:T(8,128)(2,1)} %get-tuple-element.25), calls=%async_computation.2 | async-start | bytes 2555904 | tf_op jit(solution)/shard_map/all_to_all | solution.py:341
  95.3 3.1 %collective-permute-start.1 = (bf16[64,1664]{1,0:T(8,128)(2,1)S(1)}, bf16[64,1664]{1,0:T(8,128)(2,1)S(1)}, u32[]{:S(2)}, u32[]{:S(2)}) collective-permute-start(bf16[64,1664]{1,0:T(8,128)(2,1)S(1)} %copy-done.2), channel_id=1, source_target_pairs={{0,1},{1,0},{2,3},{3,2},{4,5},{5,4},{6,7},{7,6},{8,9},{9,8},{10,11... | collective-permute-start | bytes 638984 | tf_op jit(solution)/shard_map/ppermute | solution.py:275
  98.4 1.9 collective-permute-start.2
  100.3 1.4 collective-permute-done.2.s3_ref
  102.4 8.8 %grads.1 = bf16[8,16,32,128]{3,2,1,0:T(8,128)(2,1)} custom-call(s32[3]{0:T(128)} %pad_add_fusion.where_ref, bf16[64,1664]{1,0:T(8,128)(2,1)} %copy-done.1, bf16[64,1664]{1,0:T(8,128)(2,1)} %copy-done.9, bf16[64,1664]{1,0:T(8,128)(2,1)} %copy-done.8, bf16[64,1664]{1,0:T(8,128)(2,1)} %copy-done.10, bf16[256,128]{1,0:T(8,128)(2,1)} %dense_ref.3, ...), custom_call_target="tpu_custom_call" | custom-call | flops 2000000000 | bytes 4602892 | tf_op jit(solution)/shard_map/grads/pallas_call | solution.py:48
  111.2 14.2 %all-to-all-done.2.rows_ref = bf16[16,312,128]{2,1,0:T(8,128)(2,1)S(1)} async-done(((bf16[16,312,128]{2,1,0:T(8,128)(2,1)}), bf16[16,312,128]{2,1,0:T(8,128)(2,1)S(1)}, u32[]{:S(2)}, u32[]{:S(2)}) %all-to-all-start.2) | async-done | bytes 1277984 | tf_op jit(solution)/shard_map/all_to_all | solution.py:341
  125.4 3.5 %scatter.1 = bf16[1024,128]{1,0:T(8,128)(2,1)S(1)} custom-call(s32[16,312]{1,0:T(8,128)S(1)} %bitcast.32, bf16[16,312,128]{2,1,0:T(8,128)(2,1)S(1)} %all-to-all-done.2.rows_ref), custom_call_target="tpu_custom_call" | custom-call | flops 1300000000 | bytes 1297920 | tf_op jit(solution)/shard_map/scatter/pallas_call | solution.py:48
  128.9 23.6 %all_to_all.45 = bf16[16,64,128]{2,1,0:T(8,128)(2,1)S(1)} all-to-all(bf16[16,64,128]{2,1,0:T(8,128)(2,1)S(1)} %bitcast.30), channel_id=1, replica_groups=mesh['xl'=2,'z'=8,'y'=8,'xh'=2,'core'=2] {'y','core'}, dimensions={0} | all-to-all | bytes 524288 | tf_op jit(solution)/shard_map/all_to_all | solution.py:376
  152.5 3.7 %collective-permute-start.3 = (f32[64,128]{1,0:T(8,128)S(1)}, f32[64,128]{1,0:T(8,128)S(1)}, u32[]{:S(2)}, u32[]{:S(2)}) collective-permute-start(f32[64,128]{1,0:T(8,128)S(1)} %convert_reduce_fusion), channel_id=1, source_target_pairs={{0,2},{2,0},{1,3},{3,1},{4,6},{6,4},{5,7},{7,5},{8,10},{10,8},{9,1... | collective-permute-start | bytes 98312 | tf_op jit(solution)/shard_map/ppermute | solution.py:275
  156.3 7.9 %reduce-scatter.2.cloned.1.call-done = bf16[512,128]{1,0:T(8,128)(2,1)} async-done(((bf16[4096,128]{1,0:T(8,128)(2,1)}), bf16[512,128]{1,0:T(8,128)(2,1)}) %reduce-scatter.2.cloned.1.call-update) | async-done | bytes 131088 | tf_op jit(solution)/shard_map/reduce_scatter | solution.py:363
  164.2 7.6 %all-to-all-start.4 = ((bf16[16,32,128]{2,1,0:T(8,128)(2,1)}), bf16[16,32,128]{2,1,0:T(8,128)(2,1)S(1)}, u32[]{:S(2)}, u32[]{:S(2)}) async-start(bf16[16,32,128]{2,1,0:T(8,128)(2,1)} %bitcast.34), calls=%async_computation.5 | async-start | bytes 262144 | tf_op jit(solution)/shard_map/all_to_all | solution.py:380
  171.8 7.5 %all-to-all-done.4 = bf16[16,32,128]{2,1,0:T(8,128)(2,1)S(1)} async-done(((bf16[16,32,128]{2,1,0:T(8,128)(2,1)}), bf16[16,32,128]{2,1,0:T(8,128)(2,1)S(1)}, u32[]{:S(2)}, u32[]{:S(2)}) %all-to-all-start.4) | async-done | bytes 131104 | tf_op jit(solution)/shard_map/all_to_all | solution.py:380
  180.1 10.7 %all-to-all-start.5 = ((bf16[16,64,128]{2,1,0:T(8,128)(2,1)}), bf16[16,64,128]{2,1,0:T(8,128)(2,1)S(1)}, u32[]{:S(2)}, u32[]{:S(2)}) async-start(bf16[16,64,128]{2,1,0:T(8,128)(2,1)} %bitcast.13), calls=%async_computation.6 | async-start | bytes 524288 | tf_op jit(solution)/shard_map/all_to_all | solution.py:383
  192.0 10.5 %all-to-all-done.5 = bf16[16,64,128]{2,1,0:T(8,128)(2,1)S(1)} async-done(((bf16[16,64,128]{2,1,0:T(8,128)(2,1)}), bf16[16,64,128]{2,1,0:T(8,128)(2,1)S(1)}, u32[]{:S(2)}, u32[]{:S(2)}) %all-to-all-start.5) | async-done | bytes 262176 | tf_op jit(solution)/shard_map/all_to_all | solution.py:383
  202.6 1.1 fusion
  (42 shorter events, 5.6 us)
Async XLA Ops:
  7.2 72.1 %all-gather.3.cloned.1.call-start = ((), (), s32[]{:S(2)}) async-start(), calls=%async_computation.8 | async-start | bytes 4587520 | tf_op jit(solution)/shard_map/gather_weights/all_gather | solution.py:311
  7.2 27.0 %copy-start = (f32[1024,128]{1,0:T(8,128)S(1)}, f32[1024,128]{1,0:T(8,128)}, u32[]{:S(2)}) copy-start(f32[1024,128]{1,0:T(8,128)} %table_ref.1) | copy-start | bytes 1572868
  38.3 3.9 %copy-start.5 = (f32[1792]{0:T(1024)S(1)}, f32[1792]{0:T(1024)}, u32[]{:S(2)}) copy-start(f32[1792]{0:T(1024)} %param.22) | copy-start | bytes 21508
  38.3 4.5 %copy-start.6 = (f32[1792]{0:T(1024)S(1)}, f32[1792]{0:T(1024)}, u32[]{:S(2)}) copy-start(f32[1792]{0:T(1024)} %param.23) | copy-start | bytes 21508
  38.3 5.1 %copy-start.7 = (s32[256]{0:T(256)S(1)}, s32[256]{0:T(256)}, u32[]{:S(2)}) copy-start(s32[256]{0:T(256)} %param.18) | copy-start | bytes 3076
  38.3 33.5 %copy-start.3 = (s32[16,312]{1,0:T(8,128)S(1)}, s32[16,312]{1,0:T(8,128)}, u32[]{:S(2)}) copy-start(s32[16,312]{1,0:T(8,128)} %get-tuple-element.21.src_ref) | copy-start | bytes 59908
  38.3 33.5 %all-to-all-start.1 = ((bf16[16,312,128]{2,1,0:T(8,128)(2,1)}), bf16[16,312,128]{2,1,0:T(8,128)(2,1)S(1)}, u32[]{:S(2)}, u32[]{:S(2)}) async-start(bf16[16,312,128]{2,1,0:T(8,128)(2,1)} %fetch.1), calls=%async_computation.1 | async-start | bytes 2555904 | tf_op jit(solution)/shard_map/all_to_all | solution.py:316
  74.7 4.6 %copy-start.1 = (bf16[64,1664]{1,0:T(8,128)(2,1)}, bf16[64,1664]{1,0:T(8,128)(2,1)S(1)}, u32[]{:S(2)}) copy-start(bf16[64,1664]{1,0:T(8,128)(2,1)S(1)} %pool.1.pooled_ref.s0_ref) | copy-start | bytes 638980
  74.7 14.2 %collective-permute-start = (bf16[64,1664]{1,0:T(8,128)(2,1)S(1)}, bf16[64,1664]{1,0:T(8,128)(2,1)S(1)}, u32[]{:S(2)}, u32[]{:S(2)}) collective-permute-start(bf16[64,1664]{1,0:T(8,128)(2,1)S(1)} %pool.1.pooled_ref.s0_ref), channel_id=1, source_target_pairs={{0,2},{2,0},{1,3},{3,1},{4,6},{6,4},{5,7},{7,5},{8,10},{10,8},{9,1... | collective-permute-start | bytes 638984 | tf_op jit(solution)/shard_map/ppermute | solution.py:275
  88.8 9.5 %copy-start.8 = (bf16[64,1664]{1,0:T(8,128)(2,1)}, bf16[64,1664]{1,0:T(8,128)(2,1)S(1)}, u32[]{:S(2)}) copy-start(bf16[64,1664]{1,0:T(8,128)(2,1)S(1)} %collective-permute-done.s2_ref) | copy-start | bytes 638980
  88.9 6.4 %copy-start.2 = (bf16[64,1664]{1,0:T(8,128)(2,1)S(1)}, bf16[64,1664]{1,0:T(8,128)(2,1)}, u32[]{:S(2)}) copy-start(bf16[64,1664]{1,0:T(8,128)(2,1)} %copy-done.1) | copy-start | bytes 638980
  88.9 36.5 %all-to-all-start.2 = ((bf16[16,312,128]{2,1,0:T(8,128)(2,1)}), bf16[16,312,128]{2,1,0:T(8,128)(2,1)S(1)}, u32[]{:S(2)}, u32[]{:S(2)}) async-start(bf16[16,312,128]{2,1,0:T(8,128)(2,1)} %get-tuple-element.25), calls=%async_computation.2 | async-start | bytes 2555904 | tf_op jit(solution)/shard_map/all_to_all | solution.py:341
  95.2 69.0 %reduce-scatter.2.cloned.1.call-start = ((), (), s32[]{:S(2)}) async-start(), calls=%async_computation.7 | async-start | bytes 1179648 | tf_op jit(solution)/shard_map/reduce_scatter | solution.py:363
  95.3 5.0 %collective-permute-start.1 = (bf16[64,1664]{1,0:T(8,128)(2,1)S(1)}, bf16[64,1664]{1,0:T(8,128)(2,1)S(1)}, u32[]{:S(2)}, u32[]{:S(2)}) collective-permute-start(bf16[64,1664]{1,0:T(8,128)(2,1)S(1)} %copy-done.2), channel_id=1, source_target_pairs={{0,1},{1,0},{2,3},{3,2},{4,5},{5,4},{6,7},{7,6},{8,9},{9,8},{10,11... | collective-permute-start | bytes 638984 | tf_op jit(solution)/shard_map/ppermute | solution.py:275
  98.4 3.4 %collective-permute-start.2 = (bf16[64,1664]{1,0:T(8,128)(2,1)S(1)}, bf16[64,1664]{1,0:T(8,128)(2,1)S(1)}, u32[]{:S(2)}, u32[]{:S(2)}) collective-permute-start(bf16[64,1664]{1,0:T(8,128)(2,1)S(1)} %collective-permute-done.s2_ref), channel_id=1, source_target_pairs={{0,1},{1,0},{2,3},{3,2},{4,5},{5,4},{6,7},{7,6},{8,9},{9,8},{10,11... | collective-permute-start | bytes 638984 | tf_op jit(solution)/shard_map/ppermute | solution.py:275
  100.3 1.4 copy-start.9
  101.7 0.7 copy-start.10
  152.5 19.3 %collective-permute-start.3 = (f32[64,128]{1,0:T(8,128)S(1)}, f32[64,128]{1,0:T(8,128)S(1)}, u32[]{:S(2)}, u32[]{:S(2)}) collective-permute-start(f32[64,128]{1,0:T(8,128)S(1)} %convert_reduce_fusion), channel_id=1, source_target_pairs={{0,2},{2,0},{1,3},{3,1},{4,6},{6,4},{5,7},{7,5},{8,10},{10,8},{9,1... | collective-permute-start | bytes 98312 | tf_op jit(solution)/shard_map/ppermute | solution.py:275
  164.2 38.4 %copy-start.4 = (f32[1024,128]{1,0:T(8,128)S(1)}, f32[1024,128]{1,0:T(8,128)}, u32[]{:S(2)}) copy-start(f32[1024,128]{1,0:T(8,128)} %param.13) | copy-start | bytes 1572868
  164.2 15.1 %all-to-all-start.4 = ((bf16[16,32,128]{2,1,0:T(8,128)(2,1)}), bf16[16,32,128]{2,1,0:T(8,128)(2,1)S(1)}, u32[]{:S(2)}, u32[]{:S(2)}) async-start(bf16[16,32,128]{2,1,0:T(8,128)(2,1)} %bitcast.34), calls=%async_computation.5 | async-start | bytes 262144 | tf_op jit(solution)/shard_map/all_to_all | solution.py:380
  180.1 22.4 %all-to-all-start.5 = ((bf16[16,64,128]{2,1,0:T(8,128)(2,1)}), bf16[16,64,128]{2,1,0:T(8,128)(2,1)S(1)}, u32[]{:S(2)}, u32[]{:S(2)}) async-start(bf16[16,64,128]{2,1,0:T(8,128)(2,1)} %bitcast.13), calls=%async_computation.6 | async-start | bytes 524288 | tf_op jit(solution)/shard_map/all_to_all | solution.py:383
Sparse Core Ops, SparseCore 0:
  14.5 59.4 all-gather.2
  125.5 38.5 reduce-scatter.1

commit v5 on v4

--- a/solution.py
+++ b/solution.py
@@ -93,9 +93,7 @@
     shards = iota((SHARDS, BAG * N), 0).astype(F32)
     slots = iota((CAP, BAG * N), 0).astype(F32)
     base = jnp.zeros((SHARDS, 1), F32)
-    ids = jnp.zeros((SHARDS, CAP), F32)
-    src = jnp.zeros((SHARDS, CAP), F32)
-    src_t = jnp.zeros((CAP, SHARDS), F32)
+    found = jnp.zeros((4 * SHARDS, CAP), F32)
     for f in range(F):
         hit = shards == shard[f : f + 1, :]
         one = jnp.where(hit, 1.0, 0.0)
@@ -103,17 +101,15 @@
         base = base + jnp.sum(one, axis=1, keepdims=True)
         rank = jnp.sum(one * before, axis=0, keepdims=True)
         place = jnp.where(slots == rank, 1.0, 0.0).astype(BF)
-
-        def put(v):
-            return jnp.where(hit, v[f : f + 1, :], 0.0).astype(BF)
-
-        lo, hi = put(bag_lo), put(bag_hi)
-        ids = ids + dot(put(row_lo), place, 1, 1) + dot(put(row_hi), place, 1, 1)
-        src = src + dot(lo, place, 1, 1) + dot(hi, place, 1, 1)
-        src_t = src_t + dot(place, lo, 1, 1) + dot(place, hi, 1, 1)
+        values = [
+            jnp.where(hit, v[f : f + 1, :], 0.0) for v in (row_lo, row_hi, bag_lo, bag_hi)
+        ]
+        found = found + dot(jnp.concatenate(values, axis=0).astype(BF), place, 1, 1)
+    ids = found[0:SHARDS] + found[SHARDS : 2 * SHARDS]
+    src = found[2 * SHARDS : 3 * SHARDS] + found[3 * SHARDS :] - 1.0
     ids_ref[...] = ids.astype(I32)
-    src_ref[...] = src.astype(I32) - 1
-    src_t_ref[...] = src_t.astype(I32) - 1
+    src_ref[...] = src.astype(I32)
+    src_t_ref[...] = jnp.transpose(src).astype(I32)
     for move in moves[3:]:
         move.wait()
     for j in range(BLOCKS):
@@ -359,7 +355,7 @@
         limit=56,
         far=(6,),
     )
-    arrived, part = lax.optimization_barrier((arrived, part))
+    arrived, _ = lax.optimization_barrier((arrived, part))
     over_y = lax.psum_scatter(
         part.reshape(DP * SHARDS * CHUNK, E), "y", scatter_dimension=0, tiled=True
     )

time: 211 us -> 198 us (0.938)
  waiting for transfers between devices: 68.5 us -> 60.5 us
  starting transfers between devices: 41.8 us -> 38.8 us
  Pallas kernels: 35.9 us -> 33.5 us
    reduce_scatter x1, waiting for transfers between devices: 7.89 us -> 0.02 us  [local(): lax.psum_scatter(part.reshape(DP * SHARDS * CHUNK, E), 'y', scatter_dimen...]
    all_to_all x1, starting transfers between devices: 7.63 us -> 4.16 us  [local(): lax.all_to_all(over_y, EMB, split_axis=0, concat_axis=0, tiled=True)]
    pallas_call x6, Pallas kernels: 35.9 us -> 33.5 us  [call(): pl.pallas_call(kernel, out_shape=outs, in_specs=[SMEM if x.size < 8 else...]
  transfers between devices with their start and end apart: 10 -> 10, of which waited for: 6 -> 5; matrix products, arithmetic and copies ran while one was open for 2% -> 2% of each run, Pallas kernels for 14% -> 15%
where the time goes in v5:
time: 198 us; the launch traced here: 197 us
  waiting for transfers between devices  60.5 us (31%)
  blocking collectives  42.2 us (21%)
  starting transfers between devices  38.8 us (20%)
  Pallas kernels  33.5 us (17%)
  between operations  14.3 us (7%)
  local copies, waits for them, and re-layouts  5.45 us (3%)
    pallas_call x6, Pallas kernels, call(): pl.pallas_call(kernel, out_shape=outs, in_specs=[SMEM if x.size < 8 else...  33.5 us
    all_to_all x1, waiting for transfers between devices, local(): lax.all_to_all(fetched, EMB, split_axis=0, concat_axis=0, tiled=True)  27 us
    all_to_all x1, blocking collectives, local(): lax.all_to_all(row_grad, owners, split_axis=0, concat_axis=0, tiled=True)  23.2 us
    all_to_all x1, blocking collectives, local(): ids = lax.all_to_all(ids, EMB, split_axis=0, concat_axis=0, tiled=True)  19 us
    all_to_all x1, waiting for transfers between devices, local(): arrived = lax.all_to_all(send, EMB, split_axis=0, concat_axis=0, tiled=True)  14.2 us
    ppermute x4, starting transfers between devices, partner(): return lax.ppermute(value, axes, [(i, i ^ mask) for i in range(size)])  12.7 us
    all_to_all x1, starting transfers between devices, local(): lax.all_to_all(spread, owners, split_axis=0, concat_axis=0, tiled=True)  11.7 us
    all_to_all x1, waiting for transfers between devices, local(): lax.all_to_all(spread, owners, split_axis=0, concat_axis=0, tiled=True)  10.5 us
  transfers between devices with their start and end apart: 10, of which 5 were waited for; matrix products, arithmetic and copies ran while one was open for 2% of the time, Pallas kernels for 15%

profile of v5, /device:TPU:1, one launch (start us, length us, event | category | flops | bytes accessed | tf_op | source)
XLA Modules:
  0.0 196.8 jit_solution(1344192653471643757)
XLA Ops:
  7.2 4.8 %index.1 = (s32[16,312]{1,0:T(8,128)}, s32[16,312]{1,0:T(8,128)}, s32[312,16]{1,0:T(8,128)}, bf16[3584,128]{1,0:T(8,128)(2,1)}) custom-call(s32[52,1,64]{2,1,0:T(1,128)} %bitcast.40, s32[52,64]{1,0:T(8,128)} %bitcast.39, s32[13,64]{1,0:T(8,128)} %bitcast.41, bf16[1792,128]{1,0:T(8,128)(2,1)} %down_hbm.1, bf16[128,1792]{1,0:T(8,128)(2,1)} %up_hbm.1), custom_call_target="tpu_custom_call" | custom-call | flops 400000000 | bytes 947456 | tf_op jit(solution)/shard_map/index/pallas_call | solution.py:48
  12.0 0.8 copy.21
  12.8 19.0 %all_to_all.44 = s32[16,1,312]{2,1,0:T(1,128)S(1)} all-to-all(s32[16,1,312]{2,1,0:T(1,128)S(1)} %copy.21), channel_id=1, replica_groups=mesh['xl'=2,'z'=8,'y'=8,'xh'=2,'core'=2] {'xl','z'}, dimensions={0} | all-to-all | bytes 39936 | tf_op jit(solution)/shard_map/all_to_all | solution.py:308
  31.9 4.1 %fetch.1 = bf16[16,312,128]{2,1,0:T(8,128)(2,1)} custom-call(s32[16,312]{1,0:T(8,128)S(1)} %bitcast.31, f32[1024,128]{1,0:T(8,128)S(1)} %copy-done), custom_call_target="tpu_custom_call" | custom-call | flops 1300000000 | bytes 544256 | tf_op jit(solution)/shard_map/fetch/pallas_call | solution.py:48
  36.0 3.8 %all-to-all-start.1 = ((bf16[16,312,128]{2,1,0:T(8,128)(2,1)}), bf16[16,312,128]{2,1,0:T(8,128)(2,1)S(1)}, u32[]{:S(2)}, u32[]{:S(2)}) async-start(bf16[16,312,128]{2,1,0:T(8,128)(2,1)} %fetch.1), calls=%async_computation.1 | async-start | bytes 2555904 | tf_op jit(solution)/shard_map/all_to_all | solution.py:312
  41.1 0.8 copy.22.label_ref
  42.5 27.0 %all-to-all-done.1.rows_ref = bf16[16,312,128]{2,1,0:T(8,128)(2,1)S(1)} async-done(((bf16[16,312,128]{2,1,0:T(8,128)(2,1)}), bf16[16,312,128]{2,1,0:T(8,128)(2,1)S(1)}, u32[]{:S(2)}, u32[]{:S(2)}) %all-to-all-start.1) | async-done | bytes 1277984 | tf_op jit(solution)/shard_map/all_to_all | solution.py:312
  69.5 2.8 %pool.1.pooled_ref.s0_ref = bf16[64,1664]{1,0:T(8,128)(2,1)S(1)} custom-call(bf16[16,312,128]{2,1,0:T(8,128)(2,1)S(1)} %all-to-all-done.1.rows_ref, s32[16,312]{1,0:T(8,128)S(1)} %copy-done.3), custom_call_target="tpu_custom_call" | custom-call | flops 1060000000 | bytes 1297920 | tf_op jit(solution)/shard_map/pool/pallas_call | solution.py:48
  72.3 4.5 %collective-permute-start = (bf16[64,1664]{1,0:T(8,128)(2,1)S(1)}, bf16[64,1664]{1,0:T(8,128)(2,1)S(1)}, u32[]{:S(2)}, u32[]{:S(2)}) collective-permute-start(bf16[64,1664]{1,0:T(8,128)(2,1)S(1)} %pool.1.pooled_ref.s0_ref), channel_id=1, source_target_pairs={{0,2},{2,0},{1,3},{3,1},{4,6},{6,4},{5,7},{7,5},{8,10},{10,8},{9,1... | collective-permute-start | bytes 638984 | tf_op jit(solution)/shard_map/ppermute | solution.py:271
  76.9 9.6 %main.1 = (f32[64,1664]{1,0:T(8,128)}, bf16[16,312,128]{2,1,0:T(8,128)(2,1)}) custom-call(s32[3]{0:T(128)} %pad_add_fusion.where_ref, bf16[64,1664]{1,0:T(8,128)(2,1)} %copy-done.1, bf16[256,128]{1,0:T(8,128)(2,1)} %dense_ref.3, bf16[4,3584,128]{2,1,0:T(8,128)(2,1)} %bitcast.37, f32[1,1792]{1,0:T(1,128)} %reshape.45.bias_ref, f32[1,1792]{1,0:T(1,128)} %reshape.46.head_ref, ...), custom_call_target="tpu_custom_call" | custom-call | flops 10000000000 | bytes 4409868 | tf_op jit(solution)/shard_map/main/pallas_call | solution.py:48
  86.5 6.3 %all-to-all-start.2 = ((bf16[16,312,128]{2,1,0:T(8,128)(2,1)}), bf16[16,312,128]{2,1,0:T(8,128)(2,1)S(1)}, u32[]{:S(2)}, u32[]{:S(2)}) async-start(bf16[16,312,128]{2,1,0:T(8,128)(2,1)} %get-tuple-element.24), calls=%async_computation.2 | async-start | bytes 2555904 | tf_op jit(solution)/shard_map/all_to_all | solution.py:337
  92.9 3.1 %collective-permute-start.1 = (bf16[64,1664]{1,0:T(8,128)(2,1)S(1)}, bf16[64,1664]{1,0:T(8,128)(2,1)S(1)}, u32[]{:S(2)}, u32[]{:S(2)}) collective-permute-start(bf16[64,1664]{1,0:T(8,128)(2,1)S(1)} %copy-done.2), channel_id=1, source_target_pairs={{0,1},{1,0},{2,3},{3,2},{4,5},{5,4},{6,7},{7,6},{8,9},{9,8},{10,11... | collective-permute-start | bytes 638984 | tf_op jit(solution)/shard_map/ppermute | solution.py:271
  96.0 1.9 collective-permute-start.2
  98.0 1.4 collective-permute-done.2.s3_ref
  100.1 8.8 %grads.1 = bf16[8,16,32,128]{3,2,1,0:T(8,128)(2,1)} custom-call(s32[3]{0:T(128)} %pad_add_fusion.where_ref, bf16[64,1664]{1,0:T(8,128)(2,1)} %copy-done.1, bf16[64,1664]{1,0:T(8,128)(2,1)} %copy-done.9, bf16[64,1664]{1,0:T(8,128)(2,1)} %copy-done.8, bf16[64,1664]{1,0:T(8,128)(2,1)} %copy-done.10, bf16[256,128]{1,0:T(8,128)(2,1)} %dense_ref.3, ...), custom_call_target="tpu_custom_call" | custom-call | flops 2000000000 | bytes 4602892 | tf_op jit(solution)/shard_map/grads/pallas_call | solution.py:48
  108.9 14.2 %all-to-all-done.2.rows_ref = bf16[16,312,128]{2,1,0:T(8,128)(2,1)S(1)} async-done(((bf16[16,312,128]{2,1,0:T(8,128)(2,1)}), bf16[16,312,128]{2,1,0:T(8,128)(2,1)S(1)}, u32[]{:S(2)}, u32[]{:S(2)}) %all-to-all-start.2) | async-done | bytes 1277984 | tf_op jit(solution)/shard_map/all_to_all | solution.py:337
  123.0 3.4 %scatter.1 = bf16[1024,128]{1,0:T(8,128)(2,1)S(1)} custom-call(s32[16,312]{1,0:T(8,128)S(1)} %bitcast.32, bf16[16,312,128]{2,1,0:T(8,128)(2,1)S(1)} %all-to-all-done.2.rows_ref), custom_call_target="tpu_custom_call" | custom-call | flops 1300000000 | bytes 1297920 | tf_op jit(solution)/shard_map/scatter/pallas_call | solution.py:48
  126.5 23.2 %all_to_all.45 = bf16[16,64,128]{2,1,0:T(8,128)(2,1)S(1)} all-to-all(bf16[16,64,128]{2,1,0:T(8,128)(2,1)S(1)} %bitcast.30), channel_id=1, replica_groups=mesh['xl'=2,'z'=8,'y'=8,'xh'=2,'core'=2] {'y','core'}, dimensions={0} | all-to-all | bytes 524288 | tf_op jit(solution)/shard_map/all_to_all | solution.py:372
  149.7 3.2 %collective-permute-start.3 = (f32[64,128]{1,0:T(8,128)S(1)}, f32[64,128]{1,0:T(8,128)S(1)}, u32[]{:S(2)}, u32[]{:S(2)}) collective-permute-start(f32[64,128]{1,0:T(8,128)S(1)} %convert_reduce_fusion), channel_id=1, source_target_pairs={{0,2},{2,0},{1,3},{3,1},{4,6},{6,4},{5,7},{7,5},{8,10},{10,8},{9,1... | collective-permute-start | bytes 98312 | tf_op jit(solution)/shard_map/ppermute | solution.py:271
  152.9 4.2 %all-to-all-start.4 = ((bf16[16,32,128]{2,1,0:T(8,128)(2,1)}), bf16[16,32,128]{2,1,0:T(8,128)(2,1)S(1)}, u32[]{:S(2)}, u32[]{:S(2)}) async-start(bf16[16,32,128]{2,1,0:T(8,128)(2,1)} %bitcast.34), calls=%async_computation.5 | async-start | bytes 262144 | tf_op jit(solution)/shard_map/all_to_all | solution.py:376
  157.1 7.4 %all-to-all-done.4 = bf16[16,32,128]{2,1,0:T(8,128)(2,1)S(1)} async-done(((bf16[16,32,128]{2,1,0:T(8,128)(2,1)}), bf16[16,32,128]{2,1,0:T(8,128)(2,1)S(1)}, u32[]{:S(2)}, u32[]{:S(2)}) %all-to-all-start.4) | async-done | bytes 131104 | tf_op jit(solution)/shard_map/all_to_all | solution.py:376
  165.3 11.7 %all-to-all-start.5 = ((bf16[16,64,128]{2,1,0:T(8,128)(2,1)}), bf16[16,64,128]{2,1,0:T(8,128)(2,1)S(1)}, u32[]{:S(2)}, u32[]{:S(2)}) async-start(bf16[16,64,128]{2,1,0:T(8,128)(2,1)} %bitcast.13), calls=%async_computation.6 | async-start | bytes 524288 | tf_op jit(solution)/shard_map/all_to_all | solution.py:379
  178.2 10.5 %all-to-all-done.5 = bf16[16,64,128]{2,1,0:T(8,128)(2,1)S(1)} async-done(((bf16[16,64,128]{2,1,0:T(8,128)(2,1)}), bf16[16,64,128]{2,1,0:T(8,128)(2,1)S(1)}, u32[]{:S(2)}, u32[]{:S(2)}) %all-to-all-start.5) | async-done | bytes 262176 | tf_op jit(solution)/shard_map/all_to_all | solution.py:379
  188.9 1.1 fusion
  (42 shorter events, 4.9 us)
Async XLA Ops:
  7.2 69.7 %all-gather.3.cloned.1.call-start = ((), (), s32[]{:S(2)}) async-start(), calls=%async_computation.8 | async-start | bytes 4587520 | tf_op jit(solution)/shard_map/gather_weights/all_gather | solution.py:307
  7.2 24.6 %copy-start = (f32[1024,128]{1,0:T(8,128)S(1)}, f32[1024,128]{1,0:T(8,128)}, u32[]{:S(2)}) copy-start(f32[1024,128]{1,0:T(8,128)} %table_ref.1) | copy-start | bytes 1572868
  36.0 3.9 %copy-start.5 = (f32[1792]{0:T(1024)S(1)}, f32[1792]{0:T(1024)}, u32[]{:S(2)}) copy-start(f32[1792]{0:T(1024)} %param.22) | copy-start | bytes 21508
  36.0 4.5 %copy-start.6 = (f32[1792]{0:T(1024)S(1)}, f32[1792]{0:T(1024)}, u32[]{:S(2)}) copy-start(f32[1792]{0:T(1024)} %param.23) | copy-start | bytes 21508
  36.0 5.1 %copy-start.7 = (s32[256]{0:T(256)S(1)}, s32[256]{0:T(256)}, u32[]{:S(2)}) copy-start(s32[256]{0:T(256)} %param.18) | copy-start | bytes 3076
  36.0 33.5 %copy-start.3 = (s32[16,312]{1,0:T(8,128)S(1)}, s32[16,312]{1,0:T(8,128)}, u32[]{:S(2)}) copy-start(s32[16,312]{1,0:T(8,128)} %get-tuple-element.20.src_ref) | copy-start | bytes 59908
  36.0 33.5 %all-to-all-start.1 = ((bf16[16,312,128]{2,1,0:T(8,128)(2,1)}), bf16[16,312,128]{2,1,0:T(8,128)(2,1)S(1)}, u32[]{:S(2)}, u32[]{:S(2)}) async-start(bf16[16,312,128]{2,1,0:T(8,128)(2,1)} %fetch.1), calls=%async_computation.1 | async-start | bytes 2555904 | tf_op jit(solution)/shard_map/all_to_all | solution.py:312
  72.3 4.6 %copy-start.1 = (bf16[64,1664]{1,0:T(8,128)(2,1)}, bf16[64,1664]{1,0:T(8,128)(2,1)S(1)}, u32[]{:S(2)}) copy-start(bf16[64,1664]{1,0:T(8,128)(2,1)S(1)} %pool.1.pooled_ref.s0_ref) | copy-start | bytes 638980
  72.3 14.2 %collective-permute-start = (bf16[64,1664]{1,0:T(8,128)(2,1)S(1)}, bf16[64,1664]{1,0:T(8,128)(2,1)S(1)}, u32[]{:S(2)}, u32[]{:S(2)}) collective-permute-start(bf16[64,1664]{1,0:T(8,128)(2,1)S(1)} %pool.1.pooled_ref.s0_ref), channel_id=1, source_target_pairs={{0,2},{2,0},{1,3},{3,1},{4,6},{6,4},{5,7},{7,5},{8,10},{10,8},{9,1... | collective-permute-start | bytes 638984 | tf_op jit(solution)/shard_map/ppermute | solution.py:271
  86.5 9.5 %copy-start.8 = (bf16[64,1664]{1,0:T(8,128)(2,1)}, bf16[64,1664]{1,0:T(8,128)(2,1)S(1)}, u32[]{:S(2)}) copy-start(bf16[64,1664]{1,0:T(8,128)(2,1)S(1)} %collective-permute-done.s2_ref) | copy-start | bytes 638980
  86.5 6.4 %copy-start.2 = (bf16[64,1664]{1,0:T(8,128)(2,1)S(1)}, bf16[64,1664]{1,0:T(8,128)(2,1)}, u32[]{:S(2)}) copy-start(bf16[64,1664]{1,0:T(8,128)(2,1)} %copy-done.1) | copy-start | bytes 638980
  86.5 36.5 %all-to-all-start.2 = ((bf16[16,312,128]{2,1,0:T(8,128)(2,1)}), bf16[16,312,128]{2,1,0:T(8,128)(2,1)S(1)}, u32[]{:S(2)}, u32[]{:S(2)}) async-start(bf16[16,312,128]{2,1,0:T(8,128)(2,1)} %get-tuple-element.24), calls=%async_computation.2 | async-start | bytes 2555904 | tf_op jit(solution)/shard_map/all_to_all | solution.py:337
  92.8 60.1 %reduce-scatter.2.cloned.1.call-start = ((), (), s32[]{:S(2)}) async-start(), calls=%async_computation.7 | async-start | bytes 1179648 | tf_op jit(solution)/shard_map/reduce_scatter | solution.py:359
  92.9 5.0 %collective-permute-start.1 = (bf16[64,1664]{1,0:T(8,128)(2,1)S(1)}, bf16[64,1664]{1,0:T(8,128)(2,1)S(1)}, u32[]{:S(2)}, u32[]{:S(2)}) collective-permute-start(bf16[64,1664]{1,0:T(8,128)(2,1)S(1)} %copy-done.2), channel_id=1, source_target_pairs={{0,1},{1,0},{2,3},{3,2},{4,5},{5,4},{6,7},{7,6},{8,9},{9,8},{10,11... | collective-permute-start | bytes 638984 | tf_op jit(solution)/shard_map/ppermute | solution.py:271
  96.0 3.4 %collective-permute-start.2 = (bf16[64,1664]{1,0:T(8,128)(2,1)S(1)}, bf16[64,1664]{1,0:T(8,128)(2,1)S(1)}, u32[]{:S(2)}, u32[]{:S(2)}) collective-permute-start(bf16[64,1664]{1,0:T(8,128)(2,1)S(1)} %collective-permute-done.s2_ref), channel_id=1, source_target_pairs={{0,1},{1,0},{2,3},{3,2},{4,5},{5,4},{6,7},{7,6},{8,9},{9,8},{10,11... | collective-permute-start | bytes 638984 | tf_op jit(solution)/shard_map/ppermute | solution.py:271
  97.9 1.4 copy-start.9
  99.4 0.7 copy-start.10
  149.7 7.4 %collective-permute-start.3 = (f32[64,128]{1,0:T(8,128)S(1)}, f32[64,128]{1,0:T(8,128)S(1)}, u32[]{:S(2)}, u32[]{:S(2)}) collective-permute-start(f32[64,128]{1,0:T(8,128)S(1)} %convert_reduce_fusion), channel_id=1, source_target_pairs={{0,2},{2,0},{1,3},{3,1},{4,6},{6,4},{5,7},{7,5},{8,10},{10,8},{9,1... | collective-permute-start | bytes 98312 | tf_op jit(solution)/shard_map/ppermute | solution.py:271
  152.9 35.9 %copy-start.4 = (f32[1024,128]{1,0:T(8,128)S(1)}, f32[1024,128]{1,0:T(8,128)}, u32[]{:S(2)}) copy-start(f32[1024,128]{1,0:T(8,128)} %param.13) | copy-start | bytes 1572868
  152.9 11.6 %all-to-all-start.4 = ((bf16[16,32,128]{2,1,0:T(8,128)(2,1)}), bf16[16,32,128]{2,1,0:T(8,128)(2,1)S(1)}, u32[]{:S(2)}, u32[]{:S(2)}) async-start(bf16[16,32,128]{2,1,0:T(8,128)(2,1)} %bitcast.34), calls=%async_computation.5 | async-start | bytes 262144 | tf_op jit(solution)/shard_map/all_to_all | solution.py:376
  165.3 23.4 %all-to-all-start.5 = ((bf16[16,64,128]{2,1,0:T(8,128)(2,1)}), bf16[16,64,128]{2,1,0:T(8,128)(2,1)S(1)}, u32[]{:S(2)}, u32[]{:S(2)}) async-start(bf16[16,64,128]{2,1,0:T(8,128)(2,1)} %bitcast.13), calls=%async_computation.6 | async-start | bytes 524288 | tf_op jit(solution)/shard_map/all_to_all | solution.py:379
Sparse Core Ops, SparseCore 0:
  12.2 59.4 all-gather.2
  109.0 39.6 reduce-scatter.1

commit v6 on v5

--- a/solution.py
+++ b/solution.py
@@ -150,7 +150,8 @@
     return hidden, crossed, xf, x_next, grad_logit, grad_next, grad_next * xf
 
 
-def pool_kernel(rows_ref, src_ref, pooled_ref, acc_ref):
+def pool_kernel(rows_ref, src_ref, pack_ref, pooled_ref, down_ref, up_ref, acc_ref, sems):
+    moves = start_weights(pack_ref, down_ref, up_ref, sems)
     bags = iota((BAGS, CAP), 0)
     for s in range(SHARDS):
         pick = jnp.where(bags == src_ref[s : s + 1, :], 1.0, 0.0).astype(BF)
@@ -161,17 +162,16 @@
             acc_ref[...] += term
     for f in range(F):
         pooled_ref[:, f * E : (f + 1) * E] = acc_ref[f * N : (f + 1) * N, :].astype(BF)
+    for move in moves:
+        move.wait()
 
 
 def main_kernel(
-    where_ref, pooled_ref, dense_ref, pack_ref, bias_ref, head_ref, label_ref, feedback_ref,
-    src_t_ref, carried_ref, send_ref, down_ref, up_ref, sems,
+    where_ref, pooled_ref, dense_ref, down_ref, up_ref, bias_ref, head_ref, label_ref, feedback_ref,
+    src_t_ref, carried_ref, send_ref,
 ):
-    moves = start_weights(pack_ref, down_ref, up_ref, sems)
     first = pl.multiple_of(where_ref[0] * N, N)
     x = jnp.concatenate([dense_ref[pl.ds(first, N), :], pooled_ref[...]], axis=1)
-    for move in moves:
-        move.wait()
     up, bias, head = up_ref[...], bias_ref[...], head_ref[...]
     _, crossed, _, _, _, grad_next, cross = forward(
         x, down_ref[...], up, bias, head, label_ref[pl.ds(first, N), :]
@@ -190,17 +190,14 @@
 
 
 def grads_kernel(
-    where_ref, s0_ref, s1_ref, s2_ref, s3_ref, dense_ref, pack_ref, bias_ref, head_ref, label_ref,
-    out_ref, x_ref, down_ref, up_ref, hidden_ref, down_grad_ref, up_grad_ref, sems,
+    where_ref, s0_ref, s1_ref, s2_ref, s3_ref, dense_ref, down_ref, up_ref, bias_ref, head_ref,
+    label_ref, out_ref, x_ref, hidden_ref, down_grad_ref, up_grad_ref,
 ):
-    moves = start_weights(pack_ref, down_ref, up_ref, sems)
     t = where_ref[0]
     x_ref[:, 0:E] = dense_ref[...]
     for m, ref in enumerate((s0_ref, s1_ref, s2_ref, s3_ref)):
         x_ref[pl.ds(pl.multiple_of((t ^ m) * N, N), N), E:] = ref[...]
     x = x_ref[...]
-    for move in moves:
-        move.wait()
     hidden, _, _, x_next, grad_logit, _, cross = forward(
         x, down_ref[...], up_ref[...], bias_ref[...], head_ref[...], label_ref[...]
     )
@@ -250,8 +247,10 @@
             axis=0,
         )
         got = dot(select, block_rows).astype(BF)
+        w = where_ref[2] ^ e
+        place = ((w >> 3) & 1) * 8 + (w & 1) * 4 + ((w >> 1) & 3)
         for k in range(DP):
-            out_ref[k, e] = got[CHUNK * k : CHUNK * (k + 1)]
+            out_ref[k, place] = got[CHUNK * k : CHUNK * (k + 1)]
 
 
 def scatter_kernel(ids_ref, rows_ref, out_ref, acc_ref):
@@ -310,28 +309,27 @@
         fetch_kernel, [sds((SHARDS, CAP, E), BF)], (ids, emb_table), "fetch", flops=1_300_000_000
     )
     returned = lax.all_to_all(fetched, EMB, split_axis=0, concat_axis=0, tiled=True)
-    (pooled,) = call(
+    pooled, down_all, up_all = call(
         pool_kernel,
-        [sds((N, POOL), BF)],
-        (returned, src),
+        [sds((N, POOL), BF), sds((DX, TP * RANK), BF), sds((TP * RANK, DX), BF)],
+        (returned, src, pack_all),
         "pool",
-        scratch=[pltpu.VMEM((BAGS, E), F32)],
+        scratch=[
+            pltpu.VMEM((BAGS, E), F32),
+            pltpu.SemaphoreType.DMA((TP * (1 + BLOCKS),)),
+        ],
         flops=1_060_000_000,
+        limit=47,
+        far=(2,),
     )
     far = partner(pooled, "xh", 1)
     carried, send = call(
         main_kernel,
         (sds((N, POOL), F32), sds((SHARDS, CAP, E), BF)),
-        (where, pooled, dense_input, pack_all, bias, head, label, feedback, src_t),
+        (where, pooled, dense_input, down_all, up_all, bias, head, label, feedback, src_t),
         "main",
-        scratch=[
-            pltpu.VMEM((DX, TP * RANK), BF),
-            pltpu.VMEM((TP * RANK, DX), BF),
-            pltpu.SemaphoreType.DMA((TP * (1 + BLOCKS),)),
-        ],
         flops=10_000_000_000,
-        limit=56,
-        far=(3,),
+        limit=40,
     )
     far, again, send = lax.optimization_barrier((far, pooled, send))
     arrived = lax.all_to_all(send, EMB, split_axis=0, concat_axis=0, tiled=True)
@@ -340,20 +338,16 @@
     (part,) = call(
         grads_kernel,
         [sds((DP, SHARDS, CHUNK, E), BF)],
-        (where, pooled, near, far, far_near, dense_input, pack_all, bias, head, label),
+        (where, pooled, near, far, far_near, dense_input, down_all, up_all, bias, head, label),
         "grads",
         scratch=[
             pltpu.VMEM((DENSE, DX), BF),
-            pltpu.VMEM((DX, TP * RANK), BF),
-            pltpu.VMEM((TP * RANK, DX), BF),
             pltpu.VMEM((TP, DENSE, RANK), BF),
             pltpu.VMEM((DX, RANK), BF),
             pltpu.VMEM((DX, RANK), BF),
-            pltpu.SemaphoreType.DMA((TP * (1 + BLOCKS),)),
         ],
         flops=2_000_000_000,
-        limit=56,
-        far=(6,),
+        limit=40,
     )
     arrived, _ = lax.optimization_barrier((arrived, part))
     over_y = lax.psum_scatter(
@@ -373,14 +367,20 @@
     mine = jnp.sum(by_y.reshape(pieces, ROWS // pieces, E).astype(F32), axis=0)
     mine = (mine + partner(mine, "xh", 1)).astype(BF)
     over_y = over_y.reshape(SHARDS, CHUNK, E)
-    over_all = lax.all_to_all(over_y, EMB, split_axis=0, concat_axis=0, tiled=True)
+    pairs = [over_y[0:4].astype(F32)] + [
+        partner(over_y[4 * c : 4 * c + 4], EMB, mask).astype(F32)
+        for c, mask in ((1, 1), (2, 8), (3, 9))
+    ]
+    pairs = (pairs[0] + pairs[1]) + (pairs[2] + pairs[3])
     spread = jnp.broadcast_to(mine[None], (pieces, ROWS // pieces, E)).reshape(ROWS, E)
-    spread, over_all = lax.optimization_barrier((spread, over_all))
+    last = [pairs[0]] + [pairs[i].astype(BF) for i in (1, 2, 3)]
+    spread, *last = lax.optimization_barrier((spread, *last))
     full = lax.all_to_all(spread, owners, split_axis=0, concat_axis=0, tiled=True)
+    last = [last[0]] + [partner(last[i], EMB, 2 * i).astype(F32) for i in (1, 2, 3)]
+    grads = (last[0] + last[1]) + (last[2] + last[3])
     full = full.astype(F32)
     accum_new = row_accum + full * full
     table_new = emb_table - LEARN * full / jnp.sqrt(accum_new)
-    grads = jnp.sum(over_all.astype(F32), axis=0)
     grad_down = grads[0:GROUP]
     grad_up = grads[GROUP : 2 * GROUP].T
     grad_head = grads[2 * GROUP, 0:GROUP]

time: 198 us -> 215 us (1.086)
  starting transfers between devices: 38.8 us -> 68.3 us
  blocking collectives: 42.2 us -> 19 us
  waiting for transfers between devices: 60.5 us -> 74.3 us
  Pallas kernels: 33.5 us -> 30.2 us
    all_to_all x1 -> x0, blocking collectives: 23.2 us -> none  [local(): lax.all_to_all(row_grad, owners, split_axis=0, concat_axis=0, tiled=True)]
    ppermute x4 -> x10, starting transfers between devices: 12.7 us -> 32.4 us  [partner(): return lax.ppermute(value, axes, [(i, i ^ mask) for i in range(size)])]
    reduce_scatter x1, waiting for transfers between devices: 0.02 us -> 11.8 us  [local(): lax.psum_scatter(part.reshape(DP * SHARDS * CHUNK, E), 'y', scatter_dimen...]
    all_to_all x1, waiting for transfers between devices: 7.4 us -> 0.01 us  [local(): lax.all_to_all(row_grad, owners, split_axis=0, concat_axis=0, tiled=True)]
    all_to_all x1, starting transfers between devices: 4.16 us -> 9.39 us  [local(): lax.all_to_all(row_grad, owners, split_axis=0, concat_axis=0, tiled=True)]
    ppermute x4 -> x10, waiting for transfers between devices: 1.42 us -> 5.69 us  [partner(): return lax.ppermute(value, axes, [(i, i ^ mask) for i in range(size)])]
    pallas_call x6, Pallas kernels: 33.5 us -> 30.2 us  [call(): pl.pallas_call(kernel, out_shape=outs, in_specs=[SMEM if x.size < 8 else...]
    all_to_all x1, starting transfers between devices: 6.31 us -> 8.98 us  [local(): arrived = lax.all_to_all(send, EMB, split_axis=0, concat_axis=0, tiled=True)]
  transfers between devices with their start and end apart: 10 -> 16, of which waited for: 5 -> 10; matrix products, arithmetic and copies ran while one was open for 2% -> 1% of each run, Pallas kernels for 15% -> 9%
where the time goes in v6:
time: 215 us; the launch traced here: 214 us
  waiting for transfers between devices  74.3 us (35%)
  starting transfers between devices  68.3 us (32%)
  Pallas kernels  30.2 us (14%)
  blocking collectives  19 us (9%)
  between operations  14.4 us (7%)
  local copies, waits for them, and re-layouts  6.72 us (3%)
    ppermute x10, starting transfers between devices, partner(): return lax.ppermute(value, axes, [(i, i ^ mask) for i in range(size)])  32.4 us
    pallas_call x6, Pallas kernels, call(): pl.pallas_call(kernel, out_shape=outs, in_specs=[SMEM if x.size < 8 else...  30.2 us
    all_to_all x1, waiting for transfers between devices, local(): lax.all_to_all(fetched, EMB, split_axis=0, concat_axis=0, tiled=True)  29.3 us
    all_to_all x1, blocking collectives, local(): ids = lax.all_to_all(ids, EMB, split_axis=0, concat_axis=0, tiled=True)  19 us
    all_to_all x1, waiting for transfers between devices, local(): arrived = lax.all_to_all(send, EMB, split_axis=0, concat_axis=0, tiled=True)  14.9 us
    all_to_all x1, starting transfers between devices, local(): lax.all_to_all(spread, owners, split_axis=0, concat_axis=0, tiled=True)  13.7 us
    reduce_scatter x1, waiting for transfers between devices, local(): lax.psum_scatter(part.reshape(DP * SHARDS * CHUNK, E), 'y', scatter_dimen...  11.8 us
    all_to_all x1, waiting for transfers between devices, local(): lax.all_to_all(spread, owners, split_axis=0, concat_axis=0, tiled=True)  10.5 us
  transfers between devices with their start and end apart: 16, of which 10 were waited for; matrix products, arithmetic and copies ran while one was open for 1% of the time, Pallas kernels for 9%

profile of v6, /device:TPU:1, one launch (start us, length us, event | category | flops | bytes accessed | tf_op | source)
XLA Modules:
  0.0 214.4 jit_solution(7937185396095169660)
XLA Ops:
  7.2 4.8 %index.1 = (s32[16,312]{1,0:T(8,128)}, s32[16,312]{1,0:T(8,128)}, s32[312,16]{1,0:T(8,128)}, bf16[3584,128]{1,0:T(8,128)(2,1)}) custom-call(s32[52,1,64]{2,1,0:T(1,128)} %bitcast.52, s32[52,64]{1,0:T(8,128)} %bitcast.51, s32[13,64]{1,0:T(8,128)} %bitcast.53, bf16[1792,128]{1,0:T(8,128)(2,1)} %down_hbm.1, bf16[128,1792]{1,0:T(8,128)(2,1)} %up_hbm.1), custom_call_target="tpu_custom_call" | custom-call | flops 400000000 | bytes 947456 | tf_op jit(solution)/shard_map/index/pallas_call | solution.py:48
  12.8 19.0 %all_to_all.39 = s32[16,1,312]{2,1,0:T(1,128)S(1)} all-to-all(s32[16,1,312]{2,1,0:T(1,128)S(1)} %copy.21), channel_id=1, replica_groups=mesh['xl'=2,'z'=8,'y'=8,'xh'=2,'core'=2] {'xl','z'}, dimensions={0} | all-to-all | bytes 39936 | tf_op jit(solution)/shard_map/all_to_all | solution.py:307
  31.8 4.1 %fetch.1 = bf16[16,312,128]{2,1,0:T(8,128)(2,1)} custom-call(s32[16,312]{1,0:T(8,128)S(1)} %bitcast.42, f32[1024,128]{1,0:T(8,128)S(1)} %copy-done), custom_call_target="tpu_custom_call" | custom-call | flops 1300000000 | bytes 544256 | tf_op jit(solution)/shard_map/fetch/pallas_call | solution.py:48
  36.0 3.8 %all-to-all-start.1 = ((bf16[16,312,128]{2,1,0:T(8,128)(2,1)}), bf16[16,312,128]{2,1,0:T(8,128)(2,1)S(1)}, u32[]{:S(2)}, u32[]{:S(2)}) async-start(bf16[16,312,128]{2,1,0:T(8,128)(2,1)} %fetch.1), calls=%async_computation.1 | async-start | bytes 2555904 | tf_op jit(solution)/shard_map/all_to_all | solution.py:311
  40.1 29.3 %all-to-all-done.1.rows_ref = bf16[16,312,128]{2,1,0:T(8,128)(2,1)S(1)} async-done(((bf16[16,312,128]{2,1,0:T(8,128)(2,1)}), bf16[16,312,128]{2,1,0:T(8,128)(2,1)S(1)}, u32[]{:S(2)}, u32[]{:S(2)}) %all-to-all-start.1) | async-done | bytes 1277984 | tf_op jit(solution)/shard_map/all_to_all | solution.py:311
  69.5 2.2 %all-gather.3.cloned.1.call-done = bf16[14336,128]{1,0:T(8,128)(2,1)} async-done(((bf16[3584,128]{1,0:T(8,128)(2,1)}), bf16[14336,128]{1,0:T(8,128)(2,1)}) %all-gather.3.cloned.1.call-update) | async-done | bytes 3670032 | tf_op jit(solution)/shard_map/gather_weights/all_gather | solution.py:306
  71.7 5.2 %pool.1 = (bf16[64,1664]{1,0:T(8,128)(2,1)S(1)}, bf16[1792,512]{1,0:T(8,128)(2,1)S(1)}, bf16[512,1792]{1,0:T(8,128)(2,1)S(1)}) custom-call(bf16[16,312,128]{2,1,0:T(8,128)(2,1)S(1)} %all-to-all-done.1.rows_ref, s32[16,312]{1,0:T(8,128)S(1)} %copy-done.1, bf16[4,3584,128]{2,1,0:T(8,128)(2,1)} %bitcast.44), custom_call_target="tpu_custom_call" | custom-call | flops 1060000000 | bytes 4967936 | tf_op jit(solution)/shard_map/pool/pallas_call | solution.py:48
  76.9 2.4 %collective-permute-start = (bf16[64,1664]{1,0:T(8,128)(2,1)S(1)}, bf16[64,1664]{1,0:T(8,128)(2,1)S(1)}, u32[]{:S(2)}, u32[]{:S(2)}) collective-permute-start(bf16[64,1664]{1,0:T(8,128)(2,1)S(1)} %get-tuple-element.34.pooled_ref.s0_ref), channel_id=1, source_target_pairs={{0,2},{2,0},{1,3},{3,1},{4,6},{6,4},{5,7},{7,5},{8,10},{10,8},{9,1... | collective-permute-start | bytes 638984 | tf_op jit(solution)/shard_map/ppermute | solution.py:270
  79.3 6.4 %main.1 = (f32[64,1664]{1,0:T(8,128)}, bf16[16,312,128]{2,1,0:T(8,128)(2,1)}) custom-call(s32[3]{0:T(128)S(1)} %pad_add_fusion.where_ref, bf16[64,1664]{1,0:T(8,128)(2,1)S(1)} %get-tuple-element.34.pooled_ref.s0_ref, bf16[256,128]{1,0:T(8,128)(2,1)S(1)} %copy-done.7, bf16[1792,512]{1,0:T(8,128)(2,1)S(1)} %get-tuple-element.29.down_ref, ...), custom_call_target="tpu_custom_call" | custom-call | flops 10000000000 | bytes 4409868 | tf_op jit(solution)/shard_map/main/pallas_call | solution.py:48
  86.1 9.0 %all-to-all-start.2 = ((bf16[16,312,128]{2,1,0:T(8,128)(2,1)}), bf16[16,312,128]{2,1,0:T(8,128)(2,1)S(1)}, u32[]{:S(2)}, u32[]{:S(2)}) async-start(bf16[16,312,128]{2,1,0:T(8,128)(2,1)} %get-tuple-element.33), calls=%async_computation.2 | async-start | bytes 2555904 | tf_op jit(solution)/shard_map/all_to_all | solution.py:335
  95.1 3.3 %collective-permute-start.1 = (bf16[64,1664]{1,0:T(8,128)(2,1)S(1)}, bf16[64,1664]{1,0:T(8,128)(2,1)S(1)}, u32[]{:S(2)}, u32[]{:S(2)}) collective-permute-start(bf16[64,1664]{1,0:T(8,128)(2,1)S(1)} %get-tuple-element.34.pooled_ref.s0_ref), channel_id=1, source_target_pairs={{0,1},{1,0},{2,3},{3,2},{4,5},{5,4},{6,7},{7,6},{8,9},{9,8},{10,11... | collective-permute-start | bytes 638984 | tf_op jit(solution)/shard_map/ppermute | solution.py:270
  104.7 5.6 %grads.1 = bf16[8,16,32,128]{3,2,1,0:T(8,128)(2,1)} custom-call(s32[3]{0:T(128)S(1)} %pad_add_fusion.where_ref, bf16[64,1664]{1,0:T(8,128)(2,1)S(1)} %get-tuple-element.34.pooled_ref.s0_ref, bf16[64,1664]{1,0:T(8,128)(2,1)S(1)} %collective-permute-done.1.s1_ref, bf16[64,1664]{1,0:T(8,128)(2,1)S(1)} %collective-permute-done.s2_ref, ...), custom_call_target="tpu_custom_call" | custom-call | flops 2000000000 | bytes 4602892 | tf_op jit(solution)/shard_map/grads/pallas_call | solution.py:48
  110.3 14.9 %all-to-all-done.2.rows_ref = bf16[16,312,128]{2,1,0:T(8,128)(2,1)S(1)} async-done(((bf16[16,312,128]{2,1,0:T(8,128)(2,1)}), bf16[16,312,128]{2,1,0:T(8,128)(2,1)S(1)}, u32[]{:S(2)}, u32[]{:S(2)}) %all-to-all-start.2) | async-done | bytes 1277984 | tf_op jit(solution)/shard_map/all_to_all | solution.py:335
  125.2 4.2 %scatter.1 = bf16[1024,128]{1,0:T(8,128)(2,1)} custom-call(s32[16,312]{1,0:T(8,128)S(1)} %bitcast.43, bf16[16,312,128]{2,1,0:T(8,128)(2,1)S(1)} %all-to-all-done.2.rows_ref), custom_call_target="tpu_custom_call" | custom-call | flops 1300000000 | bytes 1297920 | tf_op jit(solution)/shard_map/scatter/pallas_call | solution.py:48
  129.3 9.4 %all-to-all-start.3 = ((bf16[16,64,128]{2,1,0:T(8,128)(2,1)}), bf16[16,64,128]{2,1,0:T(8,128)(2,1)S(1)}, u32[]{:S(2)}, u32[]{:S(2)}) async-start(bf16[16,64,128]{2,1,0:T(8,128)(2,1)} %bitcast.9), calls=%async_computation.3 | async-start | bytes 524288 | tf_op jit(solution)/shard_map/all_to_all | solution.py:366
  138.7 11.8 %reduce-scatter.2.cloned.1.call-done = bf16[512,128]{1,0:T(8,128)(2,1)} async-done(((bf16[4096,128]{1,0:T(8,128)(2,1)}), bf16[512,128]{1,0:T(8,128)(2,1)}) %reduce-scatter.2.cloned.1.call-update) | async-done | bytes 131088 | tf_op jit(solution)/shard_map/reduce_scatter | solution.py:353
  151.3 4.1 %collective-permute-start.6 = (bf16[4,32,128]{2,1,0:T(8,128)(2,1)S(1)}, bf16[4,32,128]{2,1,0:T(8,128)(2,1)S(1)}, u32[]{:S(2)}, u32[]{:S(2)}) collective-permute-start(bf16[4,32,128]{2,1,0:T(8,128)(2,1)S(1)} %bitcast.48), channel_id=1, source_target_pairs={{0,288},{32,256},{64,352},{96,320},{128,416},{160,384},{192,480},{... | collective-permute-start | bytes 98312 | tf_op jit(solution)/shard_map/ppermute | solution.py:270
  157.4 2.3 %collective-permute-start.4 = (bf16[4,32,128]{2,1,0:T(8,128)(2,1)S(1)}, bf16[4,32,128]{2,1,0:T(8,128)(2,1)S(1)}, u32[]{:S(2)}, u32[]{:S(2)}) collective-permute-start(bf16[4,32,128]{2,1,0:T(8,128)(2,1)S(1)} %bitcast.46), channel_id=1, source_target_pairs={{0,32},{32,0},{64,96},{96,64},{128,160},{160,128},{192,224},{224,1... | collective-permute-start | bytes 98312 | tf_op jit(solution)/shard_map/ppermute | solution.py:270
  160.1 1.9 collective-permute-done.4
  162.2 4.7 %collective-permute-start.3 = (f32[64,128]{1,0:T(8,128)S(1)}, f32[64,128]{1,0:T(8,128)S(1)}, u32[]{:S(2)}, u32[]{:S(2)}) collective-permute-start(f32[64,128]{1,0:T(8,128)S(1)} %convert_reduce_fusion), channel_id=1, source_target_pairs={{0,2},{2,0},{1,3},{3,1},{4,6},{6,4},{5,7},{7,5},{8,10},{10,8},{9,1... | collective-permute-start | bytes 98312 | tf_op jit(solution)/shard_map/ppermute | solution.py:270
  169.2 5.7 %collective-permute-start.9 = (bf16[32,128]{1,0:T(8,128)(2,1)S(1)}, bf16[32,128]{1,0:T(8,128)(2,1)S(1)}, u32[]{:S(2)}, u32[]{:S(2)}) collective-permute-start(bf16[32,128]{1,0:T(8,128)(2,1)S(1)} %get-tuple-element.42), channel_id=1, source_target_pairs={{0,192},{32,224},{64,128},{96,160},{128,64},{160,96},{192,0},{224,... | collective-permute-start | bytes 24584 | tf_op jit(solution)/shard_map/ppermute | solution.py:270
  175.0 4.1 %collective-permute-start.8 = (bf16[32,128]{1,0:T(8,128)(2,1)S(1)}, bf16[32,128]{1,0:T(8,128)(2,1)S(1)}, u32[]{:S(2)}, u32[]{:S(2)}) collective-permute-start(bf16[32,128]{1,0:T(8,128)(2,1)S(1)} %get-tuple-element.41), channel_id=1, source_target_pairs={{0,128},{32,160},{64,192},{96,224},{128,0},{160,32},{192,64},{224,... | collective-permute-start | bytes 24584 | tf_op jit(solution)/shard_map/ppermute | solution.py:270
  181.0 13.7 %all-to-all-start.4 = ((bf16[16,64,128]{2,1,0:T(8,128)(2,1)}), bf16[16,64,128]{2,1,0:T(8,128)(2,1)S(1)}, u32[]{:S(2)}, u32[]{:S(2)}) async-start(bf16[16,64,128]{2,1,0:T(8,128)(2,1)} %bitcast.20), calls=%async_computation.5 | async-start | bytes 524288 | tf_op jit(solution)/shard_map/all_to_all | solution.py:378
  195.9 10.5 %all-to-all-done.4 = bf16[16,64,128]{2,1,0:T(8,128)(2,1)S(1)} async-done(((bf16[16,64,128]{2,1,0:T(8,128)(2,1)}), bf16[16,64,128]{2,1,0:T(8,128)(2,1)S(1)}, u32[]{:S(2)}, u32[]{:S(2)}) %all-to-all-start.4) | async-done | bytes 262176 | tf_op jit(solution)/shard_map/all_to_all | solution.py:378
  (61 shorter events, 17.7 us)
Async XLA Ops:
  7.2 64.5 %all-gather.3.cloned.1.call-start = ((), (), s32[]{:S(2)}) async-start(), calls=%async_computation.7 | async-start | bytes 4587520 | tf_op jit(solution)/shard_map/gather_weights/all_gather | solution.py:306
  7.2 24.6 %copy-start = (f32[1024,128]{1,0:T(8,128)S(1)}, f32[1024,128]{1,0:T(8,128)}, u32[]{:S(2)}) copy-start(f32[1024,128]{1,0:T(8,128)} %table_ref.1) | copy-start | bytes 1572868
  36.0 35.7 %copy-start.1 = (s32[16,312]{1,0:T(8,128)S(1)}, s32[16,312]{1,0:T(8,128)}, u32[]{:S(2)}) copy-start(s32[16,312]{1,0:T(8,128)} %get-tuple-element.26.src_ref) | copy-start | bytes 59908
  36.0 33.5 %all-to-all-start.1 = ((bf16[16,312,128]{2,1,0:T(8,128)(2,1)}), bf16[16,312,128]{2,1,0:T(8,128)(2,1)S(1)}, u32[]{:S(2)}, u32[]{:S(2)}) async-start(bf16[16,312,128]{2,1,0:T(8,128)(2,1)} %fetch.1), calls=%async_computation.1 | async-start | bytes 2555904 | tf_op jit(solution)/shard_map/all_to_all | solution.py:311
  71.7 7.6 %copy-start.6 = (f32[64,1664]{1,0:T(8,128)S(1)}, f32[64,1664]{1,0:T(8,128)}, u32[]{:S(2)}) copy-start(f32[64,1664]{1,0:T(8,128)} %feedback_ref.1) | copy-start | bytes 1277956
  71.7 7.6 %copy-start.7 = (bf16[256,128]{1,0:T(8,128)(2,1)S(1)}, bf16[256,128]{1,0:T(8,128)(2,1)}, u32[]{:S(2)}) copy-start(bf16[256,128]{1,0:T(8,128)(2,1)} %dense_ref.3) | copy-start | bytes 196612
  71.7 7.6 %copy-start.8 = (s32[312,16]{1,0:T(8,128)S(1)}, s32[312,16]{1,0:T(8,128)}, u32[]{:S(2)}) copy-start(s32[312,16]{1,0:T(8,128)} %get-tuple-element.31.src_t_ref) | copy-start | bytes 59908
  76.8 8.9 %copy-start.2 = (bf16[1792,512]{1,0:T(8,128)(2,1)}, bf16[1792,512]{1,0:T(8,128)(2,1)S(1)}, u32[]{:S(2)}) copy-start(bf16[1792,512]{1,0:T(8,128)(2,1)S(1)} %get-tuple-element.29.down_ref) | copy-start | bytes 5505028
  76.8 8.8 %copy-start.4 = (bf16[512,1792]{1,0:T(8,128)(2,1)}, bf16[512,1792]{1,0:T(8,128)(2,1)S(1)}, u32[]{:S(2)}) copy-start(bf16[512,1792]{1,0:T(8,128)(2,1)S(1)} %get-tuple-element.30.up_ref) | copy-start | bytes 5505028
  76.9 9.2 %collective-permute-start = (bf16[64,1664]{1,0:T(8,128)(2,1)S(1)}, bf16[64,1664]{1,0:T(8,128)(2,1)S(1)}, u32[]{:S(2)}, u32[]{:S(2)}) collective-permute-start(bf16[64,1664]{1,0:T(8,128)(2,1)S(1)} %get-tuple-element.34.pooled_ref.s0_ref), channel_id=1, source_target_pairs={{0,2},{2,0},{1,3},{3,1},{4,6},{6,4},{5,7},{7,5},{8,10},{10,8},{9,1... | collective-permute-start | bytes 638984 | tf_op jit(solution)/shard_map/ppermute | solution.py:270
  86.1 39.1 %all-to-all-start.2 = ((bf16[16,312,128]{2,1,0:T(8,128)(2,1)}), bf16[16,312,128]{2,1,0:T(8,128)(2,1)S(1)}, u32[]{:S(2)}, u32[]{:S(2)}) async-start(bf16[16,312,128]{2,1,0:T(8,128)(2,1)} %get-tuple-element.33), calls=%async_computation.2 | async-start | bytes 2555904 | tf_op jit(solution)/shard_map/all_to_all | solution.py:335
  95.0 55.4 %reduce-scatter.2.cloned.1.call-start = ((), (), s32[]{:S(2)}) async-start(), calls=%async_computation.6 | async-start | bytes 1179648 | tf_op jit(solution)/shard_map/reduce_scatter | solution.py:353
  95.1 5.2 %collective-permute-start.1 = (bf16[64,1664]{1,0:T(8,128)(2,1)S(1)}, bf16[64,1664]{1,0:T(8,128)(2,1)S(1)}, u32[]{:S(2)}, u32[]{:S(2)}) collective-permute-start(bf16[64,1664]{1,0:T(8,128)(2,1)S(1)} %get-tuple-element.34.pooled_ref.s0_ref), channel_id=1, source_target_pairs={{0,1},{1,0},{2,3},{3,2},{4,5},{5,4},{6,7},{7,6},{8,9},{9,8},{10,11... | collective-permute-start | bytes 638984 | tf_op jit(solution)/shard_map/ppermute | solution.py:270
  98.4 3.4 %collective-permute-start.2 = (bf16[64,1664]{1,0:T(8,128)(2,1)S(1)}, bf16[64,1664]{1,0:T(8,128)(2,1)S(1)}, u32[]{:S(2)}, u32[]{:S(2)}) collective-permute-start(bf16[64,1664]{1,0:T(8,128)(2,1)S(1)} %collective-permute-done.s2_ref), channel_id=1, source_target_pairs={{0,1},{1,0},{2,3},{3,2},{4,5},{5,4},{6,7},{7,6},{8,9},{9,8},{10,11... | collective-permute-start | bytes 638984 | tf_op jit(solution)/shard_map/ppermute | solution.py:270
  129.3 32.8 %all-to-all-start.3 = ((bf16[16,64,128]{2,1,0:T(8,128)(2,1)}), bf16[16,64,128]{2,1,0:T(8,128)(2,1)S(1)}, u32[]{:S(2)}, u32[]{:S(2)}) async-start(bf16[16,64,128]{2,1,0:T(8,128)(2,1)} %bitcast.9), calls=%async_computation.3 | async-start | bytes 524288 | tf_op jit(solution)/shard_map/all_to_all | solution.py:366
  151.3 8.4 %collective-permute-start.6 = (bf16[4,32,128]{2,1,0:T(8,128)(2,1)S(1)}, bf16[4,32,128]{2,1,0:T(8,128)(2,1)S(1)}, u32[]{:S(2)}, u32[]{:S(2)}) collective-permute-start(bf16[4,32,128]{2,1,0:T(8,128)(2,1)S(1)} %bitcast.48), channel_id=1, source_target_pairs={{0,288},{32,256},{64,352},{96,320},{128,416},{160,384},{192,480},{... | collective-permute-start | bytes 98312 | tf_op jit(solution)/shard_map/ppermute | solution.py:270
  155.5 4.7 %collective-permute-start.5 = (bf16[4,32,128]{2,1,0:T(8,128)(2,1)S(1)}, bf16[4,32,128]{2,1,0:T(8,128)(2,1)S(1)}, u32[]{:S(2)}, u32[]{:S(2)}) collective-permute-start(bf16[4,32,128]{2,1,0:T(8,128)(2,1)S(1)} %bitcast.47), channel_id=1, source_target_pairs={{0,256},{32,288},{64,320},{96,352},{128,384},{160,416},{192,448},{... | collective-permute-start | bytes 98312 | tf_op jit(solution)/shard_map/ppermute | solution.py:270
  157.4 4.7 %collective-permute-start.4 = (bf16[4,32,128]{2,1,0:T(8,128)(2,1)S(1)}, bf16[4,32,128]{2,1,0:T(8,128)(2,1)S(1)}, u32[]{:S(2)}, u32[]{:S(2)}) collective-permute-start(bf16[4,32,128]{2,1,0:T(8,128)(2,1)S(1)} %bitcast.46), channel_id=1, source_target_pairs={{0,32},{32,0},{64,96},{96,64},{128,160},{160,128},{192,224},{224,1... | collective-permute-start | bytes 98312 | tf_op jit(solution)/shard_map/ppermute | solution.py:270
  162.1 44.4 %copy-start.9 = (f32[1024,128]{1,0:T(8,128)S(1)}, f32[1024,128]{1,0:T(8,128)}, u32[]{:S(2)}) copy-start(f32[1024,128]{1,0:T(8,128)} %param.13) | copy-start | bytes 1572868
  162.2 6.3 %collective-permute-start.3 = (f32[64,128]{1,0:T(8,128)S(1)}, f32[64,128]{1,0:T(8,128)S(1)}, u32[]{:S(2)}, u32[]{:S(2)}) collective-permute-start(f32[64,128]{1,0:T(8,128)S(1)} %convert_reduce_fusion), channel_id=1, source_target_pairs={{0,2},{2,0},{1,3},{3,1},{4,6},{6,4},{5,7},{7,5},{8,10},{10,8},{9,1... | collective-permute-start | bytes 98312 | tf_op jit(solution)/shard_map/ppermute | solution.py:270
  169.2 25.4 %collective-permute-start.9 = (bf16[32,128]{1,0:T(8,128)(2,1)S(1)}, bf16[32,128]{1,0:T(8,128)(2,1)S(1)}, u32[]{:S(2)}, u32[]{:S(2)}) collective-permute-start(bf16[32,128]{1,0:T(8,128)(2,1)S(1)} %get-tuple-element.42), channel_id=1, source_target_pairs={{0,192},{32,224},{64,128},{96,160},{128,64},{160,96},{192,0},{224,... | collective-permute-start | bytes 24584 | tf_op jit(solution)/shard_map/ppermute | solution.py:270
  175.0 19.7 %collective-permute-start.8 = (bf16[32,128]{1,0:T(8,128)(2,1)S(1)}, bf16[32,128]{1,0:T(8,128)(2,1)S(1)}, u32[]{:S(2)}, u32[]{:S(2)}) collective-permute-start(bf16[32,128]{1,0:T(8,128)(2,1)S(1)} %get-tuple-element.41), channel_id=1, source_target_pairs={{0,128},{32,160},{64,192},{96,224},{128,0},{160,32},{192,64},{224,... | collective-permute-start | bytes 24584 | tf_op jit(solution)/shard_map/ppermute | solution.py:270
  179.1 15.6 %collective-permute-start.7 = (bf16[32,128]{1,0:T(8,128)(2,1)S(1)}, bf16[32,128]{1,0:T(8,128)(2,1)S(1)}, u32[]{:S(2)}, u32[]{:S(2)}) collective-permute-start(bf16[32,128]{1,0:T(8,128)(2,1)S(1)} %get-tuple-element.40), channel_id=1, source_target_pairs={{0,64},{32,96},{64,0},{96,32},{128,192},{160,224},{192,128},{224,1... | collective-permute-start | bytes 24584 | tf_op jit(solution)/shard_map/ppermute | solution.py:270
  181.0 25.4 %all-to-all-start.4 = ((bf16[16,64,128]{2,1,0:T(8,128)(2,1)}), bf16[16,64,128]{2,1,0:T(8,128)(2,1)S(1)}, u32[]{:S(2)}, u32[]{:S(2)}) async-start(bf16[16,64,128]{2,1,0:T(8,128)(2,1)} %bitcast.20), calls=%async_computation.5 | async-start | bytes 524288 | tf_op jit(solution)/shard_map/all_to_all | solution.py:378
  (5 other events, 14.7 us)
Sparse Core Ops, SparseCore 0:
  12.1 59.4 all-gather.2
  110.4 39.9 reduce-scatter.1

commit v7 on v6

--- a/solution.py
+++ b/solution.py
@@ -125,18 +125,13 @@
         out_ref[s] = dot(pick, table).astype(BF)
 
 
-def start_weights(pack_ref, down_ref, up_ref, sems):
-    moves = []
+def arrange(pack_ref, down_ref, up_ref):
     for k in range(TP):
-        block = pl.ds(k * RANK, RANK)
-        moves.append((pack_ref.at[k, pl.ds(0, DX), :], down_ref.at[:, block]))
+        block = slice(k * RANK, (k + 1) * RANK)
+        down_ref[:, block] = pack_ref[k, 0:DX, :]
         for j in range(BLOCKS):
-            lanes = pl.ds(j * E, E)
-            moves.append((pack_ref.at[k, pl.ds(DX + j * E, E), :], up_ref.at[block, lanes]))
-    moves = [pltpu.make_async_copy(a, b, sems.at[i]) for i, (a, b) in enumerate(moves)]
-    for move in moves:
-        move.start()
-    return moves
+            rows = slice(DX + j * E, DX + (j + 1) * E)
+            up_ref[block, j * E : (j + 1) * E] = pack_ref[k, rows, :]
 
 
 def forward(x, down, up, bias, head, labels):
@@ -150,8 +145,12 @@
     return hidden, crossed, xf, x_next, grad_logit, grad_next, grad_next * xf
 
 
-def pool_kernel(rows_ref, src_ref, pack_ref, pooled_ref, down_ref, up_ref, acc_ref, sems):
-    moves = start_weights(pack_ref, down_ref, up_ref, sems)
+def pool_kernel(rows_ref, src_ref, pack_hbm, pooled_ref, pack_ref, acc_ref, sems):
+    moves = [
+        pltpu.make_async_copy(pack_hbm.at[k], pack_ref.at[k], sems.at[k]) for k in range(TP)
+    ]
+    for move in moves:
+        move.start()
     bags = iota((BAGS, CAP), 0)
     for s in range(SHARDS):
         pick = jnp.where(bags == src_ref[s : s + 1, :], 1.0, 0.0).astype(BF)
@@ -167,9 +166,10 @@
 
 
 def main_kernel(
-    where_ref, pooled_ref, dense_ref, down_ref, up_ref, bias_ref, head_ref, label_ref, feedback_ref,
-    src_t_ref, carried_ref, send_ref,
+    where_ref, pooled_ref, dense_ref, pack_ref, bias_ref, head_ref, label_ref, feedback_ref,
+    src_t_ref, carried_ref, send_ref, down_ref, up_ref,
 ):
+    arrange(pack_ref, down_ref, up_ref)
     first = pl.multiple_of(where_ref[0] * N, N)
     x = jnp.concatenate([dense_ref[pl.ds(first, N), :], pooled_ref[...]], axis=1)
     up, bias, head = up_ref[...], bias_ref[...], head_ref[...]
@@ -190,9 +190,10 @@
 
 
 def grads_kernel(
-    where_ref, s0_ref, s1_ref, s2_ref, s3_ref, dense_ref, down_ref, up_ref, bias_ref, head_ref,
-    label_ref, out_ref, x_ref, hidden_ref, down_grad_ref, up_grad_ref,
+    where_ref, s0_ref, s1_ref, s2_ref, s3_ref, dense_ref, pack_ref, bias_ref, head_ref, label_ref,
+    out_ref, x_ref, hidden_ref, down_grad_ref, up_grad_ref, down_ref, up_ref,
 ):
+    arrange(pack_ref, down_ref, up_ref)
     t = where_ref[0]
     x_ref[:, 0:E] = dense_ref[...]
     for m, ref in enumerate((s0_ref, s1_ref, s2_ref, s3_ref)):
@@ -309,14 +310,14 @@
         fetch_kernel, [sds((SHARDS, CAP, E), BF)], (ids, emb_table), "fetch", flops=1_300_000_000
     )
     returned = lax.all_to_all(fetched, EMB, split_axis=0, concat_axis=0, tiled=True)
-    pooled, down_all, up_all = call(
+    pooled, weights = call(
         pool_kernel,
-        [sds((N, POOL), BF), sds((DX, TP * RANK), BF), sds((TP * RANK, DX), BF)],
+        [sds((N, POOL), BF), sds((TP, 2 * DX, E), BF)],
         (returned, src, pack_all),
         "pool",
         scratch=[
             pltpu.VMEM((BAGS, E), F32),
-            pltpu.SemaphoreType.DMA((TP * (1 + BLOCKS),)),
+            pltpu.SemaphoreType.DMA((TP,)),
         ],
         flops=1_060_000_000,
         limit=47,
@@ -326,8 +327,9 @@
     carried, send = call(
         main_kernel,
         (sds((N, POOL), F32), sds((SHARDS, CAP, E), BF)),
-        (where, pooled, dense_input, down_all, up_all, bias, head, label, feedback, src_t),
+        (where, pooled, dense_input, weights, bias, head, label, feedback, src_t),
         "main",
+        scratch=[pltpu.VMEM((DX, TP * RANK), BF), pltpu.VMEM((TP * RANK, DX), BF)],
         flops=10_000_000_000,
         limit=40,
     )
@@ -338,13 +340,15 @@
     (part,) = call(
         grads_kernel,
         [sds((DP, SHARDS, CHUNK, E), BF)],
-        (where, pooled, near, far, far_near, dense_input, down_all, up_all, bias, head, label),
+        (where, pooled, near, far, far_near, dense_input, weights, bias, head, label),
         "grads",
         scratch=[
             pltpu.VMEM((DENSE, DX), BF),
             pltpu.VMEM((TP, DENSE, RANK), BF),
             pltpu.VMEM((DX, RANK), BF),
             pltpu.VMEM((DX, RANK), BF),
+            pltpu.VMEM((DX, TP * RANK), BF),
+            pltpu.VMEM((TP * RANK, DX), BF),
         ],
         flops=2_000_000_000,
         limit=40,
@@ -366,17 +370,18 @@
     by_y = lax.all_to_all(row_grad, owners, split_axis=0, concat_axis=0, tiled=True)
     mine = jnp.sum(by_y.reshape(pieces, ROWS // pieces, E).astype(F32), axis=0)
     mine = (mine + partner(mine, "xh", 1)).astype(BF)
+    spread = jnp.broadcast_to(mine[None], (pieces, ROWS // pieces, E)).reshape(ROWS, E)
+    spread, over_y = lax.optimization_barrier((spread, over_y))
+    full = lax.all_to_all(spread, owners, split_axis=0, concat_axis=0, tiled=True)
     over_y = over_y.reshape(SHARDS, CHUNK, E)
     pairs = [over_y[0:4].astype(F32)] + [
         partner(over_y[4 * c : 4 * c + 4], EMB, mask).astype(F32)
         for c, mask in ((1, 1), (2, 8), (3, 9))
     ]
     pairs = (pairs[0] + pairs[1]) + (pairs[2] + pairs[3])
-    spread = jnp.broadcast_to(mine[None], (pieces, ROWS // pieces, E)).reshape(ROWS, E)
-    last = [pairs[0]] + [pairs[i].astype(BF) for i in (1, 2, 3)]
-    spread, *last = lax.optimization_barrier((spread, *last))
-    full = lax.all_to_all(spread, owners, split_axis=0, concat_axis=0, tiled=True)
-    last = [last[0]] + [partner(last[i], EMB, 2 * i).astype(F32) for i in (1, 2, 3)]
+    last = [pairs[0]] + [
+        partner(pairs[i].astype(BF), EMB, 2 * i).astype(F32) for i in (1, 2, 3)
+    ]
     grads = (last[0] + last[1]) + (last[2] + last[3])
     full = full.astype(F32)
     accum_new = row_accum + full * full

time: 215 us -> 207 us (0.963)
  blocking collectives: 19 us -> 41.7 us
  starting transfers between devices: 68.3 us -> 51.1 us
  waiting for transfers between devices: 74.3 us -> 63.9 us
  Pallas kernels: 30.2 us -> 27.7 us
    all_to_all x0 -> x1, blocking collectives: none -> 22.6 us  [local(): lax.all_to_all(row_grad, owners, split_axis=0, concat_axis=0, tiled=True)]
    reduce_scatter x1, waiting for transfers between devices: 11.8 us -> 0.02 us  [local(): lax.psum_scatter(part.reshape(DP * SHARDS * CHUNK, E), 'y', scatter_dimen...]
    all_to_all x1 -> x0, starting transfers between devices: 9.39 us -> none  [local(): lax.all_to_all(row_grad, owners, split_axis=0, concat_axis=0, tiled=True)]
    all_to_all x1, starting transfers between devices: 13.7 us -> 6.66 us  [local(): lax.all_to_all(spread, owners, split_axis=0, concat_axis=0, tiled=True)]
    pallas_call x6, Pallas kernels: 30.2 us -> 27.7 us  [call(): pl.pallas_call(kernel, out_shape=outs, in_specs=[SMEM if x.size < 8 else...]
  transfers between devices with their start and end apart: 16 -> 15, of which waited for: 10 -> 7; matrix products, arithmetic and copies ran while one was open for 1% -> 1% of each run, Pallas kernels for 9% -> 10%
where the time goes in v7:
time: 207 us; the launch traced here: 206 us
  waiting for transfers between devices  63.9 us (31%)
  starting transfers between devices  51.1 us (25%)
  blocking collectives  41.7 us (20%)
  Pallas kernels  27.7 us (13%)
  between operations  14.4 us (7%)
  local copies, waits for them, and re-layouts  5.81 us (3%)
    ppermute x10, starting transfers between devices, partner(): return lax.ppermute(value, axes, [(i, i ^ mask) for i in range(size)])  31.4 us
    all_to_all x1, waiting for transfers between devices, local(): lax.all_to_all(fetched, EMB, split_axis=0, concat_axis=0, tiled=True)  29.3 us
    pallas_call x6, Pallas kernels, call(): pl.pallas_call(kernel, out_shape=outs, in_specs=[SMEM if x.size < 8 else...  27.7 us
    all_to_all x1, blocking collectives, local(): lax.all_to_all(row_grad, owners, split_axis=0, concat_axis=0, tiled=True)  22.6 us
    all_to_all x1, blocking collectives, local(): ids = lax.all_to_all(ids, EMB, split_axis=0, concat_axis=0, tiled=True)  19 us
    all_to_all x1, waiting for transfers between devices, local(): arrived = lax.all_to_all(send, EMB, split_axis=0, concat_axis=0, tiled=True)  15.8 us
    all_to_all x1, waiting for transfers between devices, local(): lax.all_to_all(spread, owners, split_axis=0, concat_axis=0, tiled=True)  10.5 us
    all_to_all x1, starting transfers between devices, local(): arrived = lax.all_to_all(send, EMB, split_axis=0, concat_axis=0, tiled=True)  9.07 us
  transfers between devices with their start and end apart: 15, of which 7 were waited for; matrix products, arithmetic and copies ran while one was open for 1% of the time, Pallas kernels for 10%

profile of v7, /device:TPU:1, one launch (start us, length us, event | category | flops | bytes accessed | tf_op | source)
XLA Modules:
  0.0 205.8 jit_solution(2333709880543252173)
XLA Ops:
  7.2 4.8 %index.1 = (s32[16,312]{1,0:T(8,128)}, s32[16,312]{1,0:T(8,128)}, s32[312,16]{1,0:T(8,128)}, bf16[3584,128]{1,0:T(8,128)(2,1)}) custom-call(s32[52,1,64]{2,1,0:T(1,128)} %bitcast.57, s32[52,64]{1,0:T(8,128)} %bitcast.56, s32[13,64]{1,0:T(8,128)} %bitcast.58, bf16[1792,128]{1,0:T(8,128)(2,1)} %down_hbm.1, bf16[128,1792]{1,0:T(8,128)(2,1)} %up_hbm.1), custom_call_target="tpu_custom_call" | custom-call | flops 400000000 | bytes 947456 | tf_op jit(solution)/shard_map/index/pallas_call | solution.py:48
  12.8 19.0 %all_to_all.39 = s32[16,1,312]{2,1,0:T(1,128)S(1)} all-to-all(s32[16,1,312]{2,1,0:T(1,128)S(1)} %copy.21), channel_id=1, replica_groups=mesh['xl'=2,'z'=8,'y'=8,'xh'=2,'core'=2] {'xl','z'}, dimensions={0} | all-to-all | bytes 39936 | tf_op jit(solution)/shard_map/all_to_all | solution.py:308
  31.8 4.1 %fetch.1 = bf16[16,312,128]{2,1,0:T(8,128)(2,1)} custom-call(s32[16,312]{1,0:T(8,128)S(1)} %bitcast.47, f32[1024,128]{1,0:T(8,128)S(1)} %copy-done), custom_call_target="tpu_custom_call" | custom-call | flops 1300000000 | bytes 544256 | tf_op jit(solution)/shard_map/fetch/pallas_call | solution.py:48
  36.0 3.8 %all-to-all-start.1 = ((bf16[16,312,128]{2,1,0:T(8,128)(2,1)}), bf16[16,312,128]{2,1,0:T(8,128)(2,1)S(1)}, u32[]{:S(2)}, u32[]{:S(2)}) async-start(bf16[16,312,128]{2,1,0:T(8,128)(2,1)} %fetch.1), calls=%async_computation.1 | async-start | bytes 2555904 | tf_op jit(solution)/shard_map/all_to_all | solution.py:312
  40.1 29.3 %all-to-all-done.1.rows_ref = bf16[16,312,128]{2,1,0:T(8,128)(2,1)S(1)} async-done(((bf16[16,312,128]{2,1,0:T(8,128)(2,1)}), bf16[16,312,128]{2,1,0:T(8,128)(2,1)S(1)}, u32[]{:S(2)}, u32[]{:S(2)}) %all-to-all-start.1) | async-done | bytes 1277984 | tf_op jit(solution)/shard_map/all_to_all | solution.py:312
  69.5 2.2 %all-gather.3.cloned.1.call-done = bf16[14336,128]{1,0:T(8,128)(2,1)} async-done(((bf16[3584,128]{1,0:T(8,128)(2,1)}), bf16[14336,128]{1,0:T(8,128)(2,1)}) %all-gather.3.cloned.1.call-update) | async-done | bytes 3670032 | tf_op jit(solution)/shard_map/gather_weights/all_gather | solution.py:307
  71.7 2.9 %pool.1 = (bf16[64,1664]{1,0:T(8,128)(2,1)S(1)}, bf16[4,3584,128]{2,1,0:T(8,128)(2,1)S(1)}) custom-call(bf16[16,312,128]{2,1,0:T(8,128)(2,1)S(1)} %all-to-all-done.1.rows_ref, s32[16,312]{1,0:T(8,128)S(1)} %copy-done.1, bf16[4,3584,128]{2,1,0:T(8,128)(2,1)} %bitcast.49), custom_call_target="tpu_custom_call" | custom-call | flops 1060000000 | bytes 4967936 | tf_op jit(solution)/shard_map/pool/pallas_call | solution.py:48
  74.5 2.4 %collective-permute-start = (bf16[64,1664]{1,0:T(8,128)(2,1)S(1)}, bf16[64,1664]{1,0:T(8,128)(2,1)S(1)}, u32[]{:S(2)}, u32[]{:S(2)}) collective-permute-start(bf16[64,1664]{1,0:T(8,128)(2,1)S(1)} %get-tuple-element.29.pooled_ref.s0_ref), channel_id=1, source_target_pairs={{0,2},{2,0},{1,3},{3,1},{4,6},{6,4},{5,7},{7,5},{8,10},{10,8},{9,1... | collective-permute-start | bytes 638984 | tf_op jit(solution)/shard_map/ppermute | solution.py:271
  76.9 6.8 %main.1 = (f32[64,1664]{1,0:T(8,128)}, bf16[16,312,128]{2,1,0:T(8,128)(2,1)}) custom-call(s32[3]{0:T(128)S(1)} %pad_add_fusion.where_ref, bf16[64,1664]{1,0:T(8,128)(2,1)S(1)} %get-tuple-element.29.pooled_ref.s0_ref, bf16[256,128]{1,0:T(8,128)(2,1)S(1)} %copy-done.5, bf16[4,3584,128]{2,1,0:T(8,128)(2,1)S(1)} %get-tuple-element.25.pack_ref, ...), custom_call_target="tpu_custom_call" | custom-call | flops 10000000000 | bytes 4409868 | tf_op jit(solution)/shard_map/main/pallas_call | solution.py:48
  83.7 9.1 %all-to-all-start.2 = ((bf16[16,312,128]{2,1,0:T(8,128)(2,1)}), bf16[16,312,128]{2,1,0:T(8,128)(2,1)S(1)}, u32[]{:S(2)}, u32[]{:S(2)}) async-start(bf16[16,312,128]{2,1,0:T(8,128)(2,1)} %get-tuple-element.28), calls=%async_computation.2 | async-start | bytes 2555904 | tf_op jit(solution)/shard_map/all_to_all | solution.py:337
  92.9 3.2 %collective-permute-start.1 = (bf16[64,1664]{1,0:T(8,128)(2,1)S(1)}, bf16[64,1664]{1,0:T(8,128)(2,1)S(1)}, u32[]{:S(2)}, u32[]{:S(2)}) collective-permute-start(bf16[64,1664]{1,0:T(8,128)(2,1)S(1)} %get-tuple-element.29.pooled_ref.s0_ref), channel_id=1, source_target_pairs={{0,1},{1,0},{2,3},{3,2},{4,5},{5,4},{6,7},{7,6},{8,9},{9,8},{10,11... | collective-permute-start | bytes 638984 | tf_op jit(solution)/shard_map/ppermute | solution.py:271
  101.5 5.7 %grads.1 = bf16[8,16,32,128]{3,2,1,0:T(8,128)(2,1)} custom-call(s32[3]{0:T(128)S(1)} %pad_add_fusion.where_ref, bf16[64,1664]{1,0:T(8,128)(2,1)S(1)} %get-tuple-element.29.pooled_ref.s0_ref, bf16[64,1664]{1,0:T(8,128)(2,1)S(1)} %collective-permute-done.1.s1_ref, bf16[64,1664]{1,0:T(8,128)(2,1)S(1)} %collective-permute-done.s2_ref, ...), custom_call_target="tpu_custom_call" | custom-call | flops 2000000000 | bytes 4602892 | tf_op jit(solution)/shard_map/grads/pallas_call | solution.py:48
  107.2 15.8 %all-to-all-done.2.rows_ref = bf16[16,312,128]{2,1,0:T(8,128)(2,1)S(1)} async-done(((bf16[16,312,128]{2,1,0:T(8,128)(2,1)}), bf16[16,312,128]{2,1,0:T(8,128)(2,1)S(1)}, u32[]{:S(2)}, u32[]{:S(2)}) %all-to-all-start.2) | async-done | bytes 1277984 | tf_op jit(solution)/shard_map/all_to_all | solution.py:337
  123.0 3.4 %scatter.1 = bf16[1024,128]{1,0:T(8,128)(2,1)S(1)} custom-call(s32[16,312]{1,0:T(8,128)S(1)} %bitcast.48, bf16[16,312,128]{2,1,0:T(8,128)(2,1)S(1)} %all-to-all-done.2.rows_ref), custom_call_target="tpu_custom_call" | custom-call | flops 1300000000 | bytes 1297920 | tf_op jit(solution)/shard_map/scatter/pallas_call | solution.py:48
  126.4 22.6 %all_to_all.40 = bf16[16,64,128]{2,1,0:T(8,128)(2,1)S(1)} all-to-all(bf16[16,64,128]{2,1,0:T(8,128)(2,1)S(1)} %bitcast.46), channel_id=1, replica_groups=mesh['xl'=2,'z'=8,'y'=8,'xh'=2,'core'=2] {'y','core'}, dimensions={0} | all-to-all | bytes 524288 | tf_op jit(solution)/shard_map/all_to_all | solution.py:370
  149.1 4.2 %collective-permute-start.3 = (f32[64,128]{1,0:T(8,128)S(1)}, f32[64,128]{1,0:T(8,128)S(1)}, u32[]{:S(2)}, u32[]{:S(2)}) collective-permute-start(f32[64,128]{1,0:T(8,128)S(1)} %convert_reduce_fusion), channel_id=1, source_target_pairs={{0,2},{2,0},{1,3},{3,1},{4,6},{6,4},{5,7},{7,5},{8,10},{10,8},{9,1... | collective-permute-start | bytes 98312 | tf_op jit(solution)/shard_map/ppermute | solution.py:271
  156.9 3.6 %collective-permute-start.6 = (bf16[4,32,128]{2,1,0:T(8,128)(2,1)S(1)}, bf16[4,32,128]{2,1,0:T(8,128)(2,1)S(1)}, u32[]{:S(2)}, u32[]{:S(2)}) collective-permute-start(bf16[4,32,128]{2,1,0:T(8,128)(2,1)S(1)} %bitcast.53), channel_id=1, source_target_pairs={{0,288},{32,256},{64,352},{96,320},{128,416},{160,384},{192,480},{... | collective-permute-start | bytes 98312 | tf_op jit(solution)/shard_map/ppermute | solution.py:271
  160.6 2.7 %collective-permute-start.5 = (bf16[4,32,128]{2,1,0:T(8,128)(2,1)S(1)}, bf16[4,32,128]{2,1,0:T(8,128)(2,1)S(1)}, u32[]{:S(2)}, u32[]{:S(2)}) collective-permute-start(bf16[4,32,128]{2,1,0:T(8,128)(2,1)S(1)} %bitcast.52), channel_id=1, source_target_pairs={{0,256},{32,288},{64,320},{96,352},{128,384},{160,416},{192,448},{... | collective-permute-start | bytes 98312 | tf_op jit(solution)/shard_map/ppermute | solution.py:271
  165.4 2.6 %collective-permute-done.4 = bf16[4,32,128]{2,1,0:T(8,128)(2,1)S(1)} collective-permute-done((bf16[4,32,128]{2,1,0:T(8,128)(2,1)S(1)}, bf16[4,32,128]{2,1,0:T(8,128)(2,1)S(1)}, u32[]{:S(2)}, u32[]{:S(2)}) %collective-permute-start.4) | collective-permute-done | bytes 32800 | tf_op jit(solution)/shard_map/ppermute | solution.py:271
  168.0 2.5 %collective-permute-start.9 = (bf16[32,128]{1,0:T(8,128)(2,1)S(1)}, bf16[32,128]{1,0:T(8,128)(2,1)S(1)}, u32[]{:S(2)}, u32[]{:S(2)}) collective-permute-start(bf16[32,128]{1,0:T(8,128)(2,1)S(1)} %get-tuple-element.46), channel_id=1, source_target_pairs={{0,192},{32,224},{64,128},{96,160},{128,64},{160,96},{192,0},{224,... | collective-permute-start | bytes 24584 | tf_op jit(solution)/shard_map/ppermute | solution.py:271
  170.5 5.8 %collective-permute-start.8 = (bf16[32,128]{1,0:T(8,128)(2,1)S(1)}, bf16[32,128]{1,0:T(8,128)(2,1)S(1)}, u32[]{:S(2)}, u32[]{:S(2)}) collective-permute-start(bf16[32,128]{1,0:T(8,128)(2,1)S(1)} %get-tuple-element.47), channel_id=1, source_target_pairs={{0,128},{32,160},{64,192},{96,224},{128,0},{160,32},{192,64},{224,... | collective-permute-start | bytes 24584 | tf_op jit(solution)/shard_map/ppermute | solution.py:271
  176.3 3.1 %collective-permute-start.7 = (bf16[32,128]{1,0:T(8,128)(2,1)S(1)}, bf16[32,128]{1,0:T(8,128)(2,1)S(1)}, u32[]{:S(2)}, u32[]{:S(2)}) collective-permute-start(bf16[32,128]{1,0:T(8,128)(2,1)S(1)} %get-tuple-element.45), channel_id=1, source_target_pairs={{0,64},{32,96},{64,0},{96,32},{128,192},{160,224},{192,128},{224,1... | collective-permute-start | bytes 24584 | tf_op jit(solution)/shard_map/ppermute | solution.py:271
  179.4 6.7 %all-to-all-start.4 = ((bf16[16,64,128]{2,1,0:T(8,128)(2,1)}), bf16[16,64,128]{2,1,0:T(8,128)(2,1)S(1)}, u32[]{:S(2)}, u32[]{:S(2)}) async-start(bf16[16,64,128]{2,1,0:T(8,128)(2,1)} %bitcast.12), calls=%async_computation.5 | async-start | bytes 524288 | tf_op jit(solution)/shard_map/all_to_all | solution.py:375
  187.3 10.5 %all-to-all-done.4 = bf16[16,64,128]{2,1,0:T(8,128)(2,1)S(1)} async-done(((bf16[16,64,128]{2,1,0:T(8,128)(2,1)}), bf16[16,64,128]{2,1,0:T(8,128)(2,1)S(1)}, u32[]{:S(2)}, u32[]{:S(2)}) %all-to-all-start.4) | async-done | bytes 262176 | tf_op jit(solution)/shard_map/all_to_all | solution.py:375
  (55 shorter events, 14.7 us)
Async XLA Ops:
  7.2 64.5 %all-gather.3.cloned.1.call-start = ((), (), s32[]{:S(2)}) async-start(), calls=%async_computation.7 | async-start | bytes 4587520 | tf_op jit(solution)/shard_map/gather_weights/all_gather | solution.py:307
  7.2 24.6 %copy-start = (f32[1024,128]{1,0:T(8,128)S(1)}, f32[1024,128]{1,0:T(8,128)}, u32[]{:S(2)}) copy-start(f32[1024,128]{1,0:T(8,128)} %table_ref.1) | copy-start | bytes 1572868
  36.0 3.9 %copy-start.9 = (f32[1792]{0:T(1024)S(1)}, f32[1792]{0:T(1024)}, u32[]{:S(2)}) copy-start(f32[1792]{0:T(1024)} %param.23) | copy-start | bytes 21508
  36.0 3.9 %copy-start.10 = (s32[256]{0:T(256)S(1)}, s32[256]{0:T(256)}, u32[]{:S(2)}) copy-start(s32[256]{0:T(256)} %param.18) | copy-start | bytes 3076
  36.0 35.7 %copy-start.1 = (s32[16,312]{1,0:T(8,128)S(1)}, s32[16,312]{1,0:T(8,128)}, u32[]{:S(2)}) copy-start(s32[16,312]{1,0:T(8,128)} %get-tuple-element.22.src_ref) | copy-start | bytes 59908
  36.0 33.5 %all-to-all-start.1 = ((bf16[16,312,128]{2,1,0:T(8,128)(2,1)}), bf16[16,312,128]{2,1,0:T(8,128)(2,1)S(1)}, u32[]{:S(2)}, u32[]{:S(2)}) async-start(bf16[16,312,128]{2,1,0:T(8,128)(2,1)} %fetch.1), calls=%async_computation.1 | async-start | bytes 2555904 | tf_op jit(solution)/shard_map/all_to_all | solution.py:312
  71.7 5.2 %copy-start.4 = (f32[64,1664]{1,0:T(8,128)S(1)}, f32[64,1664]{1,0:T(8,128)}, u32[]{:S(2)}) copy-start(f32[64,1664]{1,0:T(8,128)} %feedback_ref.1) | copy-start | bytes 1277956
  71.7 5.3 %copy-start.5 = (bf16[256,128]{1,0:T(8,128)(2,1)S(1)}, bf16[256,128]{1,0:T(8,128)(2,1)}, u32[]{:S(2)}) copy-start(bf16[256,128]{1,0:T(8,128)(2,1)} %dense_ref.3) | copy-start | bytes 196612
  71.7 5.3 %copy-start.6 = (s32[312,16]{1,0:T(8,128)S(1)}, s32[312,16]{1,0:T(8,128)}, u32[]{:S(2)}) copy-start(s32[312,16]{1,0:T(8,128)} %get-tuple-element.26.src_t_ref) | copy-start | bytes 59908
  74.5 9.2 %copy-start.2 = (bf16[4,3584,128]{2,1,0:T(8,128)(2,1)}, bf16[4,3584,128]{2,1,0:T(8,128)(2,1)S(1)}, u32[]{:S(2)}) copy-start(bf16[4,3584,128]{2,1,0:T(8,128)(2,1)S(1)} %get-tuple-element.25.pack_ref) | copy-start | bytes 11010052
  74.5 9.2 %collective-permute-start = (bf16[64,1664]{1,0:T(8,128)(2,1)S(1)}, bf16[64,1664]{1,0:T(8,128)(2,1)S(1)}, u32[]{:S(2)}, u32[]{:S(2)}) collective-permute-start(bf16[64,1664]{1,0:T(8,128)(2,1)S(1)} %get-tuple-element.29.pooled_ref.s0_ref), channel_id=1, source_target_pairs={{0,2},{2,0},{1,3},{3,1},{4,6},{6,4},{5,7},{7,5},{8,10},{10,8},{9,1... | collective-permute-start | bytes 638984 | tf_op jit(solution)/shard_map/ppermute | solution.py:271
  83.7 39.2 %all-to-all-start.2 = ((bf16[16,312,128]{2,1,0:T(8,128)(2,1)}), bf16[16,312,128]{2,1,0:T(8,128)(2,1)S(1)}, u32[]{:S(2)}, u32[]{:S(2)}) async-start(bf16[16,312,128]{2,1,0:T(8,128)(2,1)} %get-tuple-element.28), calls=%async_computation.2 | async-start | bytes 2555904 | tf_op jit(solution)/shard_map/all_to_all | solution.py:337
  92.8 62.5 %reduce-scatter.2.cloned.1.call-start = ((), (), s32[]{:S(2)}) async-start(), calls=%async_computation.6 | async-start | bytes 1179648 | tf_op jit(solution)/shard_map/reduce_scatter | solution.py:357
  92.9 5.1 %collective-permute-start.1 = (bf16[64,1664]{1,0:T(8,128)(2,1)S(1)}, bf16[64,1664]{1,0:T(8,128)(2,1)S(1)}, u32[]{:S(2)}, u32[]{:S(2)}) collective-permute-start(bf16[64,1664]{1,0:T(8,128)(2,1)S(1)} %get-tuple-element.29.pooled_ref.s0_ref), channel_id=1, source_target_pairs={{0,1},{1,0},{2,3},{3,2},{4,5},{5,4},{6,7},{7,6},{8,9},{9,8},{10,11... | collective-permute-start | bytes 638984 | tf_op jit(solution)/shard_map/ppermute | solution.py:271
  96.1 3.4 %collective-permute-start.2 = (bf16[64,1664]{1,0:T(8,128)(2,1)S(1)}, bf16[64,1664]{1,0:T(8,128)(2,1)S(1)}, u32[]{:S(2)}, u32[]{:S(2)}) collective-permute-start(bf16[64,1664]{1,0:T(8,128)(2,1)S(1)} %collective-permute-done.s2_ref), channel_id=1, source_target_pairs={{0,1},{1,0},{2,3},{3,2},{4,5},{5,4},{6,7},{7,6},{8,9},{9,8},{10,11... | collective-permute-start | bytes 638984 | tf_op jit(solution)/shard_map/ppermute | solution.py:271
  149.1 6.2 %collective-permute-start.3 = (f32[64,128]{1,0:T(8,128)S(1)}, f32[64,128]{1,0:T(8,128)S(1)}, u32[]{:S(2)}, u32[]{:S(2)}) collective-permute-start(f32[64,128]{1,0:T(8,128)S(1)} %convert_reduce_fusion), channel_id=1, source_target_pairs={{0,2},{2,0},{1,3},{3,1},{4,6},{6,4},{5,7},{7,5},{8,10},{10,8},{9,1... | collective-permute-start | bytes 98312 | tf_op jit(solution)/shard_map/ppermute | solution.py:271
  156.1 41.8 %copy-start.7 = (f32[1024,128]{1,0:T(8,128)S(1)}, f32[1024,128]{1,0:T(8,128)}, u32[]{:S(2)}) copy-start(f32[1024,128]{1,0:T(8,128)} %param.13) | copy-start | bytes 1572868
  156.9 8.4 %collective-permute-start.6 = (bf16[4,32,128]{2,1,0:T(8,128)(2,1)S(1)}, bf16[4,32,128]{2,1,0:T(8,128)(2,1)S(1)}, u32[]{:S(2)}, u32[]{:S(2)}) collective-permute-start(bf16[4,32,128]{2,1,0:T(8,128)(2,1)S(1)} %bitcast.53), channel_id=1, source_target_pairs={{0,288},{32,256},{64,352},{96,320},{128,416},{160,384},{192,480},{... | collective-permute-start | bytes 98312 | tf_op jit(solution)/shard_map/ppermute | solution.py:271
  160.6 4.8 %collective-permute-start.5 = (bf16[4,32,128]{2,1,0:T(8,128)(2,1)S(1)}, bf16[4,32,128]{2,1,0:T(8,128)(2,1)S(1)}, u32[]{:S(2)}, u32[]{:S(2)}) collective-permute-start(bf16[4,32,128]{2,1,0:T(8,128)(2,1)S(1)} %bitcast.52), channel_id=1, source_target_pairs={{0,256},{32,288},{64,320},{96,352},{128,384},{160,416},{192,448},{... | collective-permute-start | bytes 98312 | tf_op jit(solution)/shard_map/ppermute | solution.py:271
  163.3 4.7 %collective-permute-start.4 = (bf16[4,32,128]{2,1,0:T(8,128)(2,1)S(1)}, bf16[4,32,128]{2,1,0:T(8,128)(2,1)S(1)}, u32[]{:S(2)}, u32[]{:S(2)}) collective-permute-start(bf16[4,32,128]{2,1,0:T(8,128)(2,1)S(1)} %bitcast.51), channel_id=1, source_target_pairs={{0,32},{32,0},{64,96},{96,64},{128,160},{160,128},{192,224},{224,1... | collective-permute-start | bytes 98312 | tf_op jit(solution)/shard_map/ppermute | solution.py:271
  168.0 18.1 %collective-permute-start.9 = (bf16[32,128]{1,0:T(8,128)(2,1)S(1)}, bf16[32,128]{1,0:T(8,128)(2,1)S(1)}, u32[]{:S(2)}, u32[]{:S(2)}) collective-permute-start(bf16[32,128]{1,0:T(8,128)(2,1)S(1)} %get-tuple-element.46), channel_id=1, source_target_pairs={{0,192},{32,224},{64,128},{96,160},{128,64},{160,96},{192,0},{224,... | collective-permute-start | bytes 24584 | tf_op jit(solution)/shard_map/ppermute | solution.py:271
  170.5 15.6 %collective-permute-start.8 = (bf16[32,128]{1,0:T(8,128)(2,1)S(1)}, bf16[32,128]{1,0:T(8,128)(2,1)S(1)}, u32[]{:S(2)}, u32[]{:S(2)}) collective-permute-start(bf16[32,128]{1,0:T(8,128)(2,1)S(1)} %get-tuple-element.47), channel_id=1, source_target_pairs={{0,128},{32,160},{64,192},{96,224},{128,0},{160,32},{192,64},{224,... | collective-permute-start | bytes 24584 | tf_op jit(solution)/shard_map/ppermute | solution.py:271
  176.3 9.8 %collective-permute-start.7 = (bf16[32,128]{1,0:T(8,128)(2,1)S(1)}, bf16[32,128]{1,0:T(8,128)(2,1)S(1)}, u32[]{:S(2)}, u32[]{:S(2)}) collective-permute-start(bf16[32,128]{1,0:T(8,128)(2,1)S(1)} %get-tuple-element.45), channel_id=1, source_target_pairs={{0,64},{32,96},{64,0},{96,32},{128,192},{160,224},{192,128},{224,1... | collective-permute-start | bytes 24584 | tf_op jit(solution)/shard_map/ppermute | solution.py:271
  179.4 18.4 %all-to-all-start.4 = ((bf16[16,64,128]{2,1,0:T(8,128)(2,1)}), bf16[16,64,128]{2,1,0:T(8,128)(2,1)S(1)}, u32[]{:S(2)}, u32[]{:S(2)}) async-start(bf16[16,64,128]{2,1,0:T(8,128)(2,1)} %bitcast.12), calls=%async_computation.5 | async-start | bytes 524288 | tf_op jit(solution)/shard_map/all_to_all | solution.py:375
  (2 other events, 5.9 us)
Sparse Core Ops, SparseCore 0:
  12.1 59.4 all-gather.2
  107.3 40.0 reduce-scatter.1

commit v8 on v7

--- a/solution.py
+++ b/solution.py
@@ -26,6 +26,7 @@
 CHUNK = 32
 BLOCKS = DX // E
 BAGS = N * F
+QUAD = 4
 LEARN = 0.5
 EMB = ("xl", "z")
 TPA = ("xh", "core")
@@ -145,15 +146,20 @@
     return hidden, crossed, xf, x_next, grad_logit, grad_next, grad_next * xf
 
 
+def quad_row(ref, s):
+    parts = [ref[k : k + 1, :].astype(F32) for k in range(QUAD * s, QUAD * (s + 1))]
+    return jnp.concatenate(parts, axis=1).astype(I32)
+
+
 def pool_kernel(rows_ref, src_ref, pack_hbm, pooled_ref, pack_ref, acc_ref, sems):
     moves = [
         pltpu.make_async_copy(pack_hbm.at[k], pack_ref.at[k], sems.at[k]) for k in range(TP)
     ]
     for move in moves:
         move.start()
-    bags = iota((BAGS, CAP), 0)
-    for s in range(SHARDS):
-        pick = jnp.where(bags == src_ref[s : s + 1, :], 1.0, 0.0).astype(BF)
+    bags = iota((BAGS, QUAD * CAP), 0)
+    for s in range(SHARDS // QUAD):
+        pick = jnp.where(bags == quad_row(src_ref, s), 1.0, 0.0).astype(BF)
         term = dot(pick, rows_ref[s])
         if s == 0:
             acc_ref[...] = term
@@ -248,16 +254,14 @@
             axis=0,
         )
         got = dot(select, block_rows).astype(BF)
-        w = where_ref[2] ^ e
-        place = ((w >> 3) & 1) * 8 + (w & 1) * 4 + ((w >> 1) & 3)
         for k in range(DP):
-            out_ref[k, place] = got[CHUNK * k : CHUNK * (k + 1)]
+            out_ref[k, e] = got[CHUNK * k : CHUNK * (k + 1)]
 
 
 def scatter_kernel(ids_ref, rows_ref, out_ref, acc_ref):
-    rows = iota((ROWS, CAP), 0)
-    for s in range(SHARDS):
-        pick = jnp.where(rows == ids_ref[s : s + 1, :], 1.0, 0.0).astype(BF)
+    rows = iota((ROWS, QUAD * CAP), 0)
+    for s in range(SHARDS // QUAD):
+        pick = jnp.where(rows == quad_row(ids_ref, s), 1.0, 0.0).astype(BF)
         term = dot(pick, rows_ref[s])
         if s == 0:
             acc_ref[...] = term
@@ -281,7 +285,7 @@
 ):
     bias, head = cross_bias.reshape(1, DX), head_weight.reshape(1, DX)
     label = labels.reshape(DENSE, 1)
-    where = jnp.stack([lax.axis_index(TPA), lax.axis_index("y"), lax.axis_index(EMB)]).astype(I32)
+    where = jnp.stack([lax.axis_index(TPA), lax.axis_index("y")]).astype(I32)
     ids, src, src_t, pack = call(
         index_kernel,
         (
@@ -313,7 +317,7 @@
     pooled, weights = call(
         pool_kernel,
         [sds((N, POOL), BF), sds((TP, 2 * DX, E), BF)],
-        (returned, src, pack_all),
+        (returned.reshape(SHARDS // QUAD, QUAD * CAP, E), src, pack_all),
         "pool",
         scratch=[
             pltpu.VMEM((BAGS, E), F32),
@@ -340,7 +344,7 @@
     (part,) = call(
         grads_kernel,
         [sds((DP, SHARDS, CHUNK, E), BF)],
-        (where, pooled, near, far, far_near, dense_input, weights, bias, head, label),
+        (where, pooled, near, far, far_near, dense_input, pack_all, bias, head, label),
         "grads",
         scratch=[
             pltpu.VMEM((DENSE, DX), BF),
@@ -360,7 +364,7 @@
     (row_grad,) = call(
         scatter_kernel,
         [sds((ROWS, E), BF)],
-        (ids, arrived),
+        (ids, arrived.reshape(SHARDS // QUAD, QUAD * CAP, E)),
         "scatter",
         scratch=[pltpu.VMEM((ROWS, E), F32)],
         flops=1_300_000_000,
@@ -370,19 +374,12 @@
     by_y = lax.all_to_all(row_grad, owners, split_axis=0, concat_axis=0, tiled=True)
     mine = jnp.sum(by_y.reshape(pieces, ROWS // pieces, E).astype(F32), axis=0)
     mine = (mine + partner(mine, "xh", 1)).astype(BF)
+    over_y = over_y.reshape(SHARDS, CHUNK, E)
+    over_all = lax.all_to_all(over_y, EMB, split_axis=0, concat_axis=0, tiled=True)
     spread = jnp.broadcast_to(mine[None], (pieces, ROWS // pieces, E)).reshape(ROWS, E)
-    spread, over_y = lax.optimization_barrier((spread, over_y))
+    spread, over_all = lax.optimization_barrier((spread, over_all))
     full = lax.all_to_all(spread, owners, split_axis=0, concat_axis=0, tiled=True)
-    over_y = over_y.reshape(SHARDS, CHUNK, E)
-    pairs = [over_y[0:4].astype(F32)] + [
-        partner(over_y[4 * c : 4 * c + 4], EMB, mask).astype(F32)
-        for c, mask in ((1, 1), (2, 8), (3, 9))
-    ]
-    pairs = (pairs[0] + pairs[1]) + (pairs[2] + pairs[3])
-    last = [pairs[0]] + [
-        partner(pairs[i].astype(BF), EMB, 2 * i).astype(F32) for i in (1, 2, 3)
-    ]
-    grads = (last[0] + last[1]) + (last[2] + last[3])
+    grads = jnp.sum(over_all.astype(F32), axis=0)
     full = full.astype(F32)
     accum_new = row_accum + full * full
     table_new = emb_table - LEARN * full / jnp.sqrt(accum_new)

time: 207 us -> 196 us (0.947)
  starting transfers between devices: 51.1 us -> 38.6 us
  waiting for transfers between devices: 63.9 us -> 66.6 us
    ppermute x10 -> x4, starting transfers between devices: 31.4 us -> 12.1 us  [partner(): return lax.ppermute(value, axes, [(i, i ^ mask) for i in range(size)])]
    all_to_all x0 -> x1, waiting for transfers between devices: none -> 7.4 us  [local(): lax.all_to_all(over_y, EMB, split_axis=0, concat_axis=0, tiled=True)]
    ppermute x10 -> x4, waiting for transfers between devices: 5.98 us -> 1.49 us  [partner(): return lax.ppermute(value, axes, [(i, i ^ mask) for i in range(size)])]
    all_to_all x0 -> x1, starting transfers between devices: none -> 3.99 us  [local(): lax.all_to_all(over_y, EMB, split_axis=0, concat_axis=0, tiled=True)]
    all_to_all x1, starting transfers between devices: 6.66 us -> 9.61 us  [local(): lax.all_to_all(spread, owners, split_axis=0, concat_axis=0, tiled=True)]
  transfers between devices with their start and end apart: 15 -> 10, of which waited for: 7 -> 7; matrix products, arithmetic and copies ran while one was open for 1% -> 1% of each run, Pallas kernels for 10% -> 10%
where the time goes in v8:
time: 196 us; the launch traced here: 195 us
  waiting for transfers between devices  66.6 us (34%)
  blocking collectives  41.4 us (21%)
  starting transfers between devices  38.6 us (20%)
  Pallas kernels  28 us (14%)
  between operations  14.3 us (7%)
  local copies, waits for them, and re-layouts  4.93 us (3%)
    all_to_all x1, waiting for transfers between devices, local(): lax.all_to_all(fetched, EMB, split_axis=0, concat_axis=0, tiled=True)  29.3 us
    pallas_call x6, Pallas kernels, call(): pl.pallas_call(kernel, out_shape=outs, in_specs=[SMEM if x.size < 8 else...  28 us
    all_to_all x1, blocking collectives, local(): lax.all_to_all(row_grad, owners, split_axis=0, concat_axis=0, tiled=True)  22.4 us
    all_to_all x1, blocking collectives, local(): ids = lax.all_to_all(ids, EMB, split_axis=0, concat_axis=0, tiled=True)  19 us
    all_to_all x1, waiting for transfers between devices, local(): arrived = lax.all_to_all(send, EMB, split_axis=0, concat_axis=0, tiled=True)  15.6 us
    ppermute x4, starting transfers between devices, partner(): return lax.ppermute(value, axes, [(i, i ^ mask) for i in range(size)])  12.1 us
    all_to_all x1, waiting for transfers between devices, local(): lax.all_to_all(spread, owners, split_axis=0, concat_axis=0, tiled=True)  10.5 us
    all_to_all x1, starting transfers between devices, local(): lax.all_to_all(spread, owners, split_axis=0, concat_axis=0, tiled=True)  9.61 us
  transfers between devices with their start and end apart: 10, of which 7 were waited for; matrix products, arithmetic and copies ran while one was open for 1% of the time, Pallas kernels for 10%

profile of v8, /device:TPU:1, one launch (start us, length us, event | category | flops | bytes accessed | tf_op | source)
XLA Modules:
  0.0 195.2 jit_solution(2475620997887811210)
XLA Ops:
  7.2 4.8 %index.1 = (s32[16,312]{1,0:T(8,128)}, s32[16,312]{1,0:T(8,128)}, s32[312,16]{1,0:T(8,128)}, bf16[3584,128]{1,0:T(8,128)(2,1)}) custom-call(s32[52,1,64]{2,1,0:T(1,128)} %bitcast.42, s32[52,64]{1,0:T(8,128)} %bitcast.41, s32[13,64]{1,0:T(8,128)} %bitcast.43, bf16[1792,128]{1,0:T(8,128)(2,1)} %down_hbm.1, bf16[128,1792]{1,0:T(8,128)(2,1)} %up_hbm.1), custom_call_target="tpu_custom_call" | custom-call | flops 400000000 | bytes 947456 | tf_op jit(solution)/shard_map/index/pallas_call | solution.py:49
  12.8 19.0 %all_to_all.44 = s32[16,1,312]{2,1,0:T(1,128)S(1)} all-to-all(s32[16,1,312]{2,1,0:T(1,128)S(1)} %copy.21), channel_id=1, replica_groups=mesh['xl'=2,'z'=8,'y'=8,'xh'=2,'core'=2] {'xl','z'}, dimensions={0} | all-to-all | bytes 39936 | tf_op jit(solution)/shard_map/all_to_all | solution.py:312
  31.9 4.1 %fetch.1 = bf16[16,312,128]{2,1,0:T(8,128)(2,1)} custom-call(s32[16,312]{1,0:T(8,128)S(1)} %bitcast.36, f32[1024,128]{1,0:T(8,128)S(1)} %copy-done.1), custom_call_target="tpu_custom_call" | custom-call | flops 1300000000 | bytes 544256 | tf_op jit(solution)/shard_map/fetch/pallas_call | solution.py:49
  36.0 3.8 %all-to-all-start.1 = ((bf16[16,312,128]{2,1,0:T(8,128)(2,1)}), bf16[16,312,128]{2,1,0:T(8,128)(2,1)S(1)}, u32[]{:S(2)}, u32[]{:S(2)}) async-start(bf16[16,312,128]{2,1,0:T(8,128)(2,1)} %fetch.1), calls=%async_computation.1 | async-start | bytes 2555904 | tf_op jit(solution)/shard_map/all_to_all | solution.py:316
  40.1 29.3 %all-to-all-done.1 = bf16[16,312,128]{2,1,0:T(8,128)(2,1)S(1)} async-done(((bf16[16,312,128]{2,1,0:T(8,128)(2,1)}), bf16[16,312,128]{2,1,0:T(8,128)(2,1)S(1)}, u32[]{:S(2)}, u32[]{:S(2)}) %all-to-all-start.1) | async-done | bytes 1277984 | tf_op jit(solution)/shard_map/all_to_all | solution.py:316
  69.5 2.2 %all-gather.3.cloned.1.call-done = bf16[14336,128]{1,0:T(8,128)(2,1)} async-done(((bf16[3584,128]{1,0:T(8,128)(2,1)}), bf16[14336,128]{1,0:T(8,128)(2,1)}) %all-gather.3.cloned.1.call-update) | async-done | bytes 3670032 | tf_op jit(solution)/shard_map/gather_weights/all_gather | solution.py:311
  71.7 3.6 %pool.1 = (bf16[64,1664]{1,0:T(8,128)(2,1)S(1)}, bf16[4,3584,128]{2,1,0:T(8,128)(2,1)S(1)}) custom-call(bf16[4,1248,128]{2,1,0:T(8,128)(2,1)S(1)} %bitcast.31, s32[16,312]{1,0:T(8,128)S(1)} %copy-done.2, bf16[4,3584,128]{2,1,0:T(8,128)(2,1)} %bitcast.32), custom_call_target="tpu_custom_call" | custom-call | flops 1060000000 | bytes 4967936 | tf_op jit(solution)/shard_map/pool/pallas_call | solution.py:49
  75.3 2.2 %collective-permute-start = (bf16[64,1664]{1,0:T(8,128)(2,1)S(1)}, bf16[64,1664]{1,0:T(8,128)(2,1)S(1)}, u32[]{:S(2)}, u32[]{:S(2)}) collective-permute-start(bf16[64,1664]{1,0:T(8,128)(2,1)S(1)} %get-tuple-element.29.pooled_ref.s0_ref), channel_id=1, source_target_pairs={{0,2},{2,0},{1,3},{3,1},{4,6},{6,4},{5,7},{7,5},{8,10},{10,8},{9,1... | collective-permute-start | bytes 638984 | tf_op jit(solution)/shard_map/ppermute | solution.py:275
  77.5 6.8 %main.1 = (f32[64,1664]{1,0:T(8,128)}, bf16[16,312,128]{2,1,0:T(8,128)(2,1)}) custom-call(s32[2]{0:T(128)S(1)} %pad_add_fusion.where_ref, bf16[64,1664]{1,0:T(8,128)(2,1)S(1)} %get-tuple-element.29.pooled_ref.s0_ref, bf16[256,128]{1,0:T(8,128)(2,1)S(1)} %copy-done.4, bf16[4,3584,128]{2,1,0:T(8,128)(2,1)S(1)} %get-tuple-element.25.pack_ref, ...), custom_call_target="tpu_custom_call" | custom-call | flops 10000000000 | bytes 4409864 | tf_op jit(solution)/shard_map/main/pallas_call | solution.py:49
  84.5 9.0 %all-to-all-start.2 = ((bf16[16,312,128]{2,1,0:T(8,128)(2,1)}), bf16[16,312,128]{2,1,0:T(8,128)(2,1)S(1)}, u32[]{:S(2)}, u32[]{:S(2)}) async-start(bf16[16,312,128]{2,1,0:T(8,128)(2,1)} %get-tuple-element.28), calls=%async_computation.2 | async-start | bytes 2555904 | tf_op jit(solution)/shard_map/all_to_all | solution.py:341
  93.5 3.3 %collective-permute-start.1 = (bf16[64,1664]{1,0:T(8,128)(2,1)S(1)}, bf16[64,1664]{1,0:T(8,128)(2,1)S(1)}, u32[]{:S(2)}, u32[]{:S(2)}) collective-permute-start(bf16[64,1664]{1,0:T(8,128)(2,1)S(1)} %get-tuple-element.29.pooled_ref.s0_ref), channel_id=1, source_target_pairs={{0,1},{1,0},{2,3},{3,2},{4,5},{5,4},{6,7},{7,6},{8,9},{9,8},{10,11... | collective-permute-start | bytes 638984 | tf_op jit(solution)/shard_map/ppermute | solution.py:275
  96.8 2.1 %collective-permute-start.2 = (bf16[64,1664]{1,0:T(8,128)(2,1)S(1)}, bf16[64,1664]{1,0:T(8,128)(2,1)S(1)}, u32[]{:S(2)}, u32[]{:S(2)}) collective-permute-start(bf16[64,1664]{1,0:T(8,128)(2,1)S(1)} %collective-permute-done.s2_ref), channel_id=1, source_target_pairs={{0,1},{1,0},{2,3},{3,2},{4,5},{5,4},{6,7},{7,6},{8,9},{9,8},{10,11... | collective-permute-start | bytes 638984 | tf_op jit(solution)/shard_map/ppermute | solution.py:275
  98.9 1.2 collective-permute-done.2.s3_ref
  100.2 2.0 %copy-done = bf16[14336,128]{1,0:T(8,128)(2,1)S(1)} copy-done((bf16[14336,128]{1,0:T(8,128)(2,1)S(1)}, bf16[14336,128]{1,0:T(8,128)(2,1)}, u32[]{:S(2)}) %copy-start) | copy-done | bytes 3670040
  102.2 5.8 %grads.1 = bf16[8,16,32,128]{3,2,1,0:T(8,128)(2,1)} custom-call(s32[2]{0:T(128)S(1)} %pad_add_fusion.where_ref, bf16[64,1664]{1,0:T(8,128)(2,1)S(1)} %get-tuple-element.29.pooled_ref.s0_ref, bf16[64,1664]{1,0:T(8,128)(2,1)S(1)} %collective-permute-done.1.s1_ref, bf16[64,1664]{1,0:T(8,128)(2,1)S(1)} %collective-permute-done.s2_ref, ...), custom_call_target="tpu_custom_call" | custom-call | flops 2000000000 | bytes 4602888 | tf_op jit(solution)/shard_map/grads/pallas_call | solution.py:49
  108.1 15.6 %all-to-all-done.2 = bf16[16,312,128]{2,1,0:T(8,128)(2,1)S(1)} async-done(((bf16[16,312,128]{2,1,0:T(8,128)(2,1)}), bf16[16,312,128]{2,1,0:T(8,128)(2,1)S(1)}, u32[]{:S(2)}, u32[]{:S(2)}) %all-to-all-start.2) | async-done | bytes 1277984 | tf_op jit(solution)/shard_map/all_to_all | solution.py:341
  123.6 2.9 %scatter.1 = bf16[1024,128]{1,0:T(8,128)(2,1)S(1)} custom-call(s32[16,312]{1,0:T(8,128)S(1)} %bitcast.37, bf16[4,1248,128]{2,1,0:T(8,128)(2,1)S(1)} %bitcast.34), custom_call_target="tpu_custom_call" | custom-call | flops 1300000000 | bytes 1297920 | tf_op jit(solution)/shard_map/scatter/pallas_call | solution.py:49
  126.5 22.4 %all_to_all.45 = bf16[16,64,128]{2,1,0:T(8,128)(2,1)S(1)} all-to-all(bf16[16,64,128]{2,1,0:T(8,128)(2,1)S(1)} %bitcast.35), channel_id=1, replica_groups=mesh['xl'=2,'z'=8,'y'=8,'xh'=2,'core'=2] {'y','core'}, dimensions={0} | all-to-all | bytes 524288 | tf_op jit(solution)/shard_map/all_to_all | solution.py:374
  148.9 4.6 %collective-permute-start.3 = (f32[64,128]{1,0:T(8,128)S(1)}, f32[64,128]{1,0:T(8,128)S(1)}, u32[]{:S(2)}, u32[]{:S(2)}) collective-permute-start(f32[64,128]{1,0:T(8,128)S(1)} %convert_reduce_fusion), channel_id=1, source_target_pairs={{0,2},{2,0},{1,3},{3,1},{4,6},{6,4},{5,7},{7,5},{8,10},{10,8},{9,1... | collective-permute-start | bytes 98312 | tf_op jit(solution)/shard_map/ppermute | solution.py:275
  153.6 4.0 %all-to-all-start.4 = ((bf16[16,32,128]{2,1,0:T(8,128)(2,1)}), bf16[16,32,128]{2,1,0:T(8,128)(2,1)S(1)}, u32[]{:S(2)}, u32[]{:S(2)}) async-start(bf16[16,32,128]{2,1,0:T(8,128)(2,1)} %bitcast.38), calls=%async_computation.5 | async-start | bytes 262144 | tf_op jit(solution)/shard_map/all_to_all | solution.py:378
  157.6 7.4 %all-to-all-done.4 = bf16[16,32,128]{2,1,0:T(8,128)(2,1)S(1)} async-done(((bf16[16,32,128]{2,1,0:T(8,128)(2,1)}), bf16[16,32,128]{2,1,0:T(8,128)(2,1)S(1)}, u32[]{:S(2)}, u32[]{:S(2)}) %all-to-all-start.4) | async-done | bytes 131104 | tf_op jit(solution)/shard_map/all_to_all | solution.py:378
  165.7 9.6 %all-to-all-start.5 = ((bf16[16,64,128]{2,1,0:T(8,128)(2,1)}), bf16[16,64,128]{2,1,0:T(8,128)(2,1)S(1)}, u32[]{:S(2)}, u32[]{:S(2)}) async-start(bf16[16,64,128]{2,1,0:T(8,128)(2,1)} %bitcast.14), calls=%async_computation.6 | async-start | bytes 524288 | tf_op jit(solution)/shard_map/all_to_all | solution.py:381
  176.6 10.5 %all-to-all-done.5 = bf16[16,64,128]{2,1,0:T(8,128)(2,1)S(1)} async-done(((bf16[16,64,128]{2,1,0:T(8,128)(2,1)}), bf16[16,64,128]{2,1,0:T(8,128)(2,1)S(1)}, u32[]{:S(2)}, u32[]{:S(2)}) %all-to-all-start.5) | async-done | bytes 262176 | tf_op jit(solution)/shard_map/all_to_all | solution.py:381
  187.2 1.1 fusion
  (40 shorter events, 3.5 us)
Async XLA Ops:
  7.2 64.5 %all-gather.3.cloned.1.call-start = ((), (), s32[]{:S(2)}) async-start(), calls=%async_computation.8 | async-start | bytes 4587520 | tf_op jit(solution)/shard_map/gather_weights/all_gather | solution.py:311
  7.2 24.6 %copy-start.1 = (f32[1024,128]{1,0:T(8,128)S(1)}, f32[1024,128]{1,0:T(8,128)}, u32[]{:S(2)}) copy-start(f32[1024,128]{1,0:T(8,128)} %table_ref.1) | copy-start | bytes 1572868
  36.0 3.9 %copy-start.7 = (f32[1792]{0:T(1024)S(1)}, f32[1792]{0:T(1024)}, u32[]{:S(2)}) copy-start(f32[1792]{0:T(1024)} %param.22) | copy-start | bytes 21508
  36.0 3.9 %copy-start.8 = (f32[1792]{0:T(1024)S(1)}, f32[1792]{0:T(1024)}, u32[]{:S(2)}) copy-start(f32[1792]{0:T(1024)} %param.23) | copy-start | bytes 21508
  36.0 3.9 %copy-start.9 = (s32[256]{0:T(256)S(1)}, s32[256]{0:T(256)}, u32[]{:S(2)}) copy-start(s32[256]{0:T(256)} %param.18) | copy-start | bytes 3076
  36.0 35.7 %copy-start.2 = (s32[16,312]{1,0:T(8,128)S(1)}, s32[16,312]{1,0:T(8,128)}, u32[]{:S(2)}) copy-start(s32[16,312]{1,0:T(8,128)} %get-tuple-element.22.src_ref) | copy-start | bytes 59908
  36.0 33.5 %all-to-all-start.1 = ((bf16[16,312,128]{2,1,0:T(8,128)(2,1)}), bf16[16,312,128]{2,1,0:T(8,128)(2,1)S(1)}, u32[]{:S(2)}, u32[]{:S(2)}) async-start(bf16[16,312,128]{2,1,0:T(8,128)(2,1)} %fetch.1), calls=%async_computation.1 | async-start | bytes 2555904 | tf_op jit(solution)/shard_map/all_to_all | solution.py:316
  71.7 5.8 %copy-start.3 = (f32[64,1664]{1,0:T(8,128)S(1)}, f32[64,1664]{1,0:T(8,128)}, u32[]{:S(2)}) copy-start(f32[64,1664]{1,0:T(8,128)} %feedback_ref.1) | copy-start | bytes 1277956
  71.7 5.8 %copy-start.4 = (bf16[256,128]{1,0:T(8,128)(2,1)S(1)}, bf16[256,128]{1,0:T(8,128)(2,1)}, u32[]{:S(2)}) copy-start(bf16[256,128]{1,0:T(8,128)(2,1)} %dense_ref.3) | copy-start | bytes 196612
  71.7 5.8 %copy-start.5 = (s32[312,16]{1,0:T(8,128)S(1)}, s32[312,16]{1,0:T(8,128)}, u32[]{:S(2)}) copy-start(s32[312,16]{1,0:T(8,128)} %get-tuple-element.26.src_t_ref) | copy-start | bytes 59908
  75.3 9.2 %collective-permute-start = (bf16[64,1664]{1,0:T(8,128)(2,1)S(1)}, bf16[64,1664]{1,0:T(8,128)(2,1)S(1)}, u32[]{:S(2)}, u32[]{:S(2)}) collective-permute-start(bf16[64,1664]{1,0:T(8,128)(2,1)S(1)} %get-tuple-element.29.pooled_ref.s0_ref), channel_id=1, source_target_pairs={{0,2},{2,0},{1,3},{3,1},{4,6},{6,4},{5,7},{7,5},{8,10},{10,8},{9,1... | collective-permute-start | bytes 638984 | tf_op jit(solution)/shard_map/ppermute | solution.py:275
  84.5 39.1 %all-to-all-start.2 = ((bf16[16,312,128]{2,1,0:T(8,128)(2,1)}), bf16[16,312,128]{2,1,0:T(8,128)(2,1)S(1)}, u32[]{:S(2)}, u32[]{:S(2)}) async-start(bf16[16,312,128]{2,1,0:T(8,128)(2,1)} %get-tuple-element.28), calls=%async_computation.2 | async-start | bytes 2555904 | tf_op jit(solution)/shard_map/all_to_all | solution.py:341
  93.5 60.1 %reduce-scatter.2.cloned.1.call-start = ((), (), s32[]{:S(2)}) async-start(), calls=%async_computation.7 | async-start | bytes 1179648 | tf_op jit(solution)/shard_map/reduce_scatter | solution.py:361
  93.5 5.4 %collective-permute-start.1 = (bf16[64,1664]{1,0:T(8,128)(2,1)S(1)}, bf16[64,1664]{1,0:T(8,128)(2,1)S(1)}, u32[]{:S(2)}, u32[]{:S(2)}) collective-permute-start(bf16[64,1664]{1,0:T(8,128)(2,1)S(1)} %get-tuple-element.29.pooled_ref.s0_ref), channel_id=1, source_target_pairs={{0,1},{1,0},{2,3},{3,2},{4,5},{5,4},{6,7},{7,6},{8,9},{9,8},{10,11... | collective-permute-start | bytes 638984 | tf_op jit(solution)/shard_map/ppermute | solution.py:275
  96.8 3.4 %collective-permute-start.2 = (bf16[64,1664]{1,0:T(8,128)(2,1)S(1)}, bf16[64,1664]{1,0:T(8,128)(2,1)S(1)}, u32[]{:S(2)}, u32[]{:S(2)}) collective-permute-start(bf16[64,1664]{1,0:T(8,128)(2,1)S(1)} %collective-permute-done.s2_ref), channel_id=1, source_target_pairs={{0,1},{1,0},{2,3},{3,2},{4,5},{5,4},{6,7},{7,6},{8,9},{9,8},{10,11... | collective-permute-start | bytes 638984 | tf_op jit(solution)/shard_map/ppermute | solution.py:275
  100.2 2.0 %copy-start = (bf16[14336,128]{1,0:T(8,128)(2,1)S(1)}, bf16[14336,128]{1,0:T(8,128)(2,1)}, u32[]{:S(2)}) copy-start(bf16[14336,128]{1,0:T(8,128)(2,1)} %all-gather.3.cloned.1.call-done) | copy-start | bytes 11010052
  148.9 8.7 %collective-permute-start.3 = (f32[64,128]{1,0:T(8,128)S(1)}, f32[64,128]{1,0:T(8,128)S(1)}, u32[]{:S(2)}, u32[]{:S(2)}) collective-permute-start(f32[64,128]{1,0:T(8,128)S(1)} %convert_reduce_fusion), channel_id=1, source_target_pairs={{0,2},{2,0},{1,3},{3,1},{4,6},{6,4},{5,7},{7,5},{8,10},{10,8},{9,1... | collective-permute-start | bytes 98312 | tf_op jit(solution)/shard_map/ppermute | solution.py:275
  153.6 33.6 %copy-start.6 = (f32[1024,128]{1,0:T(8,128)S(1)}, f32[1024,128]{1,0:T(8,128)}, u32[]{:S(2)}) copy-start(f32[1024,128]{1,0:T(8,128)} %param.13) | copy-start | bytes 1572868
  153.6 11.4 %all-to-all-start.4 = ((bf16[16,32,128]{2,1,0:T(8,128)(2,1)}), bf16[16,32,128]{2,1,0:T(8,128)(2,1)S(1)}, u32[]{:S(2)}, u32[]{:S(2)}) async-start(bf16[16,32,128]{2,1,0:T(8,128)(2,1)} %bitcast.38), calls=%async_computation.5 | async-start | bytes 262144 | tf_op jit(solution)/shard_map/all_to_all | solution.py:378
  165.7 21.3 %all-to-all-start.5 = ((bf16[16,64,128]{2,1,0:T(8,128)(2,1)}), bf16[16,64,128]{2,1,0:T(8,128)(2,1)S(1)}, u32[]{:S(2)}, u32[]{:S(2)}) async-start(bf16[16,64,128]{2,1,0:T(8,128)(2,1)} %bitcast.14), calls=%async_computation.6 | async-start | bytes 524288 | tf_op jit(solution)/shard_map/all_to_all | solution.py:381
Sparse Core Ops, SparseCore 0:
  12.2 59.4 all-gather.2
  108.2 39.8 reduce-scatter.1

commit v9 on v8

--- a/solution.py
+++ b/solution.py
@@ -376,9 +376,14 @@
     mine = (mine + partner(mine, "xh", 1)).astype(BF)
     over_y = over_y.reshape(SHARDS, CHUNK, E)
     over_all = lax.all_to_all(over_y, EMB, split_axis=0, concat_axis=0, tiled=True)
-    spread = jnp.broadcast_to(mine[None], (pieces, ROWS // pieces, E)).reshape(ROWS, E)
+    near_half = partner(mine, "core", 1)
+    lower = lax.axis_index("core") == 0
+    mine = jnp.where(
+        lower, jnp.stack([mine, near_half]), jnp.stack([near_half, mine])
+    ).reshape(ROWS // DP, E)
+    spread = jnp.broadcast_to(mine[None], (DP, ROWS // DP, E)).reshape(ROWS, E)
     spread, over_all = lax.optimization_barrier((spread, over_all))
-    full = lax.all_to_all(spread, owners, split_axis=0, concat_axis=0, tiled=True)
+    full = lax.all_to_all(spread, "y", split_axis=0, concat_axis=0, tiled=True)
     grads = jnp.sum(over_all.astype(F32), axis=0)
     full = full.astype(F32)
     accum_new = row_accum + full * full

time: 196 us -> 193 us (0.985)
  the two profiles are of different devices: /device:TPU:1 before, /device:TPU:4 now
where the time goes in v9:
time: 193 us; the launch traced here: 192 us
  waiting for transfers between devices  66.1 us (34%)
  blocking collectives  39.5 us (20%)
  starting transfers between devices  37.7 us (20%)
  Pallas kernels  27.8 us (14%)
  between operations  14.3 us (7%)
  local copies, waits for them, and re-layouts  4.92 us (3%)
    all_to_all x1, waiting for transfers between devices, local(): lax.all_to_all(fetched, EMB, split_axis=0, concat_axis=0, tiled=True)  30.4 us
    pallas_call x6, Pallas kernels, call(): pl.pallas_call(kernel, out_shape=outs, in_specs=[SMEM if x.size < 8 else...  27.8 us
    all_to_all x1, blocking collectives, local(): lax.all_to_all(row_grad, owners, split_axis=0, concat_axis=0, tiled=True)  20.2 us
    all_to_all x1, blocking collectives, local(): ids = lax.all_to_all(ids, EMB, split_axis=0, concat_axis=0, tiled=True)  19.3 us
    all_to_all x1, waiting for transfers between devices, local(): arrived = lax.all_to_all(send, EMB, split_axis=0, concat_axis=0, tiled=True)  18.7 us
    ppermute x5, starting transfers between devices, partner(): return lax.ppermute(value, axes, [(i, i ^ mask) for i in range(size)])  11.9 us
    all_to_all x1, waiting for transfers between devices, local(): full = lax.all_to_all(spread, 'y', split_axis=0, concat_axis=0, tiled=True)  9.27 us
    all_to_all x1, starting transfers between devices, local(): lax.all_to_all(over_y, EMB, split_axis=0, concat_axis=0, tiled=True)  8.67 us
  transfers between devices with their start and end apart: 11, of which 7 were waited for; matrix products, arithmetic and copies ran while one was open for 1% of the time, Pallas kernels for 10%

profile of v9, /device:TPU:4, one launch (start us, length us, event | category | flops | bytes accessed | tf_op | source)
XLA Modules:
  0.0 191.7 jit_solution(8873649466917694503)
XLA Ops:
  7.2 4.8 %index.1 = (s32[16,312]{1,0:T(8,128)}, s32[16,312]{1,0:T(8,128)}, s32[312,16]{1,0:T(8,128)}, bf16[3584,128]{1,0:T(8,128)(2,1)}) custom-call(s32[52,1,64]{2,1,0:T(1,128)} %bitcast.48, s32[52,64]{1,0:T(8,128)} %bitcast.47, s32[13,64]{1,0:T(8,128)} %bitcast.49, bf16[1792,128]{1,0:T(8,128)(2,1)} %down_hbm.1, bf16[128,1792]{1,0:T(8,128)(2,1)} %up_hbm.1), custom_call_target="tpu_custom_call" | custom-call | flops 400000000 | bytes 947456 | tf_op jit(solution)/shard_map/index/pallas_call | solution.py:49
  12.8 19.3 %all_to_all.44 = s32[16,1,312]{2,1,0:T(1,128)S(1)} all-to-all(s32[16,1,312]{2,1,0:T(1,128)S(1)} %copy.21), channel_id=1, replica_groups=mesh['xl'=2,'z'=8,'y'=8,'xh'=2,'core'=2] {'xl','z'}, dimensions={0} | all-to-all | bytes 39936 | tf_op jit(solution)/shard_map/all_to_all | solution.py:312
  32.2 4.1 %fetch.1 = bf16[16,312,128]{2,1,0:T(8,128)(2,1)} custom-call(s32[16,312]{1,0:T(8,128)S(1)} %bitcast.39, f32[1024,128]{1,0:T(8,128)S(1)} %copy-done.1), custom_call_target="tpu_custom_call" | custom-call | flops 1300000000 | bytes 544256 | tf_op jit(solution)/shard_map/fetch/pallas_call | solution.py:49
  36.3 3.9 %all-to-all-start.1 = ((bf16[16,312,128]{2,1,0:T(8,128)(2,1)}), bf16[16,312,128]{2,1,0:T(8,128)(2,1)S(1)}, u32[]{:S(2)}, u32[]{:S(2)}) async-start(bf16[16,312,128]{2,1,0:T(8,128)(2,1)} %fetch.1), calls=%async_computation.1 | async-start | bytes 2555904 | tf_op jit(solution)/shard_map/all_to_all | solution.py:316
  40.5 30.4 %all-to-all-done.1 = bf16[16,312,128]{2,1,0:T(8,128)(2,1)S(1)} async-done(((bf16[16,312,128]{2,1,0:T(8,128)(2,1)}), bf16[16,312,128]{2,1,0:T(8,128)(2,1)S(1)}, u32[]{:S(2)}, u32[]{:S(2)}) %all-to-all-start.1) | async-done | bytes 1277984 | tf_op jit(solution)/shard_map/all_to_all | solution.py:316
  70.8 3.6 %pool.1 = (bf16[64,1664]{1,0:T(8,128)(2,1)S(1)}, bf16[4,3584,128]{2,1,0:T(8,128)(2,1)S(1)}) custom-call(bf16[4,1248,128]{2,1,0:T(8,128)(2,1)S(1)} %bitcast.34, s32[16,312]{1,0:T(8,128)S(1)} %copy-done.2, bf16[4,3584,128]{2,1,0:T(8,128)(2,1)} %bitcast.35), custom_call_target="tpu_custom_call" | custom-call | flops 1060000000 | bytes 4967936 | tf_op jit(solution)/shard_map/pool/pallas_call | solution.py:49
  74.4 2.7 %collective-permute-start = (bf16[64,1664]{1,0:T(8,128)(2,1)S(1)}, bf16[64,1664]{1,0:T(8,128)(2,1)S(1)}, u32[]{:S(2)}, u32[]{:S(2)}) collective-permute-start(bf16[64,1664]{1,0:T(8,128)(2,1)S(1)} %get-tuple-element.29.pooled_ref.s0_ref), channel_id=1, source_target_pairs={{0,2},{2,0},{1,3},{3,1},{4,6},{6,4},{5,7},{7,5},{8,10},{10,8},{9,1... | collective-permute-start | bytes 638984 | tf_op jit(solution)/shard_map/ppermute | solution.py:275
  77.2 6.7 %main.1 = (f32[64,1664]{1,0:T(8,128)}, bf16[16,312,128]{2,1,0:T(8,128)(2,1)}) custom-call(s32[2]{0:T(128)S(1)} %pad_add_fusion.where_ref, bf16[64,1664]{1,0:T(8,128)(2,1)S(1)} %get-tuple-element.29.pooled_ref.s0_ref, bf16[256,128]{1,0:T(8,128)(2,1)S(1)} %copy-done.4, bf16[4,3584,128]{2,1,0:T(8,128)(2,1)S(1)} %get-tuple-element.25.pack_ref, ...), custom_call_target="tpu_custom_call" | custom-call | flops 10000000000 | bytes 4409864 | tf_op jit(solution)/shard_map/main/pallas_call | solution.py:49
  83.9 8.4 %all-to-all-start.2 = ((bf16[16,312,128]{2,1,0:T(8,128)(2,1)}), bf16[16,312,128]{2,1,0:T(8,128)(2,1)S(1)}, u32[]{:S(2)}, u32[]{:S(2)}) async-start(bf16[16,312,128]{2,1,0:T(8,128)(2,1)} %get-tuple-element.28), calls=%async_computation.2 | async-start | bytes 2555904 | tf_op jit(solution)/shard_map/all_to_all | solution.py:341
  92.4 1.9 %collective-permute-start.1 = (bf16[64,1664]{1,0:T(8,128)(2,1)S(1)}, bf16[64,1664]{1,0:T(8,128)(2,1)S(1)}, u32[]{:S(2)}, u32[]{:S(2)}) collective-permute-start(bf16[64,1664]{1,0:T(8,128)(2,1)S(1)} %get-tuple-element.29.pooled_ref.s0_ref), channel_id=1, source_target_pairs={{0,1},{1,0},{2,3},{3,2},{4,5},{5,4},{6,7},{7,6},{8,9},{9,8},{10,11... | collective-permute-start | bytes 638984 | tf_op jit(solution)/shard_map/ppermute | solution.py:275
  94.3 2.6 %collective-permute-start.2 = (bf16[64,1664]{1,0:T(8,128)(2,1)S(1)}, bf16[64,1664]{1,0:T(8,128)(2,1)S(1)}, u32[]{:S(2)}, u32[]{:S(2)}) collective-permute-start(bf16[64,1664]{1,0:T(8,128)(2,1)S(1)} %collective-permute-done.s2_ref), channel_id=1, source_target_pairs={{0,1},{1,0},{2,3},{3,2},{4,5},{5,4},{6,7},{7,6},{8,9},{9,8},{10,11... | collective-permute-start | bytes 638984 | tf_op jit(solution)/shard_map/ppermute | solution.py:275
  97.8 2.0 %copy-done = bf16[14336,128]{1,0:T(8,128)(2,1)S(1)} copy-done((bf16[14336,128]{1,0:T(8,128)(2,1)S(1)}, bf16[14336,128]{1,0:T(8,128)(2,1)}, u32[]{:S(2)}) %copy-start) | copy-done | bytes 3670040
  99.9 5.7 %grads.1 = bf16[8,16,32,128]{3,2,1,0:T(8,128)(2,1)} custom-call(s32[2]{0:T(128)S(1)} %pad_add_fusion.where_ref, bf16[64,1664]{1,0:T(8,128)(2,1)S(1)} %get-tuple-element.29.pooled_ref.s0_ref, bf16[64,1664]{1,0:T(8,128)(2,1)S(1)} %collective-permute-done.1.s1_ref, bf16[64,1664]{1,0:T(8,128)(2,1)S(1)} %collective-permute-done.s2_ref, ...), custom_call_target="tpu_custom_call" | custom-call | flops 2000000000 | bytes 4602888 | tf_op jit(solution)/shard_map/grads/pallas_call | solution.py:49
  105.6 18.7 %all-to-all-done.2 = bf16[16,312,128]{2,1,0:T(8,128)(2,1)S(1)} async-done(((bf16[16,312,128]{2,1,0:T(8,128)(2,1)}), bf16[16,312,128]{2,1,0:T(8,128)(2,1)S(1)}, u32[]{:S(2)}, u32[]{:S(2)}) %all-to-all-start.2) | async-done | bytes 1277984 | tf_op jit(solution)/shard_map/all_to_all | solution.py:341
  124.3 2.9 %scatter.1 = bf16[1024,128]{1,0:T(8,128)(2,1)S(1)} custom-call(s32[16,312]{1,0:T(8,128)S(1)} %bitcast.40, bf16[4,1248,128]{2,1,0:T(8,128)(2,1)S(1)} %bitcast.37), custom_call_target="tpu_custom_call" | custom-call | flops 1300000000 | bytes 1297920 | tf_op jit(solution)/shard_map/scatter/pallas_call | solution.py:49
  127.2 20.2 %all_to_all.45 = bf16[16,64,128]{2,1,0:T(8,128)(2,1)S(1)} all-to-all(bf16[16,64,128]{2,1,0:T(8,128)(2,1)S(1)} %bitcast.38), channel_id=1, replica_groups=mesh['xl'=2,'z'=8,'y'=8,'xh'=2,'core'=2] {'y','core'}, dimensions={0} | all-to-all | bytes 524288 | tf_op jit(solution)/shard_map/all_to_all | solution.py:374
  147.4 2.6 %collective-permute-start.3 = (f32[64,128]{1,0:T(8,128)S(1)}, f32[64,128]{1,0:T(8,128)S(1)}, u32[]{:S(2)}, u32[]{:S(2)}) collective-permute-start(f32[64,128]{1,0:T(8,128)S(1)} %convert_reduce_fusion), channel_id=1, source_target_pairs={{0,2},{2,0},{1,3},{3,1},{4,6},{6,4},{5,7},{7,5},{8,10},{10,8},{9,1... | collective-permute-start | bytes 98312 | tf_op jit(solution)/shard_map/ppermute | solution.py:275
  150.4 8.7 %all-to-all-start.4 = ((bf16[16,32,128]{2,1,0:T(8,128)(2,1)}), bf16[16,32,128]{2,1,0:T(8,128)(2,1)S(1)}, u32[]{:S(2)}, u32[]{:S(2)}) async-start(bf16[16,32,128]{2,1,0:T(8,128)(2,1)} %bitcast.42), calls=%async_computation.5 | async-start | bytes 262144 | tf_op jit(solution)/shard_map/all_to_all | solution.py:378
  159.1 2.1 %collective-permute-start.4 = (bf16[64,128]{1,0:T(8,128)(2,1)S(1)}, bf16[64,128]{1,0:T(8,128)(2,1)S(1)}, u32[]{:S(2)}, u32[]{:S(2)}) collective-permute-start(bf16[64,128]{1,0:T(8,128)(2,1)S(1)} %add_convert_fusion), channel_id=1, source_target_pairs={{0,1},{1,0},{2,3},{3,2},{4,5},{5,4},{6,7},{7,6},{8,9},{9,8},{10,11... | collective-permute-start | bytes 49160 | tf_op jit(solution)/shard_map/ppermute | solution.py:275
  161.2 1.1 collective-permute-done.4
  162.4 5.3 %all-to-all-done.4 = bf16[16,32,128]{2,1,0:T(8,128)(2,1)S(1)} async-done(((bf16[16,32,128]{2,1,0:T(8,128)(2,1)}), bf16[16,32,128]{2,1,0:T(8,128)(2,1)S(1)}, u32[]{:S(2)}, u32[]{:S(2)}) %all-to-all-start.4) | async-done | bytes 131104 | tf_op jit(solution)/shard_map/all_to_all | solution.py:378
  168.4 4.8 %all-to-all-start.5 = ((bf16[8,128,128]{2,1,0:T(8,128)(2,1)}), bf16[8,128,128]{2,1,0:T(8,128)(2,1)S(1)}, u32[]{:S(2)}, u32[]{:S(2)}) async-start(bf16[8,128,128]{2,1,0:T(8,128)(2,1)} %bitcast.17), calls=%async_computation.6 | async-start | bytes 524288 | tf_op jit(solution)/shard_map/all_to_all | solution.py:386
  174.4 9.3 %all-to-all-done.5 = bf16[8,128,128]{2,1,0:T(8,128)(2,1)S(1)} async-done(((bf16[8,128,128]{2,1,0:T(8,128)(2,1)}), bf16[8,128,128]{2,1,0:T(8,128)(2,1)S(1)}, u32[]{:S(2)}, u32[]{:S(2)}) %all-to-all-start.5) | async-done | bytes 262176 | tf_op jit(solution)/shard_map/all_to_all | solution.py:386
  183.8 1.1 fusion
  (43 shorter events, 4.5 us)
Async XLA Ops:
  7.2 63.7 %all-gather.3.cloned.1.call-start = ((), (), s32[]{:S(2)}) async-start(), calls=%async_computation.8 | async-start | bytes 4587520 | tf_op jit(solution)/shard_map/gather_weights/all_gather | solution.py:311
  7.2 24.9 %copy-start.1 = (f32[1024,128]{1,0:T(8,128)S(1)}, f32[1024,128]{1,0:T(8,128)}, u32[]{:S(2)}) copy-start(f32[1024,128]{1,0:T(8,128)} %table_ref.1) | copy-start | bytes 1572868
  36.3 3.9 %copy-start.7 = (f32[1792]{0:T(1024)S(1)}, f32[1792]{0:T(1024)}, u32[]{:S(2)}) copy-start(f32[1792]{0:T(1024)} %param.22) | copy-start | bytes 21508
  36.3 3.9 %copy-start.8 = (f32[1792]{0:T(1024)S(1)}, f32[1792]{0:T(1024)}, u32[]{:S(2)}) copy-start(f32[1792]{0:T(1024)} %param.23) | copy-start | bytes 21508
  36.3 3.9 %copy-start.9 = (s32[256]{0:T(256)S(1)}, s32[256]{0:T(256)}, u32[]{:S(2)}) copy-start(s32[256]{0:T(256)} %param.18) | copy-start | bytes 3076
  36.3 34.5 %copy-start.2 = (s32[16,312]{1,0:T(8,128)S(1)}, s32[16,312]{1,0:T(8,128)}, u32[]{:S(2)}) copy-start(s32[16,312]{1,0:T(8,128)} %get-tuple-element.22.src_ref) | copy-start | bytes 59908
  36.3 34.5 %all-to-all-start.1 = ((bf16[16,312,128]{2,1,0:T(8,128)(2,1)}), bf16[16,312,128]{2,1,0:T(8,128)(2,1)S(1)}, u32[]{:S(2)}, u32[]{:S(2)}) async-start(bf16[16,312,128]{2,1,0:T(8,128)(2,1)} %fetch.1), calls=%async_computation.1 | async-start | bytes 2555904 | tf_op jit(solution)/shard_map/all_to_all | solution.py:316
  70.8 6.3 %copy-start.3 = (f32[64,1664]{1,0:T(8,128)S(1)}, f32[64,1664]{1,0:T(8,128)}, u32[]{:S(2)}) copy-start(f32[64,1664]{1,0:T(8,128)} %feedback_ref.1) | copy-start | bytes 1277956
  70.8 6.4 %copy-start.4 = (bf16[256,128]{1,0:T(8,128)(2,1)S(1)}, bf16[256,128]{1,0:T(8,128)(2,1)}, u32[]{:S(2)}) copy-start(bf16[256,128]{1,0:T(8,128)(2,1)} %dense_ref.3) | copy-start | bytes 196612
  70.8 6.4 %copy-start.5 = (s32[312,16]{1,0:T(8,128)S(1)}, s32[312,16]{1,0:T(8,128)}, u32[]{:S(2)}) copy-start(s32[312,16]{1,0:T(8,128)} %get-tuple-element.26.src_t_ref) | copy-start | bytes 59908
  74.4 9.5 %collective-permute-start = (bf16[64,1664]{1,0:T(8,128)(2,1)S(1)}, bf16[64,1664]{1,0:T(8,128)(2,1)S(1)}, u32[]{:S(2)}, u32[]{:S(2)}) collective-permute-start(bf16[64,1664]{1,0:T(8,128)(2,1)S(1)} %get-tuple-element.29.pooled_ref.s0_ref), channel_id=1, source_target_pairs={{0,2},{2,0},{1,3},{3,1},{4,6},{6,4},{5,7},{7,5},{8,10},{10,8},{9,1... | collective-permute-start | bytes 638984 | tf_op jit(solution)/shard_map/ppermute | solution.py:275
  83.9 40.4 %all-to-all-start.2 = ((bf16[16,312,128]{2,1,0:T(8,128)(2,1)}), bf16[16,312,128]{2,1,0:T(8,128)(2,1)S(1)}, u32[]{:S(2)}, u32[]{:S(2)}) async-start(bf16[16,312,128]{2,1,0:T(8,128)(2,1)} %get-tuple-element.28), calls=%async_computation.2 | async-start | bytes 2555904 | tf_op jit(solution)/shard_map/all_to_all | solution.py:341
  92.4 58.1 %reduce-scatter.2.cloned.1.call-start = ((), (), s32[]{:S(2)}) async-start(), calls=%async_computation.7 | async-start | bytes 1179648 | tf_op jit(solution)/shard_map/reduce_scatter | solution.py:361
  92.4 4.5 %collective-permute-start.1 = (bf16[64,1664]{1,0:T(8,128)(2,1)S(1)}, bf16[64,1664]{1,0:T(8,128)(2,1)S(1)}, u32[]{:S(2)}, u32[]{:S(2)}) collective-permute-start(bf16[64,1664]{1,0:T(8,128)(2,1)S(1)} %get-tuple-element.29.pooled_ref.s0_ref), channel_id=1, source_target_pairs={{0,1},{1,0},{2,3},{3,2},{4,5},{5,4},{6,7},{7,6},{8,9},{9,8},{10,11... | collective-permute-start | bytes 638984 | tf_op jit(solution)/shard_map/ppermute | solution.py:275
  94.3 3.5 %collective-permute-start.2 = (bf16[64,1664]{1,0:T(8,128)(2,1)S(1)}, bf16[64,1664]{1,0:T(8,128)(2,1)S(1)}, u32[]{:S(2)}, u32[]{:S(2)}) collective-permute-start(bf16[64,1664]{1,0:T(8,128)(2,1)S(1)} %collective-permute-done.s2_ref), channel_id=1, source_target_pairs={{0,1},{1,0},{2,3},{3,2},{4,5},{5,4},{6,7},{7,6},{8,9},{9,8},{10,11... | collective-permute-start | bytes 638984 | tf_op jit(solution)/shard_map/ppermute | solution.py:275
  97.8 2.0 %copy-start = (bf16[14336,128]{1,0:T(8,128)(2,1)S(1)}, bf16[14336,128]{1,0:T(8,128)(2,1)}, u32[]{:S(2)}) copy-start(bf16[14336,128]{1,0:T(8,128)(2,1)} %all-gather.3.cloned.1.call-done) | copy-start | bytes 11010052
  147.4 11.7 %collective-permute-start.3 = (f32[64,128]{1,0:T(8,128)S(1)}, f32[64,128]{1,0:T(8,128)S(1)}, u32[]{:S(2)}, u32[]{:S(2)}) collective-permute-start(f32[64,128]{1,0:T(8,128)S(1)} %convert_reduce_fusion), channel_id=1, source_target_pairs={{0,2},{2,0},{1,3},{3,1},{4,6},{6,4},{5,7},{7,5},{8,10},{10,8},{9,1... | collective-permute-start | bytes 98312 | tf_op jit(solution)/shard_map/ppermute | solution.py:275
  150.4 17.3 %all-to-all-start.4 = ((bf16[16,32,128]{2,1,0:T(8,128)(2,1)}), bf16[16,32,128]{2,1,0:T(8,128)(2,1)S(1)}, u32[]{:S(2)}, u32[]{:S(2)}) async-start(bf16[16,32,128]{2,1,0:T(8,128)(2,1)} %bitcast.42), calls=%async_computation.5 | async-start | bytes 262144 | tf_op jit(solution)/shard_map/all_to_all | solution.py:378
  159.1 24.7 %copy-start.6 = (f32[1024,128]{1,0:T(8,128)S(1)}, f32[1024,128]{1,0:T(8,128)}, u32[]{:S(2)}) copy-start(f32[1024,128]{1,0:T(8,128)} %param.13) | copy-start | bytes 1572868
  159.1 3.2 %collective-permute-start.4 = (bf16[64,128]{1,0:T(8,128)(2,1)S(1)}, bf16[64,128]{1,0:T(8,128)(2,1)S(1)}, u32[]{:S(2)}, u32[]{:S(2)}) collective-permute-start(bf16[64,128]{1,0:T(8,128)(2,1)S(1)} %add_convert_fusion), channel_id=1, source_target_pairs={{0,1},{1,0},{2,3},{3,2},{4,5},{5,4},{6,7},{7,6},{8,9},{9,8},{10,11... | collective-permute-start | bytes 49160 | tf_op jit(solution)/shard_map/ppermute | solution.py:275
  168.4 15.3 %all-to-all-start.5 = ((bf16[8,128,128]{2,1,0:T(8,128)(2,1)}), bf16[8,128,128]{2,1,0:T(8,128)(2,1)S(1)}, u32[]{:S(2)}, u32[]{:S(2)}) async-start(bf16[8,128,128]{2,1,0:T(8,128)(2,1)} %bitcast.17), calls=%async_computation.6 | async-start | bytes 524288 | tf_op jit(solution)/shard_map/all_to_all | solution.py:386
Sparse Core Ops, SparseCore 0:
  12.2 55.4 all-gather.2
  105.7 44.6 reduce-scatter.1

commit v10 on v9

--- a/solution.py
+++ b/solution.py
@@ -108,7 +108,9 @@
         found = found + dot(jnp.concatenate(values, axis=0).astype(BF), place, 1, 1)
     ids = found[0:SHARDS] + found[SHARDS : 2 * SHARDS]
     src = found[2 * SHARDS : 3 * SHARDS] + found[3 * SHARDS :] - 1.0
-    ids_ref[...] = ids.astype(I32)
+    ids = ids.astype(I32)
+    for s in range(SHARDS):
+        ids_ref[s] = ids[s : s + 1, :]
     src_ref[...] = src.astype(I32)
     src_t_ref[...] = jnp.transpose(src).astype(I32)
     for move in moves[3:]:
@@ -289,7 +291,7 @@
     ids, src, src_t, pack = call(
         index_kernel,
         (
-            sds((SHARDS, CAP), I32),
+            sds((SHARDS, 1, CAP), I32),
             sds((SHARDS, CAP), I32),
             sds((CAP, SHARDS), I32),
             sds((2 * DX, E), BF),
@@ -310,6 +312,7 @@
     with jax.named_scope("gather_weights"):
         pack_all = lax.all_gather(pack, TPA, axis=0, tiled=False)
     ids = lax.all_to_all(ids, EMB, split_axis=0, concat_axis=0, tiled=True)
+    ids = ids.reshape(SHARDS, CAP)
     (fetched,) = call(
         fetch_kernel, [sds((SHARDS, CAP, E), BF)], (ids, emb_table), "fetch", flops=1_300_000_000
     )

time: 193 us -> 193 us (level)
  no operation moved by 1% of the time
where the time goes in v10:
time: 193 us; the launch traced here: 192 us
  waiting for transfers between devices  66.1 us (34%)
  blocking collectives  39.8 us (21%)
  starting transfers between devices  38.3 us (20%)
  Pallas kernels  27.8 us (14%)
  between operations  14.3 us (7%)
  local copies, waits for them, and re-layouts  4.15 us (2%)
    all_to_all x1, waiting for transfers between devices, local(): lax.all_to_all(fetched, EMB, split_axis=0, concat_axis=0, tiled=True)  30.4 us
    pallas_call x6, Pallas kernels, call(): pl.pallas_call(kernel, out_shape=outs, in_specs=[SMEM if x.size < 8 else...  27.8 us
    all_to_all x1, blocking collectives, local(): lax.all_to_all(row_grad, owners, split_axis=0, concat_axis=0, tiled=True)  20.2 us
    all_to_all x1, blocking collectives, local(): ids = lax.all_to_all(ids, EMB, split_axis=0, concat_axis=0, tiled=True)  19.6 us
    all_to_all x1, waiting for transfers between devices, local(): arrived = lax.all_to_all(send, EMB, split_axis=0, concat_axis=0, tiled=True)  18.7 us
    ppermute x5, starting transfers between devices, partner(): return lax.ppermute(value, axes, [(i, i ^ mask) for i in range(size)])  12 us
    all_to_all x1, waiting for transfers between devices, local(): full = lax.all_to_all(spread, 'y', split_axis=0, concat_axis=0, tiled=True)  9.27 us
    all_to_all x1, starting transfers between devices, local(): arrived = lax.all_to_all(send, EMB, split_axis=0, concat_axis=0, tiled=True)  8.93 us
  transfers between devices with their start and end apart: 11, of which 7 were waited for; matrix products, arithmetic and copies ran while one was open for 1% of the time, Pallas kernels for 10%

profile of v10, /device:TPU:4, one launch (start us, length us, event | category | flops | bytes accessed | tf_op | source)
XLA Modules:
  0.0 191.7 jit_solution(8588607465429411817)
XLA Ops:
  7.2 4.8 %index.1 = (s32[16,1,312]{2,1,0:T(1,128)}, s32[16,312]{1,0:T(8,128)}, s32[312,16]{1,0:T(8,128)}, bf16[3584,128]{1,0:T(8,128)(2,1)}) custom-call(s32[52,1,64]{2,1,0:T(1,128)} %bitcast.46, s32[52,64]{1,0:T(8,128)} %bitcast.45, s32[13,64]{1,0:T(8,128)} %bitcast.47, bf16[1792,128]{1,0:T(8,128)(2,1)} %down_hbm.1, bf16[128,1792]{1,0:T(8,128)(2,1)} %up_hbm.1), custom_call_target="tpu_custom_call" | custom-call | flops 400000000 | bytes 947456 | tf_op jit(solution)/shard_map/index/pallas_call | solution.py:49
  12.0 19.6 %all_to_all.38 = s32[16,1,312]{2,1,0:T(1,128)S(1)} all-to-all(s32[16,1,312]{2,1,0:T(1,128)} %get-tuple-element.21), channel_id=1, replica_groups=mesh['xl'=2,'z'=8,'y'=8,'xh'=2,'core'=2] {'xl','z'}, dimensions={0} | all-to-all | bytes 39936 | tf_op jit(solution)/shard_map/all_to_all | solution.py:314
  31.6 4.1 %fetch.1 = bf16[16,312,128]{2,1,0:T(8,128)(2,1)} custom-call(s32[16,312]{1,0:T(8,128)S(1)} %bitcast.38, f32[1024,128]{1,0:T(8,128)S(1)} %copy-done.1), custom_call_target="tpu_custom_call" | custom-call | flops 1300000000 | bytes 544256 | tf_op jit(solution)/shard_map/fetch/pallas_call | solution.py:49
  35.7 3.8 %all-to-all-start.1 = ((bf16[16,312,128]{2,1,0:T(8,128)(2,1)}), bf16[16,312,128]{2,1,0:T(8,128)(2,1)S(1)}, u32[]{:S(2)}, u32[]{:S(2)}) async-start(bf16[16,312,128]{2,1,0:T(8,128)(2,1)} %fetch.1), calls=%async_computation.1 | async-start | bytes 2555904 | tf_op jit(solution)/shard_map/all_to_all | solution.py:319
  39.9 30.4 %all-to-all-done.1 = bf16[16,312,128]{2,1,0:T(8,128)(2,1)S(1)} async-done(((bf16[16,312,128]{2,1,0:T(8,128)(2,1)}), bf16[16,312,128]{2,1,0:T(8,128)(2,1)S(1)}, u32[]{:S(2)}, u32[]{:S(2)}) %all-to-all-start.1) | async-done | bytes 1277984 | tf_op jit(solution)/shard_map/all_to_all | solution.py:319
  70.3 3.6 %pool.1 = (bf16[64,1664]{1,0:T(8,128)(2,1)S(1)}, bf16[4,3584,128]{2,1,0:T(8,128)(2,1)S(1)}) custom-call(bf16[4,1248,128]{2,1,0:T(8,128)(2,1)S(1)} %bitcast.33, s32[16,312]{1,0:T(8,128)S(1)} %copy-done.2, bf16[4,3584,128]{2,1,0:T(8,128)(2,1)} %bitcast.34), custom_call_target="tpu_custom_call" | custom-call | flops 1060000000 | bytes 4967936 | tf_op jit(solution)/shard_map/pool/pallas_call | solution.py:49
  73.9 2.8 %collective-permute-start = (bf16[64,1664]{1,0:T(8,128)(2,1)S(1)}, bf16[64,1664]{1,0:T(8,128)(2,1)S(1)}, u32[]{:S(2)}, u32[]{:S(2)}) collective-permute-start(bf16[64,1664]{1,0:T(8,128)(2,1)S(1)} %get-tuple-element.29.pooled_ref.s0_ref), channel_id=1, source_target_pairs={{0,2},{2,0},{1,3},{3,1},{4,6},{6,4},{5,7},{7,5},{8,10},{10,8},{9,1... | collective-permute-start | bytes 638984 | tf_op jit(solution)/shard_map/ppermute | solution.py:277
  76.7 6.7 %main.1 = (f32[64,1664]{1,0:T(8,128)}, bf16[16,312,128]{2,1,0:T(8,128)(2,1)}) custom-call(s32[2]{0:T(128)S(1)} %pad_add_fusion.where_ref, bf16[64,1664]{1,0:T(8,128)(2,1)S(1)} %get-tuple-element.29.pooled_ref.s0_ref, bf16[256,128]{1,0:T(8,128)(2,1)S(1)} %copy-done.4, bf16[4,3584,128]{2,1,0:T(8,128)(2,1)S(1)} %get-tuple-element.25.pack_ref, ...), custom_call_target="tpu_custom_call" | custom-call | flops 10000000000 | bytes 4409864 | tf_op jit(solution)/shard_map/main/pallas_call | solution.py:49
  83.4 8.9 %all-to-all-start.2 = ((bf16[16,312,128]{2,1,0:T(8,128)(2,1)}), bf16[16,312,128]{2,1,0:T(8,128)(2,1)S(1)}, u32[]{:S(2)}, u32[]{:S(2)}) async-start(bf16[16,312,128]{2,1,0:T(8,128)(2,1)} %get-tuple-element.28), calls=%async_computation.2 | async-start | bytes 2555904 | tf_op jit(solution)/shard_map/all_to_all | solution.py:344
  92.4 1.9 %collective-permute-start.1 = (bf16[64,1664]{1,0:T(8,128)(2,1)S(1)}, bf16[64,1664]{1,0:T(8,128)(2,1)S(1)}, u32[]{:S(2)}, u32[]{:S(2)}) collective-permute-start(bf16[64,1664]{1,0:T(8,128)(2,1)S(1)} %get-tuple-element.29.pooled_ref.s0_ref), channel_id=1, source_target_pairs={{0,1},{1,0},{2,3},{3,2},{4,5},{5,4},{6,7},{7,6},{8,9},{9,8},{10,11... | collective-permute-start | bytes 638984 | tf_op jit(solution)/shard_map/ppermute | solution.py:277
  94.3 2.6 %collective-permute-start.2 = (bf16[64,1664]{1,0:T(8,128)(2,1)S(1)}, bf16[64,1664]{1,0:T(8,128)(2,1)S(1)}, u32[]{:S(2)}, u32[]{:S(2)}) collective-permute-start(bf16[64,1664]{1,0:T(8,128)(2,1)S(1)} %collective-permute-done.s2_ref), channel_id=1, source_target_pairs={{0,1},{1,0},{2,3},{3,2},{4,5},{5,4},{6,7},{7,6},{8,9},{9,8},{10,11... | collective-permute-start | bytes 638984 | tf_op jit(solution)/shard_map/ppermute | solution.py:277
  97.8 2.0 %copy-done = bf16[14336,128]{1,0:T(8,128)(2,1)S(1)} copy-done((bf16[14336,128]{1,0:T(8,128)(2,1)S(1)}, bf16[14336,128]{1,0:T(8,128)(2,1)}, u32[]{:S(2)}) %copy-start) | copy-done | bytes 3670040
  99.9 5.7 %grads.1 = bf16[8,16,32,128]{3,2,1,0:T(8,128)(2,1)} custom-call(s32[2]{0:T(128)S(1)} %pad_add_fusion.where_ref, bf16[64,1664]{1,0:T(8,128)(2,1)S(1)} %get-tuple-element.29.pooled_ref.s0_ref, bf16[64,1664]{1,0:T(8,128)(2,1)S(1)} %collective-permute-done.1.s1_ref, bf16[64,1664]{1,0:T(8,128)(2,1)S(1)} %collective-permute-done.s2_ref, ...), custom_call_target="tpu_custom_call" | custom-call | flops 2000000000 | bytes 4602888 | tf_op jit(solution)/shard_map/grads/pallas_call | solution.py:49
  105.6 18.7 %all-to-all-done.2 = bf16[16,312,128]{2,1,0:T(8,128)(2,1)S(1)} async-done(((bf16[16,312,128]{2,1,0:T(8,128)(2,1)}), bf16[16,312,128]{2,1,0:T(8,128)(2,1)S(1)}, u32[]{:S(2)}, u32[]{:S(2)}) %all-to-all-start.2) | async-done | bytes 1277984 | tf_op jit(solution)/shard_map/all_to_all | solution.py:344
  124.3 2.9 %scatter.1 = bf16[1024,128]{1,0:T(8,128)(2,1)S(1)} custom-call(s32[16,312]{1,0:T(8,128)S(1)} %bitcast.39, bf16[4,1248,128]{2,1,0:T(8,128)(2,1)S(1)} %bitcast.36), custom_call_target="tpu_custom_call" | custom-call | flops 1300000000 | bytes 1297920 | tf_op jit(solution)/shard_map/scatter/pallas_call | solution.py:49
  127.2 20.2 %all_to_all.39 = bf16[16,64,128]{2,1,0:T(8,128)(2,1)S(1)} all-to-all(bf16[16,64,128]{2,1,0:T(8,128)(2,1)S(1)} %bitcast.37), channel_id=1, replica_groups=mesh['xl'=2,'z'=8,'y'=8,'xh'=2,'core'=2] {'y','core'}, dimensions={0} | all-to-all | bytes 524288 | tf_op jit(solution)/shard_map/all_to_all | solution.py:377
  147.4 2.6 %collective-permute-start.3 = (f32[64,128]{1,0:T(8,128)S(1)}, f32[64,128]{1,0:T(8,128)S(1)}, u32[]{:S(2)}, u32[]{:S(2)}) collective-permute-start(f32[64,128]{1,0:T(8,128)S(1)} %convert_reduce_fusion), channel_id=1, source_target_pairs={{0,2},{2,0},{1,3},{3,1},{4,6},{6,4},{5,7},{7,5},{8,10},{10,8},{9,1... | collective-permute-start | bytes 98312 | tf_op jit(solution)/shard_map/ppermute | solution.py:277
  150.4 8.7 %all-to-all-start.4 = ((bf16[16,32,128]{2,1,0:T(8,128)(2,1)}), bf16[16,32,128]{2,1,0:T(8,128)(2,1)S(1)}, u32[]{:S(2)}, u32[]{:S(2)}) async-start(bf16[16,32,128]{2,1,0:T(8,128)(2,1)} %bitcast.41), calls=%async_computation.5 | async-start | bytes 262144 | tf_op jit(solution)/shard_map/all_to_all | solution.py:381
  159.1 2.1 %collective-permute-start.4 = (bf16[64,128]{1,0:T(8,128)(2,1)S(1)}, bf16[64,128]{1,0:T(8,128)(2,1)S(1)}, u32[]{:S(2)}, u32[]{:S(2)}) collective-permute-start(bf16[64,128]{1,0:T(8,128)(2,1)S(1)} %add_convert_fusion), channel_id=1, source_target_pairs={{0,1},{1,0},{2,3},{3,2},{4,5},{5,4},{6,7},{7,6},{8,9},{9,8},{10,11... | collective-permute-start | bytes 49160 | tf_op jit(solution)/shard_map/ppermute | solution.py:277
  161.2 1.1 collective-permute-done.4
  162.4 5.3 %all-to-all-done.4 = bf16[16,32,128]{2,1,0:T(8,128)(2,1)S(1)} async-done(((bf16[16,32,128]{2,1,0:T(8,128)(2,1)}), bf16[16,32,128]{2,1,0:T(8,128)(2,1)S(1)}, u32[]{:S(2)}, u32[]{:S(2)}) %all-to-all-start.4) | async-done | bytes 131104 | tf_op jit(solution)/shard_map/all_to_all | solution.py:381
  168.4 4.8 %all-to-all-start.5 = ((bf16[8,128,128]{2,1,0:T(8,128)(2,1)}), bf16[8,128,128]{2,1,0:T(8,128)(2,1)S(1)}, u32[]{:S(2)}, u32[]{:S(2)}) async-start(bf16[8,128,128]{2,1,0:T(8,128)(2,1)} %bitcast.16), calls=%async_computation.6 | async-start | bytes 524288 | tf_op jit(solution)/shard_map/all_to_all | solution.py:389
  174.4 9.3 %all-to-all-done.5 = bf16[8,128,128]{2,1,0:T(8,128)(2,1)S(1)} async-done(((bf16[8,128,128]{2,1,0:T(8,128)(2,1)}), bf16[8,128,128]{2,1,0:T(8,128)(2,1)S(1)}, u32[]{:S(2)}, u32[]{:S(2)}) %all-to-all-start.5) | async-done | bytes 262176 | tf_op jit(solution)/shard_map/all_to_all | solution.py:389
  183.8 1.1 fusion
  (42 shorter events, 3.8 us)
Async XLA Ops:
  7.2 24.4 %copy-start.1 = (f32[1024,128]{1,0:T(8,128)S(1)}, f32[1024,128]{1,0:T(8,128)}, u32[]{:S(2)}) copy-start(f32[1024,128]{1,0:T(8,128)} %table_ref.1) | copy-start | bytes 1572868
  7.2 63.1 %all-gather.3.cloned.1.call-start = ((), (), s32[]{:S(2)}) async-start(), calls=%async_computation.8 | async-start | bytes 4587520 | tf_op jit(solution)/shard_map/gather_weights/all_gather | solution.py:313
  35.7 3.9 %copy-start.7 = (f32[1792]{0:T(1024)S(1)}, f32[1792]{0:T(1024)}, u32[]{:S(2)}) copy-start(f32[1792]{0:T(1024)} %param.22) | copy-start | bytes 21508
  35.7 3.9 %copy-start.8 = (f32[1792]{0:T(1024)S(1)}, f32[1792]{0:T(1024)}, u32[]{:S(2)}) copy-start(f32[1792]{0:T(1024)} %param.23) | copy-start | bytes 21508
  35.7 3.9 %copy-start.9 = (s32[256]{0:T(256)S(1)}, s32[256]{0:T(256)}, u32[]{:S(2)}) copy-start(s32[256]{0:T(256)} %param.18) | copy-start | bytes 3076
  35.7 34.5 %copy-start.2 = (s32[16,312]{1,0:T(8,128)S(1)}, s32[16,312]{1,0:T(8,128)}, u32[]{:S(2)}) copy-start(s32[16,312]{1,0:T(8,128)} %get-tuple-element.22.src_ref) | copy-start | bytes 59908
  35.7 34.5 %all-to-all-start.1 = ((bf16[16,312,128]{2,1,0:T(8,128)(2,1)}), bf16[16,312,128]{2,1,0:T(8,128)(2,1)S(1)}, u32[]{:S(2)}, u32[]{:S(2)}) async-start(bf16[16,312,128]{2,1,0:T(8,128)(2,1)} %fetch.1), calls=%async_computation.1 | async-start | bytes 2555904 | tf_op jit(solution)/shard_map/all_to_all | solution.py:319
  70.2 6.4 %copy-start.3 = (f32[64,1664]{1,0:T(8,128)S(1)}, f32[64,1664]{1,0:T(8,128)}, u32[]{:S(2)}) copy-start(f32[64,1664]{1,0:T(8,128)} %feedback_ref.1) | copy-start | bytes 1277956
  70.2 6.4 %copy-start.4 = (bf16[256,128]{1,0:T(8,128)(2,1)S(1)}, bf16[256,128]{1,0:T(8,128)(2,1)}, u32[]{:S(2)}) copy-start(bf16[256,128]{1,0:T(8,128)(2,1)} %dense_ref.3) | copy-start | bytes 196612
  70.3 6.4 %copy-start.5 = (s32[312,16]{1,0:T(8,128)S(1)}, s32[312,16]{1,0:T(8,128)}, u32[]{:S(2)}) copy-start(s32[312,16]{1,0:T(8,128)} %get-tuple-element.26.src_t_ref) | copy-start | bytes 59908
  73.9 9.6 %collective-permute-start = (bf16[64,1664]{1,0:T(8,128)(2,1)S(1)}, bf16[64,1664]{1,0:T(8,128)(2,1)S(1)}, u32[]{:S(2)}, u32[]{:S(2)}) collective-permute-start(bf16[64,1664]{1,0:T(8,128)(2,1)S(1)} %get-tuple-element.29.pooled_ref.s0_ref), channel_id=1, source_target_pairs={{0,2},{2,0},{1,3},{3,1},{4,6},{6,4},{5,7},{7,5},{8,10},{10,8},{9,1... | collective-permute-start | bytes 638984 | tf_op jit(solution)/shard_map/ppermute | solution.py:277
  83.4 40.9 %all-to-all-start.2 = ((bf16[16,312,128]{2,1,0:T(8,128)(2,1)}), bf16[16,312,128]{2,1,0:T(8,128)(2,1)S(1)}, u32[]{:S(2)}, u32[]{:S(2)}) async-start(bf16[16,312,128]{2,1,0:T(8,128)(2,1)} %get-tuple-element.28), calls=%async_computation.2 | async-start | bytes 2555904 | tf_op jit(solution)/shard_map/all_to_all | solution.py:344
  92.4 58.1 %reduce-scatter.2.cloned.1.call-start = ((), (), s32[]{:S(2)}) async-start(), calls=%async_computation.7 | async-start | bytes 1179648 | tf_op jit(solution)/shard_map/reduce_scatter | solution.py:364
  92.4 4.5 %collective-permute-start.1 = (bf16[64,1664]{1,0:T(8,128)(2,1)S(1)}, bf16[64,1664]{1,0:T(8,128)(2,1)S(1)}, u32[]{:S(2)}, u32[]{:S(2)}) collective-permute-start(bf16[64,1664]{1,0:T(8,128)(2,1)S(1)} %get-tuple-element.29.pooled_ref.s0_ref), channel_id=1, source_target_pairs={{0,1},{1,0},{2,3},{3,2},{4,5},{5,4},{6,7},{7,6},{8,9},{9,8},{10,11... | collective-permute-start | bytes 638984 | tf_op jit(solution)/shard_map/ppermute | solution.py:277
  94.3 3.5 %collective-permute-start.2 = (bf16[64,1664]{1,0:T(8,128)(2,1)S(1)}, bf16[64,1664]{1,0:T(8,128)(2,1)S(1)}, u32[]{:S(2)}, u32[]{:S(2)}) collective-permute-start(bf16[64,1664]{1,0:T(8,128)(2,1)S(1)} %collective-permute-done.s2_ref), channel_id=1, source_target_pairs={{0,1},{1,0},{2,3},{3,2},{4,5},{5,4},{6,7},{7,6},{8,9},{9,8},{10,11... | collective-permute-start | bytes 638984 | tf_op jit(solution)/shard_map/ppermute | solution.py:277
  97.8 2.0 %copy-start = (bf16[14336,128]{1,0:T(8,128)(2,1)S(1)}, bf16[14336,128]{1,0:T(8,128)(2,1)}, u32[]{:S(2)}) copy-start(bf16[14336,128]{1,0:T(8,128)(2,1)} %all-gather.3.cloned.1.call-done) | copy-start | bytes 11010052
  147.4 11.7 %collective-permute-start.3 = (f32[64,128]{1,0:T(8,128)S(1)}, f32[64,128]{1,0:T(8,128)S(1)}, u32[]{:S(2)}, u32[]{:S(2)}) collective-permute-start(f32[64,128]{1,0:T(8,128)S(1)} %convert_reduce_fusion), channel_id=1, source_target_pairs={{0,2},{2,0},{1,3},{3,1},{4,6},{6,4},{5,7},{7,5},{8,10},{10,8},{9,1... | collective-permute-start | bytes 98312 | tf_op jit(solution)/shard_map/ppermute | solution.py:277
  150.4 17.3 %all-to-all-start.4 = ((bf16[16,32,128]{2,1,0:T(8,128)(2,1)}), bf16[16,32,128]{2,1,0:T(8,128)(2,1)S(1)}, u32[]{:S(2)}, u32[]{:S(2)}) async-start(bf16[16,32,128]{2,1,0:T(8,128)(2,1)} %bitcast.41), calls=%async_computation.5 | async-start | bytes 262144 | tf_op jit(solution)/shard_map/all_to_all | solution.py:381
  159.1 24.7 %copy-start.6 = (f32[1024,128]{1,0:T(8,128)S(1)}, f32[1024,128]{1,0:T(8,128)}, u32[]{:S(2)}) copy-start(f32[1024,128]{1,0:T(8,128)} %param.13) | copy-start | bytes 1572868
  159.1 3.2 %collective-permute-start.4 = (bf16[64,128]{1,0:T(8,128)(2,1)S(1)}, bf16[64,128]{1,0:T(8,128)(2,1)S(1)}, u32[]{:S(2)}, u32[]{:S(2)}) collective-permute-start(bf16[64,128]{1,0:T(8,128)(2,1)S(1)} %add_convert_fusion), channel_id=1, source_target_pairs={{0,1},{1,0},{2,3},{3,2},{4,5},{5,4},{6,7},{7,6},{8,9},{9,8},{10,11... | collective-permute-start | bytes 49160 | tf_op jit(solution)/shard_map/ppermute | solution.py:277
  168.4 15.3 %all-to-all-start.5 = ((bf16[8,128,128]{2,1,0:T(8,128)(2,1)}), bf16[8,128,128]{2,1,0:T(8,128)(2,1)S(1)}, u32[]{:S(2)}, u32[]{:S(2)}) async-start(bf16[8,128,128]{2,1,0:T(8,128)(2,1)} %bitcast.16), calls=%async_computation.6 | async-start | bytes 524288 | tf_op jit(solution)/shard_map/all_to_all | solution.py:389
Sparse Core Ops, SparseCore 0:
  12.1 55.5 all-gather.2
  105.7 44.6 reduce-scatter.1
